TPU v7x, 256 devices: a whole 4x4x8 slice. The times are simulated.
256 devices in a mesh: gx: 8 (over x, core), gy: 32 (over y, z).
Axes of the slice: x: 4, y: 4, z: 8, core: 2. Of those that a mesh axis runs over, the one named last changes fastest.
Arguments:
- forcing: float32 [8, 32, 256, 512], P('gx', 'gy'), may hold values from -26 to 26
- element_order: int32 [8, 32, 256], P('gx', 'gy'), may hold values from 0 to 255, each once within a row
- diffusivity: float32 [8, 32, 256], P('gx', 'gy'), may hold values from 0.3 to 3
- reaction: float32 [8, 32, 256], P('gx', 'gy'), may hold values from 0.02 to 0.2
- leaf_factor: float32 [8, 32, 153, 256], P('gx', 'gy'), may hold values from -0.21875 to 0.21875
- column_factor: float32 [8, 32, 425, 256], P('gx', 'gy'), may hold values from -1 to 1, as said below
- top_factor: float32 [8, 32, 425, 256], P('gx', 'gy'), may hold values from -1 to 1, as said below
Outputs:
- pressure: float32 [8, 32, 256, 512], P('gx', 'gy')
- residual: float32 [8, 32, 256, 512], P('gx', 'gy')
Inputs may be any that keep to these rules, and one draw needn't show every extreme that they name: Each device's element_order holds every structured index of its 256 elements once. `column_factor`: devices that touch the same global vertex hold equal rows for it; rows of vertices with local offset vx = 0 or vx = 4 are zero. `top_factor`: devices that touch the same global vertex hold equal rows for it.
All inputs are finite; a program needn't handle non-finite values.
Results may differ from a plain program's by a relative error of at most 0.0014.
Values sent between devices are 32-bit elements; how exact they have to be, the bound alone decides.
No kernel may reach another device: no remote copies, remote signals or barrier semaphores. Data moves between devices by JAX's collectives and lax.ppermute only.
A program may use at most 128 MiB of HBM per device.

v0:
```python
import jax
import jax.numpy as jnp
import numpy as np
from jax import lax
from jax.sharding import PartitionSpec as P

NP = 8
EX = 4
EY = 4
EZ = 16


def padded_2(x, sides, width):
    for axis, dim in sides:
        peers, length = (lax.axis_size(axis), x.shape[dim])
        up = [(i, (i + 1) % peers) for i in range(peers)]
        down = [(j, i) for i, j in up]
        last = lax.slice_in_dim(x, length - width, length, axis=dim)
        first = lax.slice_in_dim(x, 0, width, axis=dim)
        before = lax.ppermute(last, axis, up)
        after = lax.ppermute(first, axis, down)
        x = jnp.concatenate([before, x, after], axis=dim)
    return x


def legendre_columns(points, degree):
    columns_table = np.zeros((points.shape[0], degree + 1))
    columns_table[:, 0] = 1.0
    columns_table[:, 1] = points
    for level_at in range(2, degree + 1):
        columns_table[:, level_at] = (
            (2 * level_at - 1) * points * columns_table[:, level_at - 1]
            - (level_at - 1) * columns_table[:, level_at - 2]
        ) / level_at
    return columns_table


def jacobi_eigen(symmetric, npoints):
    matrix_work = symmetric.copy()
    vectors = np.eye(npoints)
    for sweep_at in range(15):
        for first_at in range(npoints):
            for second_at in range(first_at + 1, npoints):
                off_value = matrix_work[first_at, second_at]
                gap_value = matrix_work[second_at, second_at] - matrix_work[first_at, first_at]
                root_value = np.sqrt(gap_value * gap_value + 4.0 * off_value * off_value)
                sign_value = np.where(gap_value >= 0.0, 1.0, -1.0)
                denominator = np.abs(gap_value) + root_value
                safe_denominator = np.where(denominator > 0.0, denominator, 1.0)
                tangent = sign_value * 2.0 * off_value / safe_denominator
                cosine_value = 1.0 / np.sqrt(1.0 + tangent * tangent)
                sine_value = tangent * cosine_value
                rotation = np.eye(npoints)
                rotation[first_at, first_at] = cosine_value
                rotation[second_at, second_at] = cosine_value
                rotation[first_at, second_at] = sine_value
                rotation[second_at, first_at] = -sine_value
                matrix_work = rotation.T @ matrix_work @ rotation
                vectors = vectors @ rotation
    eigvals = np.array([matrix_work[place_at, place_at] for place_at in range(npoints)])
    return (eigvals, vectors)


def gll_tables(npoints):
    degree = npoints - 1
    estimate = -np.cos(np.pi * np.arange(npoints) / degree)
    for newton_at in range(100):
        columns_table = legendre_columns(estimate, degree)
        estimate = estimate - (
            estimate * columns_table[:, degree] - columns_table[:, degree - 1]
        ) / (npoints * columns_table[:, degree])
    values = legendre_columns(estimate, degree)[:, degree]
    weights = 2.0 / (degree * (degree + 1) * values**2)
    derivative = np.zeros((npoints, npoints))
    for row_at in range(npoints):
        for column_at in range(npoints):
            if row_at != column_at:
                derivative[row_at, column_at] = (
                    values[row_at] / values[column_at] / (estimate[row_at] - estimate[column_at])
                )
    derivative[0, 0] = -degree * (degree + 1) / 4.0
    derivative[degree, degree] = degree * (degree + 1) / 4.0
    stiffness = derivative.T @ (weights[:, None] * derivative)
    inv_root = 1.0 / np.sqrt(weights)
    symmetric = inv_root[:, None] * stiffness * inv_root[None, :]
    eigvals, eigvecs = jacobi_eigen(0.5 * (symmetric + symmetric.T), npoints)
    modes = inv_root[:, None] * eigvecs
    return (estimate, weights, stiffness, eigvals, modes)


def build_tables():
    points, weights, stiffness, eigvals, modes = gll_tables(8)
    massmat = weights[:, None] * np.eye(8)
    filler = np.ones(8)
    stiff_full = (
        np.kron(np.kron(stiffness, massmat), massmat)
        + np.kron(np.kron(massmat, stiffness), massmat)
        + np.kron(np.kron(massmat, massmat), stiffness)
    )
    mass_full = np.kron(np.kron(weights, weights), weights)
    eigen_full = (
        np.kron(np.kron(eigvals, filler), filler)
        + np.kron(np.kron(filler, eigvals), filler)
        + np.kron(np.kron(filler, filler), eigvals)
    )
    shape_full = np.kron(np.kron(modes, modes), modes)
    linear = np.stack([(1.0 - points) / 2.0, (1.0 + points) / 2.0], 1)
    trilinear = np.kron(np.kron(linear, linear), linear)
    return tuple(
        (
            jnp.asarray(table, dtype=jnp.float32)
            for table in (stiff_full, mass_full, eigen_full, shape_full, trilinear)
        )
    )


def weight_table():
    node_index = jnp.arange(NP * NP * NP, dtype=jnp.int32)
    index_x = node_index // (NP * NP)
    index_y = node_index // NP % NP
    index_z = node_index % NP
    count_x = jnp.where((index_x == 0) | (index_x == NP - 1), 2.0, 1.0)
    count_y = jnp.where((index_y == 0) | (index_y == NP - 1), 2.0, 1.0)
    layer_index = jnp.arange(EZ, dtype=jnp.int32)[:, None]
    count_z = jnp.where(
        (index_z[None, :] == 0) & (layer_index > 0)
        | (index_z[None, :] == NP - 1) & (layer_index < EZ - 1),
        2.0,
        1.0,
    )
    multiplicity = count_x[None, :] * count_y[None, :] * count_z
    weight = jnp.broadcast_to(1.0 / multiplicity, (EX * EY, EZ, NP * NP * NP)).reshape(
        EX * EY * EZ, NP * NP * NP
    )
    return weight.astype(jnp.float32)


def pair_sum(extended, direction):
    length = extended.shape[direction] - 2
    middle = lax.slice_in_dim(extended, 1, length + 1, axis=direction)
    preceding = lax.slice_in_dim(extended, 0, length, axis=direction)
    following = lax.slice_in_dim(extended, 2, length + 2, axis=direction)
    position = lax.broadcasted_iota(jnp.int32, middle.shape, direction) % NP
    return (
        middle
        + jnp.where(position == 0, preceding, 0.0)
        + jnp.where(position == NP - 1, following, 0.0)
    )


def assemble(element_field):
    lattice = (
        element_field.reshape(EX, EY, EZ, NP, NP, NP)
        .transpose(0, 3, 1, 4, 2, 5)
        .reshape(EX * NP, EY * NP, EZ * NP)
    )
    extended = padded_2(lattice, (("gx", 0),), 1)
    lattice = pair_sum(extended, 0)
    extended = padded_2(lattice, (("gy", 1),), 1)
    lattice = pair_sum(extended, 1)
    padded = jnp.pad(lattice, ((0, 0), (0, 0), (1, 1)))
    lattice = pair_sum(padded, 2)
    lattice = lattice.reshape(EX, NP, EY, NP, EZ, NP).transpose(0, 2, 4, 1, 3, 5)
    return lattice.reshape(EX * EY * EZ, NP * NP * NP)


def per_device(
    forcing, element_order, diffusivity, reaction, leaf_factor, column_factor, top_factor
):
    stiff_table, mass_table, eigen_table, shape_table, linear_table = build_tables()
    highest = lax.Precision.HIGHEST
    order_slots = element_order[0, 0]
    inverse = jnp.argsort(order_slots)
    source = forcing[0, 0][inverse]
    diffusion_local = diffusivity[0, 0][inverse][:, None]
    reaction_local = reaction[0, 0][inverse][:, None]
    leaf_block = leaf_factor[0, 0]
    column_block = column_factor[0, 0]
    top_block = top_factor[0, 0]
    weight = weight_table()
    reciprocal = 1.0 / (diffusion_local * eigen_table[None, :] + reaction_local)

    def global_sum(couples):
        partial_sums = jnp.stack([jnp.sum(former * latter * weight) for former, latter in couples])
        return lax.psum(partial_sums, ("gx", "gy"))

    def operate(element_field):
        element_term = jnp.dot(
            element_field, stiff_table, precision=highest, preferred_element_type=jnp.float32
        ) * diffusion_local + element_field * (mass_table[None, :] * reaction_local)
        return assemble(element_term)

    def coarse(residue):
        corner = jnp.dot(
            residue * weight, linear_table, precision=highest, preferred_element_type=jnp.float32
        ).reshape(EX, EY, EZ, 8)
        vertex = jnp.zeros((EX + 1, EY + 1, EZ + 1), jnp.float32)
        for shift_x in (0, 1):
            for shift_y in (0, 1):
                for shift_z in (0, 1):
                    piece = corner[..., shift_x * 4 + shift_y * 2 + shift_z]
                    vertex = vertex + jnp.pad(
                        piece,
                        ((shift_x, 1 - shift_x), (shift_y, 1 - shift_y), (shift_z, 1 - shift_z)),
                    )
        flat_vertex = vertex.reshape(-1)
        inner_vertex = vertex[1:EX, 1:EY, :].reshape(-1)
        leaf_coeffs = jnp.dot(
            inner_vertex, leaf_block, precision=highest, preferred_element_type=jnp.float32
        )
        column_part = jnp.dot(
            flat_vertex, column_block, precision=highest, preferred_element_type=jnp.float32
        )
        top_part = jnp.dot(
            flat_vertex, top_block, precision=highest, preferred_element_type=jnp.float32
        )
        column_coeffs = lax.psum(column_part, "gy")
        top_coeffs = lax.psum(top_part, ("gx", "gy"))
        solved = jnp.dot(
            column_block, column_coeffs, precision=highest, preferred_element_type=jnp.float32
        ) + jnp.dot(top_block, top_coeffs, precision=highest, preferred_element_type=jnp.float32)
        solved = solved.reshape(EX + 1, EY + 1, EZ + 1)
        leaf_part = jnp.dot(
            leaf_block, leaf_coeffs, precision=highest, preferred_element_type=jnp.float32
        ).reshape(EX - 1, EY - 1, EZ + 1)
        solved = solved.at[1:EX, 1:EY, :].add(leaf_part)
        gathered = []
        for shift_x in (0, 1):
            for shift_y in (0, 1):
                for shift_z in (0, 1):
                    gathered.append(
                        solved[
                            shift_x : shift_x + EX, shift_y : shift_y + EY, shift_z : shift_z + EZ
                        ]
                    )
        corner_values = jnp.stack(gathered, -1).reshape(EX * EY * EZ, 8)
        return jnp.dot(
            corner_values, linear_table.T, precision=highest, preferred_element_type=jnp.float32
        )

    def precondition(residue):
        spectral = (
            jnp.dot(residue, shape_table, precision=highest, preferred_element_type=jnp.float32)
            * reciprocal
        )
        smooth = (
            assemble(
                jnp.dot(
                    spectral, shape_table.T, precision=highest, preferred_element_type=jnp.float32
                )
            )
            * weight
        )
        return smooth + coarse(residue)

    assembled = assemble(source)
    beta_norm = jnp.sqrt(global_sum([(assembled, assembled)])[0])
    basis_one = assembled / beta_norm
    search_one = precondition(basis_one)
    image_one = operate(search_one)
    first_diag = global_sum([(image_one, basis_one)])[0]
    remainder = image_one - first_diag * basis_one
    first_sub = jnp.sqrt(global_sum([(remainder, remainder)])[0])
    basis_two = remainder / first_sub
    search_two = precondition(basis_two)
    image_two = operate(search_two)
    totals = global_sum([(image_two, basis_one), (image_two, basis_two)])
    second_top = totals[0]
    second_diag = totals[1]
    remainder = image_two - second_top * basis_one - second_diag * basis_two
    second_sub = jnp.sqrt(global_sum([(remainder, remainder)])[0])
    first_norm = jnp.sqrt(first_diag * first_diag + first_sub * first_sub)
    cosine = first_diag / first_norm
    sine_part = first_sub / first_norm
    rotated = cosine * second_top + sine_part * second_diag
    lowered = cosine * second_diag - sine_part * second_top
    second_norm = jnp.sqrt(lowered * lowered + second_sub * second_sub)
    factor_two = -(lowered / second_norm) * sine_part * beta_norm / second_norm
    factor_one = (cosine * beta_norm - rotated * factor_two) / first_norm
    pressure_field = factor_one * search_one + factor_two * search_two
    residual_field = assembled - factor_one * image_one - factor_two * image_two
    return (pressure_field[order_slots][None, None], residual_field[order_slots][None, None])


def solution(mesh):
    placed = (
        P("gx", "gy", None, None),
        P("gx", "gy", None),
        P("gx", "gy", None),
        P("gx", "gy", None),
        P("gx", "gy", None, None),
        P("gx", "gy", None, None),
        P("gx", "gy", None, None),
    )
    return jax.shard_map(
        per_device,
        mesh=mesh,
        in_specs=placed,
        out_specs=(P("gx", "gy", None, None), P("gx", "gy", None, None)),
        check_vma=False,
    )
```

profile of v0, /device:TPU:1, one launch (start us, length us, event | category | flops | bytes accessed | tf_op | source)
XLA Modules:
  0.0 1046.1 jit_solution(8710073243584607831)
XLA Ops:
  0.7 3.9 sort.17
  5.8 4.2 reshape.356
  9.9 7.6 copy.68
  17.6 6.4 reshape.357
  24.0 2.6 collective-permute-start
  31.7 6.5 collective-permute-start.3
  43.2 6.1 reshape.358
  49.3 6.8 copy.69
  56.2 3.9 fusion.13
  60.0 85.3 %psum.63 = f32[1]{0:T(128)} all-reduce(f32[1]{0:T(128)} %bitcast.5), channel_id=1, replica_groups=mesh['gx'=8,'gy'=32] {'gx','gy'}, use_global_device_ids=true, to_apply=%region_2.3 | all-reduce | flops 1 | bytes 8 | tf_op jit(solution)/shard_map/psum | solution.py:185
  146.0 3.0 bitcast_divide_fusion
  151.0 2.3 fusion.145
  154.2 59.0 %psum.64 = f32[256]{0:T(256)S(1)} all-reduce(f32[256]{0:T(256)S(1)} %bitcast.293), channel_id=1, replica_groups=mesh['gx'=8,'gy'=32] {'gy'}, use_global_device_ids=true, to_apply=%region_3.4 | all-reduce | flops 256 | bytes 2048 | tf_op jit(solution)/shard_map/psum | solution.py:217
  213.9 85.4 %psum.65 = f32[256]{0:T(256)S(1)} all-reduce(f32[256]{0:T(256)S(1)} %bitcast.289), channel_id=1, replica_groups=mesh['gx'=8,'gy'=32] {'gx','gy'}, use_global_device_ids=true, to_apply=%region_4.5 | all-reduce | flops 256 | bytes 2048 | tf_op jit(solution)/shard_map/psum | solution.py:218
  299.9 7.9 copy.70
  307.8 5.4 reshape.359
  316.1 5.1 reshape.360
  321.2 7.6 copy.72
  328.8 6.4 reshape.361
  337.9 2.3 collective-permute-done.5
  342.3 3.2 collective-permute-start.7
  347.0 6.1 reshape.362
  353.1 7.8 copy.73
  361.1 5.4 reshape.363
  372.8 5.1 reshape.368
  377.9 7.6 copy.85
  385.6 7.1 reshape.369
  395.4 2.6 collective-permute-done.9
  399.8 5.7 collective-permute-start.11
  407.8 7.0 reshape.370
  414.8 6.8 copy.86
  421.6 5.2 fusion.11
  426.7 78.6 %psum.66 = f32[]{:T(128)} all-reduce(f32[]{:T(128)} %fusion.11), channel_id=1, replica_groups=mesh['gx'=8,'gy'=32] {'gx','gy'}, use_global_device_ids=true, to_apply=%region_6.7 | all-reduce | flops 1 | bytes 8 | tf_op jit(solution)/shard_map/psum | solution.py:185
  505.3 5.8 multiply_reduce_fusion
  511.1 72.5 %psum.67 = f32[1]{0:T(128)} all-reduce(f32[1]{0:T(128)} %bitcast.35), channel_id=1, replica_groups=mesh['gx'=8,'gy'=32] {'gx','gy'}, use_global_device_ids=true, to_apply=%region_8.9 | all-reduce | flops 1 | bytes 8 | tf_op jit(solution)/shard_map/psum | solution.py:185
  584.3 4.9 fusion.1
  589.2 2.3 fusion.148
  593.3 58.9 %psum.68 = f32[256]{0:T(256)S(1)} all-reduce(f32[256]{0:T(256)S(1)} %bitcast.287), channel_id=1, replica_groups=mesh['gx'=8,'gy'=32] {'gy'}, use_global_device_ids=true, to_apply=%region_9.10 | all-reduce | flops 256 | bytes 2048 | tf_op jit(solution)/shard_map/psum | solution.py:217
  652.6 85.5 %psum.69 = f32[256]{0:T(256)S(1)} all-reduce(f32[256]{0:T(256)S(1)} %bitcast.286), channel_id=1, replica_groups=mesh['gx'=8,'gy'=32] {'gx','gy'}, use_global_device_ids=true, to_apply=%region_10.11 | all-reduce | flops 256 | bytes 2048 | tf_op jit(solution)/shard_map/psum | solution.py:218
  738.7 7.9 copy.87
  746.6 6.0 reshape.371
  752.6 3.0 convolution_multiply_fusion.1
  757.4 5.2 reshape.372
  762.5 7.6 copy.89
  770.1 6.4 reshape.373
  779.2 2.3 collective-permute-done.13
  783.6 3.2 collective-permute-start.15
  788.3 6.1 reshape.374
  794.4 7.9 copy.90
  802.3 5.3 reshape.375
  811.2 4.2 reshape.380
  815.4 7.6 copy.101
  823.1 6.4 reshape.381
  831.6 2.6 collective-permute-done.17
  834.5 5.6 collective-permute-start.19
  844.9 6.1 reshape.382
  851.0 6.8 copy.102
  857.8 6.8 fusion.3
  866.0 75.2 %psum.70 = f32[2]{0:T(128)S(1)} all-reduce(f32[2]{0:T(128)S(1)} %pad_maximum_fusion.20), channel_id=1, replica_groups=mesh['gx'=8,'gy'=32] {'gx','gy'}, use_global_device_ids=true, to_apply=%region_13.14 | all-reduce | flops 2 | bytes 16 | tf_op jit(solution)/shard_map/psum | solution.py:185
  942.5 8.0 fusion.9
  952.5 73.7 %psum.71 = f32[1]{0:T(128)} all-reduce(f32[1]{0:T(128)} %bitcast.66), channel_id=1, replica_groups=mesh['gx'=8,'gy'=32] {'gx','gy'}, use_global_device_ids=true, to_apply=%region_15.16 | all-reduce | flops 1 | bytes 8 | tf_op jit(solution)/shard_map/psum | solution.py:185
  1027.0 2.6 bitcast_multiply_fusion
  1029.6 4.7 copy.105
  1034.3 5.3 mul.365
  (201 shorter events, 65.1 us)
Async XLA Ops:
  0.6 3.9 copy-start
  17.6 20.6 %copy-start.13 = (f32[1,1,153,256]{3,1,2,0:T(1,128)S(1)}, f32[1,1,153,256]{3,1,2,0:T(1,128)}, u32[]{:S(2)}) copy-start(f32[1,1,153,256]{3,1,2,0:T(1,128)} %param.20) | copy-start | bytes 470020
  17.6 21.0 %copy-start.2 = (f32[1,1,256]{2,1,0:T(1,128)S(1)}, f32[1,1,256]{2,1,0:T(1,128)}, u32[]{:S(2)}) copy-start(f32[1,1,256]{2,1,0:T(1,128)} %param.18) | copy-start | bytes 3076
  17.6 23.0 %copy-start.3 = (f32[1,1,256]{2,1,0:T(1,128)S(1)}, f32[1,1,256]{2,1,0:T(1,128)}, u32[]{:S(2)}) copy-start(f32[1,1,256]{2,1,0:T(1,128)} %param.19) | copy-start | bytes 3076
  24.0 4.0 collective-permute-start
  26.6 3.2 collective-permute-start.1
  30.0 12.6 %collective-permute-start.2 = (f32[32,1,128]{2,1,0:T(1,128)S(1)}, f32[32,1,128]{2,1,0:T(1,128)S(1)}, u32[]{:S(2)}, u32[]{:S(2)}) collective-permute-start(f32[32,1,128]{2,1,0:T(1,128)S(1)} %get-tuple-element.46), channel_id=1, source_target_pairs={{0,1},{1,2},{2,3},{3,4},{4,5},{5,6},{6,7},{7,8},{8,9},{9,10},{10,1... | collective-permute-start | bytes 49160 | tf_op jit(solution)/shard_map/ppermute | solution.py:20
  31.7 10.9 %collective-permute-start.3 = (f32[32,1,128]{2,1,0:T(1,128)S(1)}, f32[32,1,128]{2,1,0:T(1,128)S(1)}, u32[]{:S(2)}, u32[]{:S(2)}) collective-permute-start(f32[32,1,128]{2,1,0:T(1,128)S(1)} %get-tuple-element.47), channel_id=1, source_target_pairs={{1,0},{2,1},{3,2},{4,3},{5,4},{6,5},{7,6},{8,7},{9,8},{10,9},{11,1... | collective-permute-start | bytes 49160 | tf_op jit(solution)/shard_map/ppermute | solution.py:21
  149.0 1.9 copy-start.4
  149.1 1.9 copy-start.15
  151.0 2.8 copy-start.5
  151.0 62.5 %copy-start.6 = (f32[1,1,425,256]{3,1,2,0:T(1,128)S(1)}, f32[1,1,425,256]{3,1,2,0:T(1,128)}, u32[]{:S(2)}) copy-start(f32[1,1,425,256]{3,1,2,0:T(1,128)} %param.22) | copy-start | bytes 1305604
  307.7 5.4 copy-start.8
  307.7 5.4 copy-start.26
  313.1 8.1 copy-start.10
  335.2 2.7 collective-permute-start.4
  337.1 3.2 collective-permute-start.5
  340.4 6.0 collective-permute-start.6
  342.3 4.1 collective-permute-start.7
  361.0 6.5 copy-start.16
  361.0 6.5 copy-start.17
  361.0 6.5 copy-start.18
  361.0 6.5 copy-start.19
  361.0 6.5 copy-start.20
  361.0 6.5 copy-start.21
  361.0 6.5 copy-start.22
  361.0 6.4 copy-start.23
  361.0 7.9 copy-start.7
  361.0 7.9 copy-start.24
  393.4 2.0 collective-permute-start.8
  394.5 3.5 collective-permute-start.9
  399.7 6.5 collective-permute-start.10
  399.8 6.6 collective-permute-start.11
  589.2 3.3 copy-start.14
  746.6 6.0 copy-start.9
  776.5 2.7 collective-permute-start.12
  778.4 3.2 collective-permute-start.13
  781.7 6.0 collective-permute-start.14
  783.6 4.1 collective-permute-start.15
  823.1 7.7 copy-start.25
  823.1 17.0 %copy-start.11 = (f32[256,512]{0,1:T(8,128)S(1)}, f32[256,512]{0,1:T(8,128)}, u32[]{:S(2)}) copy-start(f32[256,512]{0,1:T(8,128)} %copy-done.10) | copy-start | bytes 1572868
  829.5 2.0 collective-permute-start.16
  830.7 3.5 collective-permute-start.17
  834.4 9.9 collective-permute-start.18
  834.5 9.8 collective-permute-start.19
  1034.3 6.5 copy-start.12
  1040.8 4.8 copy-start.1
where the time goes:
time: 1060 us; the launch traced here: 1050 us
  blocking collectives  674 us (64%)
  local copies, waits for them, and re-layouts  232 us (22%)
  other arithmetic  56.3 us (5%)
  starting transfers between devices  39.2 us (4%)
  matrix products  20.6 us (2%)
  waiting for transfers between devices  15.1 us (1%)
    psum x5, blocking collectives, global_sum(): return lax.psum(partial_sums, ('gx', 'gy'))  385 us
    psum x2, blocking collectives, coarse(): top_coeffs = lax.psum(top_part, ('gx', 'gy'))  171 us
    psum x2, blocking collectives, coarse(): column_coeffs = lax.psum(column_part, 'gy')  118 us
    reshape x8, local copies, waits for them, and re-layouts, assemble(): lattice.reshape(EX, NP, EY, NP, EZ, NP).transpose(0, 2, 4, 1, 3, 5)  51.9 us
    transpose x5, local copies, waits for them, and re-layouts, assemble(): lattice = element_field.reshape(EX, EY, EZ, NP, NP, NP).transpose(0, 3, 1...  38.2 us
    reshape x5, local copies, waits for them, and re-layouts, assemble(): lattice = element_field.reshape(EX, EY, EZ, NP, NP, NP).transpose(0, 3, 1...  32.7 us
    transpose x4, local copies, waits for them, and re-layouts, assemble(): lattice.reshape(EX, NP, EY, NP, EZ, NP).transpose(0, 2, 4, 1, 3, 5)  31.4 us
    reduce_sum x5, other arithmetic, global_sum(): jnp.sum(former * latter * weight)  29.7 us
  transfers between devices with their start and end apart: 20, of which 13 were waited for; matrix products, arithmetic and copies ran while one was open for 1% of the time, Pallas kernels for 0%

commit v1 on v0

v1 whole, which is shorter than its diff:
```python
import jax
import jax.numpy as jnp
import numpy as np
from jax import lax
from jax.experimental import pallas as pl
from jax.experimental.pallas import tpu as pltpu
from jax.sharding import PartitionSpec as P

NP = 8
EX = 4
EY = 4
EZ = 16
ROWS = EX * EY * EZ
NODES = NP * NP * NP
LEVELS = EZ + 1
F32 = jnp.float32
BF16 = jnp.bfloat16


def legendre_columns(points, degree):
    columns_table = np.zeros((points.shape[0], degree + 1))
    columns_table[:, 0] = 1.0
    columns_table[:, 1] = points
    for level_at in range(2, degree + 1):
        columns_table[:, level_at] = (
            (2 * level_at - 1) * points * columns_table[:, level_at - 1]
            - (level_at - 1) * columns_table[:, level_at - 2]
        ) / level_at
    return columns_table


def jacobi_eigen(symmetric, npoints):
    matrix_work = symmetric.copy()
    vectors = np.eye(npoints)
    for sweep_at in range(15):
        for first_at in range(npoints):
            for second_at in range(first_at + 1, npoints):
                off_value = matrix_work[first_at, second_at]
                gap_value = matrix_work[second_at, second_at] - matrix_work[first_at, first_at]
                root_value = np.sqrt(gap_value * gap_value + 4.0 * off_value * off_value)
                sign_value = np.where(gap_value >= 0.0, 1.0, -1.0)
                denominator = np.abs(gap_value) + root_value
                safe_denominator = np.where(denominator > 0.0, denominator, 1.0)
                tangent = sign_value * 2.0 * off_value / safe_denominator
                cosine_value = 1.0 / np.sqrt(1.0 + tangent * tangent)
                sine_value = tangent * cosine_value
                rotation = np.eye(npoints)
                rotation[first_at, first_at] = cosine_value
                rotation[second_at, second_at] = cosine_value
                rotation[first_at, second_at] = sine_value
                rotation[second_at, first_at] = -sine_value
                matrix_work = rotation.T @ matrix_work @ rotation
                vectors = vectors @ rotation
    eigvals = np.array([matrix_work[place_at, place_at] for place_at in range(npoints)])
    return (eigvals, vectors)


def gll_tables(npoints):
    degree = npoints - 1
    estimate = -np.cos(np.pi * np.arange(npoints) / degree)
    for newton_at in range(100):
        columns_table = legendre_columns(estimate, degree)
        estimate = estimate - (
            estimate * columns_table[:, degree] - columns_table[:, degree - 1]
        ) / (npoints * columns_table[:, degree])
    values = legendre_columns(estimate, degree)[:, degree]
    weights = 2.0 / (degree * (degree + 1) * values**2)
    derivative = np.zeros((npoints, npoints))
    for row_at in range(npoints):
        for column_at in range(npoints):
            if row_at != column_at:
                derivative[row_at, column_at] = (
                    values[row_at] / values[column_at] / (estimate[row_at] - estimate[column_at])
                )
    derivative[0, 0] = -degree * (degree + 1) / 4.0
    derivative[degree, degree] = degree * (degree + 1) / 4.0
    stiffness = derivative.T @ (weights[:, None] * derivative)
    inv_root = 1.0 / np.sqrt(weights)
    symmetric = inv_root[:, None] * stiffness * inv_root[None, :]
    eigvals, eigvecs = jacobi_eigen(0.5 * (symmetric + symmetric.T), npoints)
    modes = inv_root[:, None] * eigvecs
    return (estimate, weights, stiffness, eigvals, modes)


def split_pair(table):
    high = table.astype(np.float32).astype(jnp.bfloat16)
    low = (table.astype(np.float32) - high.astype(np.float32)).astype(jnp.bfloat16)
    return np.stack([high, low])


def build_tables():
    points, weights, stiffness, eigvals, modes = gll_tables(8)
    massmat = weights[:, None] * np.eye(8)
    filler = np.ones(8)
    stiff_full = (
        np.kron(np.kron(stiffness, massmat), massmat)
        + np.kron(np.kron(massmat, stiffness), massmat)
        + np.kron(np.kron(massmat, massmat), stiffness)
    )
    mass_full = np.kron(np.kron(weights, weights), weights)
    eigen_full = (
        np.kron(np.kron(eigvals, filler), filler)
        + np.kron(np.kron(filler, eigvals), filler)
        + np.kron(np.kron(filler, filler), eigvals)
    )
    shape_full = np.kron(np.kron(modes, modes), modes)
    linear = np.stack([(1.0 - points) / 2.0, (1.0 + points) / 2.0], 1)
    trilinear = np.kron(np.kron(linear, linear), linear)
    ends = np.where((np.arange(8) == 0) | (np.arange(8) == 7), 0.5, 1.0)
    share = np.kron(np.kron(ends, ends), ends)
    rows = np.zeros((8, NODES), np.float32)
    rows[0], rows[1], rows[2] = eigen_full, mass_full, share
    loads = np.zeros((NODES, 128))
    loads[:, :8] = trilinear
    return (
        jnp.asarray(split_pair(stiff_full)),
        jnp.asarray(split_pair(shape_full)),
        jnp.asarray(split_pair(loads)),
        jnp.asarray(split_pair(loads.T)),
        jnp.asarray(rows),
    )


def lanes(width=128):
    return lax.broadcasted_iota(jnp.int32, (1, width), 1)


def halves(x):
    high = x.astype(BF16)
    return high, (x - high.astype(F32)).astype(BF16)


def product(x, table, contract=0):
    high, low = halves(x)
    dims = (((1,), (contract,)), ((), ()))

    def dot(p, q):
        return lax.dot_general(p, q, dims, preferred_element_type=F32)

    return dot(high, table[0]) + (dot(low, table[0]) + dot(high, table[1]))


def permuted(chooser, x):
    high, rest = x.astype(BF16), x
    rest = rest - high.astype(F32)
    mid = rest.astype(BF16)
    low = (rest - mid.astype(F32)).astype(BF16)

    def dot(q):
        return jnp.dot(chooser, q, preferred_element_type=F32)

    return dot(high) + (dot(mid) + dot(low))


def columns(x):
    return [x[:, 128 * c : 128 * c + 128] for c in range(4)]


def weight_of(share):
    lane = lanes(NODES) % NP
    level = lax.broadcasted_iota(jnp.int32, (ROWS, 1), 0) % EZ
    end = ((lane == 0) & (level == 0)) | ((lane == NP - 1) & (level == EZ - 1))
    return jnp.where(end, 2.0 * share, share)


def assemble_inside(cols):
    lane = lanes()
    zero = jnp.zeros((64, 128), F32)
    up = jnp.where(lane < 64, pltpu.roll(cols[3], 64, 1)[:192], 0.0)
    down = jnp.where(lane >= 64, pltpu.roll(cols[0], 64, 1)[64:], 0.0)
    cols = [
        cols[0] + jnp.concatenate([zero, up], 0),
        cols[1],
        cols[2],
        cols[3] + jnp.concatenate([down, zero], 0),
    ]
    row_y = lane // NP % NP
    row_z = lane % NP
    level = lax.broadcasted_iota(jnp.int32, (ROWS, 1), 0) % EZ
    from_below = (row_z == 0) & (level > 0)
    from_above = (row_z == NP - 1) & (level < EZ - 1)
    edge = jnp.zeros((EX, 1, EZ, 128), F32)
    result = []
    for col in cols:
        up = jnp.where(row_y == 0, pltpu.roll(col, 72, 1), 0.0).reshape(EX, EY, EZ, 128)
        down = jnp.where(row_y == NP - 1, pltpu.roll(col, 56, 1), 0.0).reshape(EX, EY, EZ, 128)
        col = (
            col
            + jnp.concatenate([edge, up[:, : EY - 1]], 1).reshape(ROWS, 128)
            + jnp.concatenate([down[:, 1:], edge], 1).reshape(ROWS, 128)
        )
        up = pltpu.roll(pltpu.roll(col, 121, 1), 1, 0)
        down = pltpu.roll(pltpu.roll(col, 7, 1), ROWS - 1, 0)
        result.append(col + jnp.where(from_below, up, 0.0) + jnp.where(from_above, down, 0.0))
    return result


def write_faces(cols, part_ref, face_x_ref, face_y_ref):
    row_y = lanes() // NP % NP
    for c in range(4):
        part_ref[:, 128 * c : 128 * c + 128] = cols[c]
    face_x_ref[0] = cols[0][:64]
    face_x_ref[1] = cols[3][192:]
    low = jnp.zeros((64, 128), F32)
    high = jnp.zeros((64, 128), F32)
    for c in range(4):
        blocks = cols[c].reshape(EX, EY, EZ, 128)
        first = jnp.where(row_y == 0, blocks[:, 0].reshape(64, 128), 0.0)
        last = jnp.where(row_y == NP - 1, blocks[:, EY - 1].reshape(64, 128), 0.0)
        low = low + (pltpu.roll(first, 8 * c, 1) if c else first)
        high = high + pltpu.roll(last, (72 + 8 * c) % 128, 1)
    face_y_ref[0] = low
    face_y_ref[1] = high


def edge_kernel(face_y_ref, before_ref, after_ref, out_low_ref, out_high_ref):
    lane = lanes()
    first = lane < 8
    last = (lane >= 88) & (lane < 96)
    out_low_ref[...] = face_y_ref[0]
    out_high_ref[...] = face_y_ref[1]
    out_low_ref[0:16] += jnp.where(first, pltpu.roll(before_ref[0:16], 64, 1), 0.0)
    out_high_ref[0:16] += jnp.where(first, pltpu.roll(before_ref[48:64], 8, 1), 0.0)
    out_low_ref[48:64] += jnp.where(last, pltpu.roll(after_ref[0:16], 88, 1), 0.0)
    out_high_ref[48:64] += jnp.where(last, pltpu.roll(after_ref[48:64], 32, 1), 0.0)


def finish(part_ref, before_x_ref, after_x_ref, before_y_ref, after_y_ref):
    lane = lanes()
    row_y = lane // NP % NP
    rest = jnp.zeros((192, 128), F32)
    before = jnp.where(lane < 64, pltpu.roll(before_x_ref[...], 64, 1), 0.0)
    after = jnp.where(lane >= 64, pltpu.roll(after_x_ref[...], 64, 1), 0.0)
    before_y, after_y = before_y_ref[...], after_y_ref[...]
    hole = jnp.zeros((EX, EY - 2, EZ, 128), F32)
    result = []
    for c in range(4):
        col = part_ref[:, 128 * c : 128 * c + 128]
        if c == 0:
            col = col + jnp.concatenate([before, rest], 0)
        if c == 3:
            col = col + jnp.concatenate([rest, after], 0)
        low = pltpu.roll(before_y, (128 - 8 * c) % 128, 1) if c else before_y
        low = jnp.where(row_y == 0, low, 0.0).reshape(EX, 1, EZ, 128)
        high = jnp.where(row_y == NP - 1, pltpu.roll(after_y, 56 - 8 * c, 1), 0.0)
        high = high.reshape(EX, 1, EZ, 128)
        result.append(col + jnp.concatenate([low, hole, high], 1).reshape(ROWS, 128))
    return jnp.concatenate(result, 1)


def factor_rows(ref, at, count):
    if at < count - 1:
        return ref[pl.ds(LEVELS * at, 24), :]
    return pltpu.roll(ref[pl.ds(LEVELS * count - 24, 24), :], LEVELS, 0)


def loads_of(unassembled, loads, leaf_ref, column_ref, top_ref, coeff_ref, leaf_out_ref):
    corner = product(unassembled, loads)
    lane = lanes()
    pad = jnp.zeros((8, 128), F32)
    lifted = []
    for at in range(EX * EY):
        piece = corner[16 * at : 16 * at + 16]
        same = jnp.concatenate([jnp.where(lane % 2 == 0, piece, 0.0), pad], 0)
        above = jnp.concatenate([jnp.where(lane % 2 == 1, piece, 0.0), pad], 0)
        lifted.append(same + pltpu.roll(above, 1, 0))
    top_sum = jnp.zeros((24, 256), F32)
    column_sum = jnp.zeros((24, 256), F32)
    leaf_sum = jnp.zeros((24, 256), F32)
    for vx in range(EX + 1):
        for vy in range(EY + 1):
            total = jnp.zeros((24, 128), F32)
            for sx in (0, 1):
                for sy in (0, 1):
                    if 0 <= vx - sx < EX and 0 <= vy - sy < EY:
                        piece = lifted[(vx - sx) * EY + vy - sy]
                        total = total + jnp.where(lane // 2 == sx * 2 + sy, piece, 0.0)
            vertex = jnp.sum(total, axis=1, keepdims=True)
            at = vx * (EY + 1) + vy
            top_sum = top_sum + factor_rows(top_ref, at, 25) * vertex
            if 0 < vx < EX:
                column_sum = column_sum + factor_rows(column_ref, at, 25) * vertex
                if 0 < vy < EY:
                    leaf_sum = leaf_sum + factor_rows(leaf_ref, (vx - 1) * 3 + vy - 1, 9) * vertex
    coeff_ref[...] = jnp.zeros((8, 128), F32)
    for at, total in ((0, top_sum), (4, column_sum)):
        total = jnp.sum(total, axis=0, keepdims=True)
        coeff_ref[at : at + 1] = total[:, :128]
        coeff_ref[at + 1 : at + 2] = total[:, 128:]
    leaf_out_ref[...] = jnp.sum(leaf_sum, axis=0, keepdims=True)


def coarse_of(coeffs, leaf_coeffs, spread, leaf_ref, column_ref, top_ref):
    lane = lanes()
    top = jnp.concatenate([coeffs[0:1], coeffs[1:2]], 1)
    column = jnp.concatenate([coeffs[4:5], coeffs[5:6]], 1)
    around = []
    for vx in range(EX + 1):
        for vy in range(EY + 1):
            at = vx * (EY + 1) + vy
            total = factor_rows(top_ref, at, 25) * top
            if 0 < vx < EX:
                total = total + factor_rows(column_ref, at, 25) * column
                if 0 < vy < EY:
                    total = total + factor_rows(leaf_ref, (vx - 1) * 3 + vy - 1, 9) * leaf_coeffs
            vertex = jnp.sum(total, axis=1, keepdims=True)
            same = jnp.broadcast_to(vertex, (24, 128))
            around.append(jnp.where(lane % 2 == 0, same, pltpu.roll(same, 23, 0))[:16])
    corners = []
    for ex in range(EX):
        for ey in range(EY):
            value = jnp.zeros((16, 128), F32)
            for sx in (0, 1):
                for sy in (0, 1):
                    piece = around[(ex + sx) * (EY + 1) + ey + sy]
                    value = jnp.where(lane // 2 == sx * 2 + sy, piece, value)
            corners.append(value)
    return product(jnp.concatenate(corners, 0), spread)


def start_kernel(
    order_ref, forcing_ref, diffusivity_ref, reaction_ref, leaf_ref, column_ref, top_ref, loads_ref,
    part_ref, face_x_ref, face_y_ref, coeff_ref, leaf_out_ref, pair_ref,
):
    slot = lax.broadcasted_iota(jnp.int32, (ROWS, ROWS), 0)
    chooser = (order_ref[...] == slot).astype(F32)
    diffusion = jnp.sum(chooser * diffusivity_ref[...], axis=1, keepdims=True)
    reacting = jnp.sum(chooser * reaction_ref[...], axis=1, keepdims=True)
    lane = lanes()
    pair_ref[...] = jnp.where(lane == 0, diffusion, reacting)
    source = permuted(chooser.astype(BF16), forcing_ref[...])
    write_faces(assemble_inside(columns(source)), part_ref, face_x_ref, face_y_ref)
    loads_of(source, loads_ref[...], leaf_ref, column_ref, top_ref, coeff_ref, leaf_out_ref)


def smooth_kernel(
    part_ref, before_x_ref, after_x_ref, before_y_ref, after_y_ref, pair_ref, shape_ref, rows_ref,
    field_ref, out_ref, face_x_ref, face_y_ref,
):
    field = finish(part_ref, before_x_ref, after_x_ref, before_y_ref, after_y_ref)
    field_ref[...] = field
    pair = pair_ref[...]
    scale = 1.0 / (pair[:, 0:1] * rows_ref[0:1] + pair[:, 1:2])
    table = shape_ref[...]
    smoothed = product(product(field, table) * scale, table, 1)
    write_faces(assemble_inside(columns(smoothed)), out_ref, face_x_ref, face_y_ref)


def stiffness_of(field, pair, stiff_ref, rows_ref):
    return product(field, stiff_ref[...]) * pair[:, 0:1] + field * (rows_ref[1:2] * pair[:, 1:2])


def total_of(x):
    return jnp.sum(jnp.sum(x, axis=0, keepdims=True), axis=1, keepdims=True)


def numbers_row(values):
    lane = lanes()
    row = jnp.zeros((1, 128), F32)
    for at, value in enumerate(values):
        row = jnp.where(lane == at, value, row)
    return row


def first_kernel(
    part_ref, before_x_ref, after_x_ref, before_y_ref, after_y_ref, pair_ref, stiff_ref, rows_ref,
    loads_ref, spread_ref, leaf_ref, column_ref, top_ref, coeff_in_ref, leaf_in_ref, source_ref,
    search_ref, out_ref, face_x_ref, face_y_ref, coeff_ref, leaf_out_ref,
):
    weight = weight_of(rows_ref[2:3])
    smoothed = finish(part_ref, before_x_ref, after_x_ref, before_y_ref, after_y_ref)
    search = smoothed * weight + coarse_of(
        coeff_in_ref[...], leaf_in_ref[...], spread_ref[...], leaf_ref, column_ref, top_ref
    )
    search_ref[...] = search
    image = stiffness_of(search, pair_ref[...], stiff_ref, rows_ref)
    write_faces(assemble_inside(columns(image)), out_ref, face_x_ref, face_y_ref)
    loads_of(image, loads_ref[...], leaf_ref, column_ref, top_ref, coeff_ref, leaf_out_ref)
    source = source_ref[...]
    coeff_ref[2:3] = numbers_row(
        [total_of(source * source * weight), total_of(image * source), total_of(image * image)]
    )


def second_kernel(
    part_ref, before_x_ref, after_x_ref, before_y_ref, after_y_ref, pair_ref, stiff_ref, rows_ref,
    spread_ref, leaf_ref, column_ref, top_ref, coeff_in_ref, leaf_in_ref, source_ref, search_ref,
    image_ref,
    second_ref, out_ref, face_x_ref, face_y_ref, sums_ref,
):
    weight = weight_of(rows_ref[2:3])
    coeffs = coeff_in_ref[...]
    norm, along, size = coeffs[2:3, 0:1], coeffs[2:3, 1:2], coeffs[2:3, 2:3]
    overlap = along / norm
    scale = 1.0 / jnp.sqrt(size)
    smoothed = finish(part_ref, before_x_ref, after_x_ref, before_y_ref, after_y_ref)
    whole = smoothed * weight + coarse_of(
        coeffs, leaf_in_ref[...], spread_ref[...], leaf_ref, column_ref, top_ref
    )
    second = (whole - overlap * search_ref[...]) * scale
    second_ref[...] = second
    source = source_ref[...]
    basis = (image_ref[...] - overlap * source) * scale
    image = stiffness_of(second, pair_ref[...], stiff_ref, rows_ref)
    write_faces(assemble_inside(columns(image)), out_ref, face_x_ref, face_y_ref)
    sums_ref[...] = numbers_row(
        [total_of(basis * basis * weight), total_of(image * source), total_of(image * basis)]
    )


def last_kernel(
    part_ref, before_x_ref, after_x_ref, before_y_ref, after_y_ref, rows_ref, sums_in_ref,
    image_ref, sums_ref,
):
    image = finish(part_ref, before_x_ref, after_x_ref, before_y_ref, after_y_ref)
    image_ref[...] = image
    square = total_of(image * image * weight_of(rows_ref[2:3]))
    sums_ref[...] = jnp.where(lanes() == 3, square, sums_in_ref[...])


def end_kernel(
    order_ref, sums_ref, coeff_ref, source_ref, search_one_ref, image_one_ref, search_two_ref,
    image_two_ref,
    pressure_ref, residual_ref,
):
    sums = jnp.sum(sums_ref[...], axis=0, keepdims=True)
    squared, dot_source, dot_basis, dot_self = (sums[:, at : at + 1] for at in range(4))
    coeffs = coeff_ref[...]
    norm, along, size = coeffs[2:3, 0:1], coeffs[2:3, 1:2], coeffs[2:3, 2:3]
    beta = jnp.sqrt(norm)
    basis_norm = jnp.sqrt(squared)
    first_diag = along / norm
    first_sub = basis_norm * jnp.sqrt(size) / beta
    second_top = dot_source / (beta * basis_norm)
    second_diag = dot_basis / squared
    second_sub_squared = jnp.maximum(
        dot_self / squared - second_top * second_top - second_diag * second_diag, 0.0
    )
    first_norm = jnp.sqrt(first_diag * first_diag + first_sub * first_sub)
    cosine = first_diag / first_norm
    sine_part = first_sub / first_norm
    rotated = cosine * second_top + sine_part * second_diag
    lowered = cosine * second_diag - sine_part * second_top
    second_norm = jnp.sqrt(lowered * lowered + second_sub_squared)
    factor_two = -(lowered / second_norm) * sine_part * beta / second_norm
    factor_one = (cosine * beta - rotated * factor_two) / first_norm
    step_one = factor_one / beta
    step_two = factor_two / basis_norm
    slot = lax.broadcasted_iota(jnp.int32, (ROWS, ROWS), 0)
    chooser = (order_ref[...] == slot).astype(F32).T.astype(BF16)
    pressure_ref[...] = permuted(
        chooser, step_one * search_one_ref[...] + step_two * search_two_ref[...]
    )
    residual_ref[...] = permuted(
        chooser, source_ref[...] - step_one * image_one_ref[...] - step_two * image_two_ref[...]
    )


FIELD = jax.ShapeDtypeStruct((ROWS, NODES), F32)
FACES = jax.ShapeDtypeStruct((2, 64, 128), F32)
FACE = jax.ShapeDtypeStruct((64, 128), F32)
COEFFS = jax.ShapeDtypeStruct((8, 128), F32)
LEAVES = jax.ShapeDtypeStruct((1, 256), F32)
NUMBERS = jax.ShapeDtypeStruct((1, 128), F32)
PAIRS = jax.ShapeDtypeStruct((ROWS, 128), F32)


def run(kernel, outs, *args):
    vmem = pl.BlockSpec(memory_space=pltpu.VMEM)
    return pl.pallas_call(
        kernel,
        out_shape=outs,
        in_specs=[vmem] * len(args),
        out_specs=tuple(vmem for _ in outs),
        compiler_params=pltpu.CompilerParams(vmem_limit_bytes=24 * 2**20),
    )(*args)


def neighbours(low, high, axis):
    peers = lax.axis_size(axis)
    up = [(i, (i + 1) % peers) for i in range(peers)]
    down = [(j, i) for i, j in up]
    return lax.ppermute(high, axis, up), lax.ppermute(low, axis, down)


def exchanged(face_x, face_y):
    before_x, after_x = neighbours(face_x[0], face_x[1], "gx")
    low, high = run(edge_kernel, (FACE, FACE), face_y, before_x, after_x)
    before_y, after_y = neighbours(low, high, "gy")
    return before_x, after_x, before_y, after_y


def summed(coeffs):
    shared = lax.psum(coeffs[:4], "gx")
    mine = jnp.concatenate([shared, coeffs[4:]], 0)
    peers = lax.axis_size("gy")
    spread = jnp.broadcast_to(mine[None], (peers, 8, 128))
    return jnp.sum(lax.all_to_all(spread, "gy", 0, 0), 0)


def per_device(
    forcing, element_order, diffusivity, reaction, leaf_factor, column_factor, top_factor
):
    stiff, shape, loads, spread, rows = build_tables()
    factors = (leaf_factor[0, 0], column_factor[0, 0], top_factor[0, 0])
    order = element_order[0]
    part, face_x, face_y, coeffs, leaves, pair = run(
        start_kernel,
        (FIELD, FACES, FACES, COEFFS, LEAVES, PAIRS),
        order, forcing[0, 0], diffusivity[0], reaction[0], *factors, loads,
    )
    coeffs = summed(coeffs)
    source, part, face_x, face_y = run(
        smooth_kernel, (FIELD, FIELD, FACES, FACES), part, *exchanged(face_x, face_y), pair, shape, rows
    )
    search_one, part, face_x, face_y, coeffs, leaves = run(
        first_kernel,
        (FIELD, FIELD, FACES, FACES, COEFFS, LEAVES),
        part, *exchanged(face_x, face_y), pair, stiff, rows, loads, spread, *factors, coeffs, leaves,
        source,
    )
    coeffs = summed(coeffs)
    image_one, part, face_x, face_y = run(
        smooth_kernel, (FIELD, FIELD, FACES, FACES), part, *exchanged(face_x, face_y), pair, shape, rows
    )
    search_two, part, face_x, face_y, sums = run(
        second_kernel,
        (FIELD, FIELD, FACES, FACES, NUMBERS),
        part, *exchanged(face_x, face_y), pair, stiff, rows, spread, *factors, coeffs, leaves, source,
        search_one, image_one,
    )
    image_two, sums = run(
        last_kernel, (FIELD, NUMBERS), part, *exchanged(face_x, face_y), rows, sums
    )
    peers = lax.axis_size(("gx", "gy"))
    sums = lax.all_to_all(jnp.broadcast_to(sums, (peers, 128)), ("gx", "gy"), 0, 0, tiled=True)
    pressure, residual = run(
        end_kernel, (FIELD, FIELD),
        order, sums, coeffs, source, search_one, image_one, search_two, image_two,
    )
    return (pressure[None, None], residual[None, None])


def solution(mesh):
    field = P("gx", "gy", None, None)
    row = P("gx", "gy", None)
    return jax.shard_map(
        per_device,
        mesh=mesh,
        in_specs=(field, row, row, row, field, field, field),
        out_specs=(field, field),
        check_vma=False,
    )
```

time: 1060 us -> 166 us (0.16); the launches traced: 1050 us -> 164 us
  blocking collectives: 674 us -> 49.6 us
  local copies, waits for them, and re-layouts: 232 us -> 31.3 us
  other arithmetic: 56.3 us -> 2.49 us
  starting transfers between devices: 39.2 us -> 59.9 us
  matrix products: 20.6 us -> 0 us
  Pallas kernels: 0 us -> 15 us
    psum x9 -> x2, blocking collectives: 674 us -> 25.2 us  [summed(): shared = lax.psum(coeffs[:4], 'gx')]
    reshape x32 -> x0, local copies, waits for them, and re-layouts: 134 us -> none  [the longest x8 51.9 us: assemble(): lattice.reshape(EX, NP, EY, NP, EZ, NP).transpose(0, 2, 4, 1, 3, 5)]
    transpose x9 -> x0, local copies, waits for them, and re-layouts: 69.6 us -> none  [the longest x5 38.2 us: assemble(): lattice = element_field.reshape(EX, EY, EZ, NP, NP, NP).transpose(0, 3, 1...]
    reduce_sum x5 -> x2, other arithmetic: 29.7 us -> 2.47 us  [summed(): return jnp.sum(lax.all_to_all(spread, 'gy', 0, 0), 0)]
    unnamed x70 -> x100, local copies, waits for them, and re-layouts: 3.04 us -> 28.6 us
    all_to_all x0 -> x1, blocking collectives: none -> 24.4 us  [per_device(): lax.all_to_all(jnp.broadcast_to(sums, (peers, 128)), ('gx', 'gy'), 0, 0,...]
    dot_general x20 -> x0, matrix products: 20.6 us -> none  [the longest x2 4.55 us: coarse(): jnp.dot(residue * weight, linear_table, precision=highest, preferred_elem...]
    pallas_call x0 -> x12, Pallas kernels: none -> 15 us  [run(): pl.pallas_call(kernel, out_shape=outs, in_specs=[vmem] * len(args), out_s...]
  transfers between devices with their start and end apart: 20 -> 22, of which waited for: 13 -> 9; matrix products, arithmetic and copies ran while one was open for 1% -> 3% of each run, Pallas kernels for 0% -> 3%
where the time goes in v1:
time: 166 us; the launch traced here: 164 us
  starting transfers between devices  59.9 us (36%)
  blocking collectives  49.6 us (30%)
  local copies, waits for them, and re-layouts  31.3 us (19%)
  Pallas kernels  15 us (9%)
  waiting for transfers between devices  5.29 us (3%)
  other arithmetic  2.49 us (2%)
    ppermute x20, starting transfers between devices, neighbours(): return (lax.ppermute(high, axis, up), lax.ppermute(low, axis, down))  48.3 us
    unnamed x100, local copies, waits for them, and re-layouts  28.6 us
    psum x2, blocking collectives, summed(): shared = lax.psum(coeffs[:4], 'gx')  25.2 us
    all_to_all x1, blocking collectives, per_device(): lax.all_to_all(jnp.broadcast_to(sums, (peers, 128)), ('gx', 'gy'), 0, 0,...  24.4 us
    pallas_call x12, Pallas kernels, run(): pl.pallas_call(kernel, out_shape=outs, in_specs=[vmem] * len(args), out_s...  15 us
    all_to_all x2, starting transfers between devices, summed(): return jnp.sum(lax.all_to_all(spread, 'gy', 0, 0), 0)  11.6 us
    ppermute x20, waiting for transfers between devices, neighbours(): return (lax.ppermute(high, axis, up), lax.ppermute(low, axis, down))  5.29 us
  transfers between devices with their start and end apart: 22, of which 9 were waited for; matrix products, arithmetic and copies ran while one was open for 3% of the time, Pallas kernels for 3%

profile of v1, /device:TPU:1, one launch (start us, length us, event | category | flops | bytes accessed | tf_op | source)
XLA Modules:
  0.0 164.5 jit_solution(11418566150396997849)
XLA Ops:
  0.6 0.9 copy.20
  1.6 1.3 copy_bitcast_fusion
  3.6 1.4 shard_map.131
  5.1 0.8 copy-done.22
  6.4 3.2 %collective-permute-start.1 = (f32[64,128]{1,0:T(8,128)S(1)}, f32[64,128]{1,0:T(8,128)S(1)}, u32[]{:S(2)}, u32[]{:S(2)}) collective-permute-start(f32[64,128]{1,0:T(8,128)S(1)} %get-tuple-element.88), channel_id=1, source_target_pairs={{32,0},{64,32},{96,64},{128,96},{160,128},{192,160},{224,192},{0,2... | collective-permute-start | bytes 98312 | tf_op jit(solution)/shard_map/ppermute | solution.py:483
  9.7 12.3 %psum.14 = f32[4,128]{1,0:T(4,128)S(1)} all-reduce(f32[4,128]{1,0:T(4,128)S(1)} %get-tuple-element.92), channel_id=1, replica_groups=mesh['gx'=8,'gy'=32] {'gx'}, use_global_device_ids=true, to_apply=%region_0.0 | all-reduce | flops 512 | bytes 4096 | tf_op jit(solution)/shard_map/psum | solution.py:494
  22.6 1.6 collective-permute-start.2
  24.2 6.4 %collective-permute-start.3 = (f32[64,128]{1,0:T(8,128)S(1)}, f32[64,128]{1,0:T(8,128)S(1)}, u32[]{:S(2)}, u32[]{:S(2)}) collective-permute-start(f32[64,128]{1,0:T(8,128)S(1)} %get-tuple-element.45), channel_id=1, source_target_pairs={{1,0},{2,1},{3,2},{4,3},{5,4},{6,5},{7,6},{8,7},{9,8},{10,9},{11,1... | collective-permute-start | bytes 98312 | tf_op jit(solution)/shard_map/ppermute | solution.py:483
  30.6 0.7 broadcast_in_dim.10
  31.2 6.1 %all-to-all-start = ((f32[32,8,128]{2,1,0:T(8,128)}), f32[32,8,128]{2,1,0:T(8,128)}, u32[]{:S(2)}, u32[]{:S(2)}) async-start(f32[32,8,128]{2,1,0:T(8,128)} %broadcast_in_dim.10), calls=%async_computation | async-start | bytes 262144 | tf_op jit(solution)/shard_map/all_to_all | solution.py:498
  38.0 0.6 copy-done.36
  38.6 0.9 copy-done.6
  39.5 1.0 copy-done.23
  40.5 0.8 copy-done.29
  41.3 0.8 copy-done.35
  42.1 0.8 copy-done.37
  42.8 1.7 %shard_map.133 = (f32[256,512]{1,0:T(8,128)S(1)}, f32[256,512]{1,0:T(8,128)S(1)}, f32[2,64,128]{2,1,0:T(8,128)S(1)}, f32[2,64,128]{2,1,0:T(8,128)S(1)}) custom-call(f32[256,512]{1,0:T(8,128)S(1)} %copy-done.23, f32[64,128]{1,0:T(8,128)S(1)} %copy-done.29, f32[64,128]{1,0:T(8,128)S(1)} %collective-permute-done.1.after_ref.after_x_ref, ...), custom_call_target="tpu_custom_call" | custom-call | tf_op jit(solution)/shard_map/pallas_call | solution.py:470
  44.5 0.8 copy-done.24
  45.3 4.4 %collective-permute-start.5 = (f32[64,128]{1,0:T(8,128)S(1)}, f32[64,128]{1,0:T(8,128)S(1)}, u32[]{:S(2)}, u32[]{:S(2)}) collective-permute-start(f32[64,128]{1,0:T(8,128)S(1)} %get-tuple-element.86), channel_id=1, source_target_pairs={{32,0},{64,32},{96,64},{128,96},{160,128},{192,160},{224,192},{0,2... | collective-permute-start | bytes 98312 | tf_op jit(solution)/shard_map/ppermute | solution.py:483
  49.8 0.9 collective-permute-done.5.after_ref.after_x_ref
  51.0 0.7 shard_map.134
  51.7 1.4 collective-permute-start.6
  53.1 3.4 %collective-permute-start.7 = (f32[64,128]{1,0:T(8,128)}, f32[64,128]{1,0:T(8,128)}, u32[]{:S(2)}, u32[]{:S(2)}) collective-permute-start(f32[64,128]{1,0:T(8,128)} %get-tuple-element.51), channel_id=1, source_target_pairs={{1,0},{2,1},{3,2},{4,3},{5,4},{6,5},{7,6},{8,7},{9,8},{10,9},{11,1... | collective-permute-start | bytes 98312 | tf_op jit(solution)/shard_map/ppermute | solution.py:483
  56.5 1.5 reduce_sum.18.coeff_in_ref
  58.8 0.9 copy-done.3
  59.7 0.9 copy-done.7
  60.6 0.9 copy-done.14
  61.6 0.9 copy-done.17
  62.5 1.0 copy-done.25
  63.6 0.8 copy-done.31
  64.3 2.8 %shard_map.135 = (f32[256,512]{1,0:T(8,128)S(1)}, f32[256,512]{1,0:T(8,128)S(1)}, f32[2,64,128]{2,1,0:T(8,128)S(1)}, f32[2,64,128]{2,1,0:T(8,128)S(1)}, f32[8,128]{1,0:T(8,128)S(1)}, /*index=5*/f32[1,256]{1,0:T(1,128)S(1)}) custom-call(f32[256,512]{1,0:T(8,128)S(1)} %copy-done.25, f32[64,128]{1,0:T(8,128)S(1)} %copy-done.31, ...), custom_call_target="tpu_custom_call" | custom-call | tf_op jit(solution)/shard_map/pallas_call | solution.py:470
  67.2 0.8 copy-done.10
  68.0 0.8 copy-done.18
  68.8 0.6 slice_bitcast_fusion.4
  69.4 4.4 %collective-permute-start.9 = (f32[64,128]{1,0:T(8,128)}, f32[64,128]{1,0:T(8,128)S(1)}, u32[]{:S(2)}, u32[]{:S(2)}) collective-permute-start(f32[64,128]{1,0:T(8,128)} %get-tuple-element.84), channel_id=1, source_target_pairs={{32,0},{64,32},{96,64},{128,96},{160,128},{192,160},{224,192},{0,2... | collective-permute-start | bytes 98312 | tf_op jit(solution)/shard_map/ppermute | solution.py:483
  74.4 12.9 %psum.15 = f32[4,128]{1,0:T(4,128)} all-reduce(f32[4,128]{1,0:T(4,128)} %get-tuple-element.90), channel_id=1, replica_groups=mesh['gx'=8,'gy'=32] {'gx'}, use_global_device_ids=true, to_apply=%region_2.0 | all-reduce | flops 512 | bytes 4096 | tf_op jit(solution)/shard_map/psum | solution.py:494
  87.4 0.8 copy-done.33
  88.2 1.5 shard_map.136
  89.7 5.1 %collective-permute-start.11 = (f32[64,128]{1,0:T(8,128)}, f32[64,128]{1,0:T(8,128)}, u32[]{:S(2)}, u32[]{:S(2)}) collective-permute-start(f32[64,128]{1,0:T(8,128)} %get-tuple-element.59), channel_id=1, source_target_pairs={{1,0},{2,1},{3,2},{4,3},{5,4},{6,5},{7,6},{8,7},{9,8},{10,9},{11,1... | collective-permute-start | bytes 98312 | tf_op jit(solution)/shard_map/ppermute | solution.py:483
  94.9 0.7 broadcast_in_dim.11
  95.5 5.5 %all-to-all-start.1 = ((f32[32,8,128]{2,1,0:T(8,128)}), f32[32,8,128]{2,1,0:T(8,128)}, u32[]{:S(2)}, u32[]{:S(2)}) async-start(f32[32,8,128]{2,1,0:T(8,128)} %broadcast_in_dim.11), calls=%async_computation.1 | async-start | bytes 262144 | tf_op jit(solution)/shard_map/all_to_all | solution.py:498
  101.1 0.9 copy-done.8
  102.0 1.0 copy-done.19
  103.0 2.5 %shard_map.137 = (f32[256,512]{1,0:T(8,128)S(1)}, f32[256,512]{1,0:T(8,128)S(1)}, f32[2,64,128]{2,1,0:T(8,128)S(1)}, f32[2,64,128]{2,1,0:T(8,128)S(1)}) custom-call(f32[256,512]{1,0:T(8,128)S(1)} %copy-done.19, f32[64,128]{1,0:T(8,128)} %collective-permute-done.8.before_ref.before_x_ref, f32[64,128]{1,0:T(8,128)S(1)} %collective-permute-done.9.after_ref.after_x_ref, ...), custom_call_target="tpu_custom_call" | custom-call | tf_op jit(solution)/shard_map/pallas_call | solution.py:470
  105.5 0.8 copy-done.12
  106.4 0.8 copy-done.20
  107.2 3.7 %collective-permute-start.13 = (f32[64,128]{1,0:T(8,128)S(1)}, f32[64,128]{1,0:T(8,128)S(1)}, u32[]{:S(2)}, u32[]{:S(2)}) collective-permute-start(f32[64,128]{1,0:T(8,128)S(1)} %get-tuple-element.82), channel_id=1, source_target_pairs={{32,0},{64,32},{96,64},{128,96},{160,128},{192,160},{224,192},{0,2... | collective-permute-start | bytes 98312 | tf_op jit(solution)/shard_map/ppermute | solution.py:483
  110.8 0.9 collective-permute-done.13.after_ref.after_x_ref
  112.1 1.3 collective-permute-start.14
  113.4 3.5 %collective-permute-start.15 = (f32[64,128]{1,0:T(8,128)S(1)}, f32[64,128]{1,0:T(8,128)S(1)}, u32[]{:S(2)}, u32[]{:S(2)}) collective-permute-start(f32[64,128]{1,0:T(8,128)S(1)} %get-tuple-element.64), channel_id=1, source_target_pairs={{1,0},{2,1},{3,2},{4,3},{5,4},{6,5},{7,6},{8,7},{9,8},{10,9},{11,1... | collective-permute-start | bytes 98312 | tf_op jit(solution)/shard_map/ppermute | solution.py:483
  116.9 0.9 reduce_sum.19.coeff_in_ref.coeff_ref
  118.2 0.7 copy-done.44
  118.9 1.0 copy-done.11
  119.9 1.0 copy-done.13
  121.0 0.9 copy-done.15
  121.9 1.0 copy-done.21
  123.0 2.0 %shard_map.139 = (f32[256,512]{1,0:T(8,128)S(1)}, f32[256,512]{1,0:T(8,128)S(1)}, f32[2,64,128]{2,1,0:T(8,128)S(1)}, f32[2,64,128]{2,1,0:T(8,128)S(1)}, f32[1,128]{1,0:T(1,128)S(1)}) custom-call(f32[256,512]{1,0:T(8,128)S(1)} %copy-done.21, f32[64,128]{1,0:T(8,128)S(1)} %collective-permute-done.12.before_ref.before_x_ref, ...), custom_call_target="tpu_custom_call" | custom-call | tf_op jit(solution)/shard_map/pallas_call | solution.py:470
  124.9 4.5 %collective-permute-start.17 = (f32[64,128]{1,0:T(8,128)S(1)}, f32[64,128]{1,0:T(8,128)S(1)}, u32[]{:S(2)}, u32[]{:S(2)}) collective-permute-start(f32[64,128]{1,0:T(8,128)S(1)} %get-tuple-element.80), channel_id=1, source_target_pairs={{32,0},{64,32},{96,64},{128,96},{160,128},{192,160},{224,192},{0,2... | collective-permute-start | bytes 98312 | tf_op jit(solution)/shard_map/ppermute | solution.py:483
  129.5 0.9 collective-permute-done.17.after_ref.after_x_ref
  130.8 5.1 %collective-permute-start.19 = (f32[64,128]{1,0:T(8,128)S(1)}, f32[64,128]{1,0:T(8,128)S(1)}, u32[]{:S(2)}, u32[]{:S(2)}) collective-permute-start(f32[64,128]{1,0:T(8,128)S(1)} %get-tuple-element.73), channel_id=1, source_target_pairs={{1,0},{2,1},{3,2},{4,3},{5,4},{6,5},{7,6},{8,7},{9,8},{10,9},{11,1... | collective-permute-start | bytes 98312 | tf_op jit(solution)/shard_map/ppermute | solution.py:483
  135.9 1.2 collective-permute-done.18.before_y_ref
  137.4 24.4 %all_to_all.18 = f32[256,1,128]{2,1,0:T(1,128)S(1)} all-to-all(f32[256,1,128]{2,1,0:T(1,128)S(1)} %broadcast_in_dim.12), channel_id=1, replica_groups=mesh['gx'=8,'gy'=32] {'gx','gy'}, dimensions={0} | all-to-all | bytes 262144 | tf_op jit(solution)/shard_map/all_to_all | solution.py:536
  161.8 0.7 copy-done.40
  162.5 1.9 %shard_map.142 = (f32[256,512]{1,0:T(8,128)}, f32[256,512]{1,0:T(8,128)}) custom-call(s32[1,256]{1,0:T(1,128)S(1)} %bitcast.41, f32[256,128]{1,0:T(8,128)S(1)} %bitcast.38, f32[8,128]{1,0:T(8,128)S(1)} %reduce_sum.19.coeff_in_ref.coeff_ref, f32[256,512]{1,0:T(8,128)S(1)} %get-tuple-element.54.source_ref, f32[256,512]{1,0:T(8,128)S(1)} %copy-done.11, ...), custom_call_target="tpu_custom_call" | custom-call | tf_op jit(solution)/shard_map/pallas_call | solution.py:470
  (109 shorter events, 5.9 us)
Async XLA Ops:
  1.6 1.4 copy-start.2
  1.6 1.4 copy-start.16
  1.6 1.4 copy-start.26
  1.6 1.4 copy-start.41
  1.6 1.4 copy-start.42
  2.9 0.7 copy-start.39
  3.6 35.0 %copy-start = (bf16[2,512,512]{2,1,0:T(8,128)(2,1)S(1)}, bf16[2,512,512]{2,1,0:T(8,128)(2,1)}, u32[]{:S(2)}) copy-start(bf16[2,512,512]{2,1,0:T(8,128)(2,1)} %constant.13.clone.shape_ref) | copy-start | bytes 3145732
  5.1 0.8 copy-start.22
  5.9 16.2 %copy-start.5 = (f32[256,128]{1,0:T(8,128)}, f32[256,128]{1,0:T(8,128)S(1)}, u32[]{:S(2)}) copy-start(f32[256,128]{1,0:T(8,128)S(1)} %get-tuple-element.46.pair_ref) | copy-start | bytes 393220
  6.4 15.5 %collective-permute-start.1 = (f32[64,128]{1,0:T(8,128)S(1)}, f32[64,128]{1,0:T(8,128)S(1)}, u32[]{:S(2)}, u32[]{:S(2)}) collective-permute-start(f32[64,128]{1,0:T(8,128)S(1)} %get-tuple-element.88), channel_id=1, source_target_pairs={{32,0},{64,32},{96,64},{128,96},{160,128},{192,160},{224,192},{0,2... | collective-permute-start | bytes 98312 | tf_op jit(solution)/shard_map/ppermute | solution.py:483
  9.7 12.3 %collective-permute-start = (f32[64,128]{1,0:T(8,128)S(1)}, f32[64,128]{1,0:T(8,128)S(1)}, u32[]{:S(2)}, u32[]{:S(2)}) collective-permute-start(f32[64,128]{1,0:T(8,128)S(1)} %get-tuple-element.89), channel_id=1, source_target_pairs={{0,32},{32,64},{64,96},{96,128},{128,160},{160,192},{192,224},{224... | collective-permute-start | bytes 98312 | tf_op jit(solution)/shard_map/ppermute | solution.py:483
  22.6 14.8 %collective-permute-start.2 = (f32[64,128]{1,0:T(8,128)S(1)}, f32[64,128]{1,0:T(8,128)S(1)}, u32[]{:S(2)}, u32[]{:S(2)}) collective-permute-start(f32[64,128]{1,0:T(8,128)S(1)} %get-tuple-element.44), channel_id=1, source_target_pairs={{0,1},{1,2},{2,3},{3,4},{4,5},{5,6},{6,7},{7,8},{8,9},{9,10},{10,1... | collective-permute-start | bytes 98312 | tf_op jit(solution)/shard_map/ppermute | solution.py:483
  24.2 13.8 %collective-permute-start.3 = (f32[64,128]{1,0:T(8,128)S(1)}, f32[64,128]{1,0:T(8,128)S(1)}, u32[]{:S(2)}, u32[]{:S(2)}) collective-permute-start(f32[64,128]{1,0:T(8,128)S(1)} %get-tuple-element.45), channel_id=1, source_target_pairs={{1,0},{2,1},{3,2},{4,3},{5,4},{6,5},{7,6},{8,7},{9,8},{10,9},{11,1... | collective-permute-start | bytes 98312 | tf_op jit(solution)/shard_map/ppermute | solution.py:483
  31.2 7.3 %copy-start.27 = (f32[8,512]{1,0:T(8,128)S(1)}, f32[8,512]{1,0:T(8,128)}, u32[]{:S(2)}) copy-start(f32[8,512]{1,0:T(8,128)} %constant.16.clone.rows_ref) | copy-start | bytes 49156
  31.2 25.3 %all-to-all-start = ((f32[32,8,128]{2,1,0:T(8,128)}), f32[32,8,128]{2,1,0:T(8,128)}, u32[]{:S(2)}, u32[]{:S(2)}) async-start(f32[32,8,128]{2,1,0:T(8,128)} %broadcast_in_dim.10), calls=%async_computation | async-start | bytes 262144 | tf_op jit(solution)/shard_map/all_to_all | solution.py:498
  38.6 0.9 copy-start.6
  39.5 1.0 copy-start.23
  40.5 0.8 copy-start.29
  41.3 0.8 copy-start.35
  42.1 0.8 copy-start.37
  42.8 15.3 %copy-start.1 = (bf16[2,512,512]{2,1,0:T(8,128)(2,1)S(1)}, bf16[2,512,512]{2,1,0:T(8,128)(2,1)}, u32[]{:S(2)}) copy-start(bf16[2,512,512]{2,1,0:T(8,128)(2,1)} %constant.12.clone.stiff_ref) | copy-start | bytes 3145732
  44.5 0.8 copy-start.24
  45.3 5.3 %collective-permute-start.5 = (f32[64,128]{1,0:T(8,128)S(1)}, f32[64,128]{1,0:T(8,128)S(1)}, u32[]{:S(2)}, u32[]{:S(2)}) collective-permute-start(f32[64,128]{1,0:T(8,128)S(1)} %get-tuple-element.86), channel_id=1, source_target_pairs={{32,0},{64,32},{96,64},{128,96},{160,128},{192,160},{224,192},{0,2... | collective-permute-start | bytes 98312 | tf_op jit(solution)/shard_map/ppermute | solution.py:483
  49.8 1.2 collective-permute-start.4
  51.0 0.7 copy-start.30
  51.7 6.5 %collective-permute-start.6 = (f32[64,128]{1,0:T(8,128)}, f32[64,128]{1,0:T(8,128)}, u32[]{:S(2)}, u32[]{:S(2)}) collective-permute-start(f32[64,128]{1,0:T(8,128)} %get-tuple-element.50), channel_id=1, source_target_pairs={{0,1},{1,2},{2,3},{3,4},{4,5},{5,6},{6,7},{7,8},{8,9},{9,10},{10,1... | collective-permute-start | bytes 98312 | tf_op jit(solution)/shard_map/ppermute | solution.py:483
  53.1 5.0 %collective-permute-start.7 = (f32[64,128]{1,0:T(8,128)}, f32[64,128]{1,0:T(8,128)}, u32[]{:S(2)}, u32[]{:S(2)}) collective-permute-start(f32[64,128]{1,0:T(8,128)} %get-tuple-element.51), channel_id=1, source_target_pairs={{1,0},{2,1},{3,2},{4,3},{5,4},{6,5},{7,6},{8,7},{9,8},{10,9},{11,1... | collective-permute-start | bytes 98312 | tf_op jit(solution)/shard_map/ppermute | solution.py:483
  58.0 0.7 copy-start.38
  58.1 0.7 copy-start.46
  58.8 0.9 copy-start.3
  59.7 0.9 copy-start.7
  60.6 0.9 copy-start.14
  61.6 0.9 copy-start.17
  62.5 1.0 copy-start.25
  63.6 0.8 copy-start.31
  67.2 0.8 copy-start.10
  68.0 0.8 copy-start.18
  69.4 18.0 %collective-permute-start.9 = (f32[64,128]{1,0:T(8,128)}, f32[64,128]{1,0:T(8,128)S(1)}, u32[]{:S(2)}, u32[]{:S(2)}) collective-permute-start(f32[64,128]{1,0:T(8,128)} %get-tuple-element.84), channel_id=1, source_target_pairs={{32,0},{64,32},{96,64},{128,96},{160,128},{192,160},{224,192},{0,2... | collective-permute-start | bytes 98312 | tf_op jit(solution)/shard_map/ppermute | solution.py:483
  73.9 13.5 %collective-permute-start.8 = (f32[64,128]{1,0:T(8,128)}, f32[64,128]{1,0:T(8,128)}, u32[]{:S(2)}, u32[]{:S(2)}) collective-permute-start(f32[64,128]{1,0:T(8,128)} %get-tuple-element.85), channel_id=1, source_target_pairs={{0,32},{32,64},{64,96},{96,128},{128,160},{160,192},{192,224},{224... | collective-permute-start | bytes 98312 | tf_op jit(solution)/shard_map/ppermute | solution.py:483
  87.4 0.8 copy-start.33
  89.7 5.2 %copy-start.48 = (f32[4,128]{1,0:T(4,128)S(1)}, f32[4,128]{1,0:T(4,128)}, u32[]{:S(2)}) copy-start(f32[4,128]{1,0:T(4,128)} %get-tuple-element.91) | copy-start | bytes 6148
  89.7 5.2 %copy-start.47 = (f32[4,128]{1,0:T(4,128)S(1)}, f32[4,128]{1,0:T(4,128)}, u32[]{:S(2)}) copy-start(f32[4,128]{1,0:T(4,128)} %psum.15) | copy-start | bytes 6148
  89.7 11.4 %collective-permute-start.10 = (f32[64,128]{1,0:T(8,128)}, f32[64,128]{1,0:T(8,128)}, u32[]{:S(2)}, u32[]{:S(2)}) collective-permute-start(f32[64,128]{1,0:T(8,128)} %get-tuple-element.58), channel_id=1, source_target_pairs={{0,1},{1,2},{2,3},{3,4},{4,5},{5,6},{6,7},{7,8},{8,9},{9,10},{10,1... | collective-permute-start | bytes 98312 | tf_op jit(solution)/shard_map/ppermute | solution.py:483
  89.7 11.4 %collective-permute-start.11 = (f32[64,128]{1,0:T(8,128)}, f32[64,128]{1,0:T(8,128)}, u32[]{:S(2)}, u32[]{:S(2)}) collective-permute-start(f32[64,128]{1,0:T(8,128)} %get-tuple-element.59), channel_id=1, source_target_pairs={{1,0},{2,1},{3,2},{4,3},{5,4},{6,5},{7,6},{8,7},{9,8},{10,9},{11,1... | collective-permute-start | bytes 98312 | tf_op jit(solution)/shard_map/ppermute | solution.py:483
  95.5 21.4 %all-to-all-start.1 = ((f32[32,8,128]{2,1,0:T(8,128)}), f32[32,8,128]{2,1,0:T(8,128)}, u32[]{:S(2)}, u32[]{:S(2)}) async-start(f32[32,8,128]{2,1,0:T(8,128)} %broadcast_in_dim.11), calls=%async_computation.1 | async-start | bytes 262144 | tf_op jit(solution)/shard_map/all_to_all | solution.py:498
  101.1 0.9 copy-start.8
  102.0 1.0 copy-start.19
  105.5 0.8 copy-start.12
  106.3 0.8 copy-start.20
  107.1 11.1 %copy-start.9 = (f32[256,128]{1,0:T(8,128)S(1)}, f32[256,128]{1,0:T(8,128)}, u32[]{:S(2)}) copy-start(f32[256,128]{1,0:T(8,128)} %copy-done.5) | copy-start | bytes 393220
  107.1 11.1 %copy-start.4 = (f32[1,1,153,256]{3,2,1,0:T(8,128)S(1)}, f32[1,1,153,256]{3,2,1,0:T(8,128)}, u32[]{:S(2)}) copy-start(f32[1,1,153,256]{3,2,1,0:T(8,128)} %copy-done.2) | copy-start | bytes 470020
  107.2 4.5 %collective-permute-start.13 = (f32[64,128]{1,0:T(8,128)S(1)}, f32[64,128]{1,0:T(8,128)S(1)}, u32[]{:S(2)}, u32[]{:S(2)}) collective-permute-start(f32[64,128]{1,0:T(8,128)S(1)} %get-tuple-element.82), channel_id=1, source_target_pairs={{32,0},{64,32},{96,64},{128,96},{160,128},{192,160},{224,192},{0,2... | collective-permute-start | bytes 98312 | tf_op jit(solution)/shard_map/ppermute | solution.py:483
  110.8 1.2 collective-permute-start.12
  112.1 6.1 %collective-permute-start.14 = (f32[64,128]{1,0:T(8,128)S(1)}, f32[64,128]{1,0:T(8,128)S(1)}, u32[]{:S(2)}, u32[]{:S(2)}) collective-permute-start(f32[64,128]{1,0:T(8,128)S(1)} %get-tuple-element.63), channel_id=1, source_target_pairs={{0,1},{1,2},{2,3},{3,4},{4,5},{5,6},{6,7},{7,8},{8,9},{9,10},{10,1... | collective-permute-start | bytes 98312 | tf_op jit(solution)/shard_map/ppermute | solution.py:483
  113.4 4.8 %collective-permute-start.15 = (f32[64,128]{1,0:T(8,128)S(1)}, f32[64,128]{1,0:T(8,128)S(1)}, u32[]{:S(2)}, u32[]{:S(2)}) collective-permute-start(f32[64,128]{1,0:T(8,128)S(1)} %get-tuple-element.64), channel_id=1, source_target_pairs={{1,0},{2,1},{3,2},{4,3},{5,4},{6,5},{7,6},{8,7},{9,8},{10,9},{11,1... | collective-permute-start | bytes 98312 | tf_op jit(solution)/shard_map/ppermute | solution.py:483
  118.9 1.0 copy-start.11
  119.9 1.0 copy-start.13
  121.0 0.9 copy-start.15
  121.9 1.0 copy-start.21
  124.9 5.4 %collective-permute-start.17 = (f32[64,128]{1,0:T(8,128)S(1)}, f32[64,128]{1,0:T(8,128)S(1)}, u32[]{:S(2)}, u32[]{:S(2)}) collective-permute-start(f32[64,128]{1,0:T(8,128)S(1)} %get-tuple-element.80), channel_id=1, source_target_pairs={{32,0},{64,32},{96,64},{128,96},{160,128},{192,160},{224,192},{0,2... | collective-permute-start | bytes 98312 | tf_op jit(solution)/shard_map/ppermute | solution.py:483
  129.4 1.2 collective-permute-start.16
  130.7 6.4 %collective-permute-start.18 = (f32[64,128]{1,0:T(8,128)S(1)}, f32[64,128]{1,0:T(8,128)S(1)}, u32[]{:S(2)}, u32[]{:S(2)}) collective-permute-start(f32[64,128]{1,0:T(8,128)S(1)} %get-tuple-element.72), channel_id=1, source_target_pairs={{0,1},{1,2},{2,3},{3,4},{4,5},{5,6},{6,7},{7,8},{8,9},{9,10},{10,1... | collective-permute-start | bytes 98312 | tf_op jit(solution)/shard_map/ppermute | solution.py:483
  130.8 6.4 %collective-permute-start.19 = (f32[64,128]{1,0:T(8,128)S(1)}, f32[64,128]{1,0:T(8,128)S(1)}, u32[]{:S(2)}, u32[]{:S(2)}) collective-permute-start(f32[64,128]{1,0:T(8,128)S(1)} %get-tuple-element.73), channel_id=1, source_target_pairs={{1,0},{2,1},{3,2},{4,3},{5,4},{6,5},{7,6},{8,7},{9,8},{10,9},{11,1... | collective-permute-start | bytes 98312 | tf_op jit(solution)/shard_map/ppermute | solution.py:483
  161.8 0.7 copy-start.40
  (7 other events, 4.4 us)

commit v2 on v1

--- a/solution.py
+++ b/solution.py
@@ -163,54 +163,119 @@
     return jnp.where(end, 2.0 * share, share)
 
 
+def first_plane(x):
+    return jnp.where(lanes() < 64, roll_lanes(x, 64), 0.0)
+
+
+def last_plane(x):
+    return jnp.where(lanes() >= 64, roll_lanes(x, 64), 0.0)
+
+
+def first_row(x):
+    return jnp.where(lanes() // NP % NP == 0, roll_lanes(x, 72), 0.0)
+
+
+def last_row(x):
+    return jnp.where(lanes() // NP % NP == NP - 1, roll_lanes(x, 56), 0.0)
+
+
+def roll_lanes(x, shift):
+    return pltpu.roll(x.reshape(-1, 128), shift, 1).reshape(x.shape)
+
+
+def sum_levels(col):
+    rows = col.shape[0]
+    row_z = lanes() % NP
+    level = lax.broadcasted_iota(jnp.int32, (rows, 1), 0) % EZ
+    up = pltpu.roll(pltpu.roll(col, 121, 1), 1, 0)
+    down = pltpu.roll(pltpu.roll(col, 7, 1), rows - 1, 0)
+    return (
+        col
+        + jnp.where((row_z == 0) & (level > 0), up, 0.0)
+        + jnp.where((row_z == NP - 1) & (level < EZ - 1), down, 0.0)
+    )
+
+
+def blocks(col, length=EY):
+    return col.reshape(-1, length, EZ, 128)
+
+
 def assemble_inside(cols):
-    lane = lanes()
-    zero = jnp.zeros((64, 128), F32)
-    up = jnp.where(lane < 64, pltpu.roll(cols[3], 64, 1)[:192], 0.0)
-    down = jnp.where(lane >= 64, pltpu.roll(cols[0], 64, 1)[64:], 0.0)
+    cols = [blocks(col) for col in cols]
+    edge = jnp.zeros((1, EY, EZ, 128), F32)
     cols = [
-        cols[0] + jnp.concatenate([zero, up], 0),
+        cols[0] + jnp.concatenate([edge, first_plane(cols[3][: EX - 1])], 0),
         cols[1],
         cols[2],
-        cols[3] + jnp.concatenate([down, zero], 0),
+        cols[3] + jnp.concatenate([last_plane(cols[0][1:]), edge], 0),
     ]
-    row_y = lane // NP % NP
-    row_z = lane % NP
-    level = lax.broadcasted_iota(jnp.int32, (ROWS, 1), 0) % EZ
-    from_below = (row_z == 0) & (level > 0)
-    from_above = (row_z == NP - 1) & (level < EZ - 1)
     edge = jnp.zeros((EX, 1, EZ, 128), F32)
     result = []
     for col in cols:
-        up = jnp.where(row_y == 0, pltpu.roll(col, 72, 1), 0.0).reshape(EX, EY, EZ, 128)
-        down = jnp.where(row_y == NP - 1, pltpu.roll(col, 56, 1), 0.0).reshape(EX, EY, EZ, 128)
         col = (
             col
-            + jnp.concatenate([edge, up[:, : EY - 1]], 1).reshape(ROWS, 128)
-            + jnp.concatenate([down[:, 1:], edge], 1).reshape(ROWS, 128)
+            + jnp.concatenate([edge, first_row(col[:, : EY - 1])], 1)
+            + jnp.concatenate([last_row(col[:, 1:]), edge], 1)
         )
-        up = pltpu.roll(pltpu.roll(col, 121, 1), 1, 0)
-        down = pltpu.roll(pltpu.roll(col, 7, 1), ROWS - 1, 0)
-        result.append(col + jnp.where(from_below, up, 0.0) + jnp.where(from_above, down, 0.0))
+        result.append(sum_levels(col.reshape(ROWS, 128)))
     return result
 
 
-def write_faces(cols, part_ref, face_x_ref, face_y_ref):
+def joined_x(own, left, right):
+    own, left, right = list(own), list(left), list(right)
+    low, high = own[0], own[3]
+    tail = jnp.zeros_like(low[1:])
+    own[0] = low + jnp.concatenate([first_plane(left[3]), tail], 0)
+    own[3] = high + jnp.concatenate([tail, last_plane(right[0])], 0)
+    left[3] = left[3] + last_plane(low[:1])
+    right[0] = right[0] + first_plane(high[EX - 1 :])
+    return [jnp.concatenate(parts, 0) for parts in zip(left, own, right)]
+
+
+def joined_y(middle, below, above):
+    first, last = middle[:, :1], middle[:, EY - 1 :]
+    hole = jnp.zeros_like(middle[:, 1 : EY - 1])
+    middle = middle + jnp.concatenate([first_row(below), hole, last_row(above)], 1)
+    return jnp.concatenate([below + last_row(first), middle, above + first_row(last)], 1)
+
+
+def assemble_wide(cols):
+    cols = [
+        cols[0][1:-1] + first_plane(cols[3][:-2]),
+        cols[1][1:-1],
+        cols[2][1:-1],
+        cols[3][1:-1] + last_plane(cols[0][2:]),
+    ]
+    return [
+        sum_levels((col[:, 1:-1] + first_row(col[:, :-2]) + last_row(col[:, 2:])).reshape(ROWS, 128))
+        for col in cols
+    ]
+
+
+def write_faces(cols, part_ref, face_left_ref, face_right_ref, face_y_ref):
     row_y = lanes() // NP % NP
     for c in range(4):
         part_ref[:, 128 * c : 128 * c + 128] = cols[c]
-    face_x_ref[0] = cols[0][:64]
-    face_x_ref[1] = cols[3][192:]
+    face_left_ref[...] = cols[0][:64]
+    face_right_ref[...] = cols[3][192:]
     low = jnp.zeros((64, 128), F32)
     high = jnp.zeros((64, 128), F32)
     for c in range(4):
-        blocks = cols[c].reshape(EX, EY, EZ, 128)
-        first = jnp.where(row_y == 0, blocks[:, 0].reshape(64, 128), 0.0)
-        last = jnp.where(row_y == NP - 1, blocks[:, EY - 1].reshape(64, 128), 0.0)
+        split = cols[c].reshape(EX, EY, EZ, 128)
+        first = jnp.where(row_y == 0, split[:, 0].reshape(64, 128), 0.0)
+        last = jnp.where(row_y == NP - 1, split[:, EY - 1].reshape(64, 128), 0.0)
         low = low + (pltpu.roll(first, 8 * c, 1) if c else first)
         high = high + pltpu.roll(last, (72 + 8 * c) % 128, 1)
     face_y_ref[0] = low
     face_y_ref[1] = high
+
+
+def write_planes(cols, part_ref, left_ref, right_ref):
+    for c in range(4):
+        at = slice(128 * c, 128 * c + 128)
+        part_ref[:, at] = cols[c]
+        left_ref[:, at] = cols[c][:64]
+        right_ref[:, at] = cols[c][192:]
 
 
 def edge_kernel(face_y_ref, before_ref, after_ref, out_low_ref, out_high_ref):
@@ -254,7 +319,7 @@
     return pltpu.roll(ref[pl.ds(LEVELS * count - 24, 24), :], LEVELS, 0)
 
 
-def loads_of(unassembled, loads, leaf_ref, column_ref, top_ref, coeff_ref, leaf_out_ref):
+def loads_of(unassembled, loads, leaf_ref, column_ref, top_ref, coeff_ref, leaf_out_ref, numbers):
     corner = product(unassembled, loads)
     lane = lanes()
     pad = jnp.zeros((8, 128), F32)
@@ -282,11 +347,13 @@
                 column_sum = column_sum + factor_rows(column_ref, at, 25) * vertex
                 if 0 < vy < EY:
                     leaf_sum = leaf_sum + factor_rows(leaf_ref, (vx - 1) * 3 + vy - 1, 9) * vertex
-    coeff_ref[...] = jnp.zeros((8, 128), F32)
+    row = lax.broadcasted_iota(jnp.int32, (8, 1), 0)
+    coeffs = jnp.where(row == 2, numbers, 0.0)
     for at, total in ((0, top_sum), (4, column_sum)):
         total = jnp.sum(total, axis=0, keepdims=True)
-        coeff_ref[at : at + 1] = total[:, :128]
-        coeff_ref[at + 1 : at + 2] = total[:, 128:]
+        coeffs = jnp.where(row == at, total[:, :128], coeffs)
+        coeffs = jnp.where(row == at + 1, total[:, 128:], coeffs)
+    coeff_ref[...] = jnp.broadcast_to(coeffs[None], coeff_ref.shape)
     leaf_out_ref[...] = jnp.sum(leaf_sum, axis=0, keepdims=True)
 
 
@@ -318,38 +385,6 @@
     return product(jnp.concatenate(corners, 0), spread)
 
 
-def start_kernel(
-    order_ref, forcing_ref, diffusivity_ref, reaction_ref, leaf_ref, column_ref, top_ref, loads_ref,
-    part_ref, face_x_ref, face_y_ref, coeff_ref, leaf_out_ref, pair_ref,
-):
-    slot = lax.broadcasted_iota(jnp.int32, (ROWS, ROWS), 0)
-    chooser = (order_ref[...] == slot).astype(F32)
-    diffusion = jnp.sum(chooser * diffusivity_ref[...], axis=1, keepdims=True)
-    reacting = jnp.sum(chooser * reaction_ref[...], axis=1, keepdims=True)
-    lane = lanes()
-    pair_ref[...] = jnp.where(lane == 0, diffusion, reacting)
-    source = permuted(chooser.astype(BF16), forcing_ref[...])
-    write_faces(assemble_inside(columns(source)), part_ref, face_x_ref, face_y_ref)
-    loads_of(source, loads_ref[...], leaf_ref, column_ref, top_ref, coeff_ref, leaf_out_ref)
-
-
-def smooth_kernel(
-    part_ref, before_x_ref, after_x_ref, before_y_ref, after_y_ref, pair_ref, shape_ref, rows_ref,
-    field_ref, out_ref, face_x_ref, face_y_ref,
-):
-    field = finish(part_ref, before_x_ref, after_x_ref, before_y_ref, after_y_ref)
-    field_ref[...] = field
-    pair = pair_ref[...]
-    scale = 1.0 / (pair[:, 0:1] * rows_ref[0:1] + pair[:, 1:2])
-    table = shape_ref[...]
-    smoothed = product(product(field, table) * scale, table, 1)
-    write_faces(assemble_inside(columns(smoothed)), out_ref, face_x_ref, face_y_ref)
-
-
-def stiffness_of(field, pair, stiff_ref, rows_ref):
-    return product(field, stiff_ref[...]) * pair[:, 0:1] + field * (rows_ref[1:2] * pair[:, 1:2])
-
-
 def total_of(x):
     return jnp.sum(jnp.sum(x, axis=0, keepdims=True), axis=1, keepdims=True)
 
@@ -362,66 +397,162 @@
     return row
 
 
+def start_kernel(
+    order, forcing, diffusivity, reaction, loads, leaf, column, top,
+    part_ref, left_ref, right_ref, coeff_ref, leaf_out_ref, pair_ref,
+):
+    slot = lax.broadcasted_iota(jnp.int32, (ROWS, ROWS), 0)
+    chooser = (order()[...] == slot).astype(F32)
+    diffusion = jnp.sum(chooser * diffusivity()[...], axis=1, keepdims=True)
+    reacting = jnp.sum(chooser * reaction()[...], axis=1, keepdims=True)
+    pair = jnp.where(lanes() == 0, diffusion, reacting)
+    pair_ref[...] = pair
+    left_ref[:, NODES:] = pair[:64]
+    right_ref[:, NODES:] = pair[192:]
+    source = permuted(chooser.astype(BF16), forcing()[...])
+    write_planes(assemble_inside(columns(source)), part_ref, left_ref, right_ref)
+    loads_of(
+        source, loads()[...], leaf(), column(), top(), coeff_ref, leaf_out_ref, numbers_row([])
+    )
+
+
+def rows_of_plane(ref, c, plane):
+    return blocks(ref[:, 128 * c : 128 * c + 128])[:, plane : plane + 1]
+
+
+def middle_kernel(part_ref, left_ref, right_ref, own_ref, gathered_ref, *refs):
+    with_pair = len(refs) == 4
+    low_ref, high_ref, spread_ref = refs[-3:]
+    row = lax.broadcasted_iota(jnp.int32, (8, 1), 0)
+    coeffs = jnp.where(row < 4, jnp.sum(gathered_ref[...], axis=0), own_ref[0])
+    spread_ref[...] = jnp.broadcast_to(coeffs[None], spread_ref.shape)
+    for plane, out_ref in ((0, low_ref), (EY - 1, high_ref)):
+        sides = [
+            [rows_of_plane(ref, c, plane) for c in range(4)] for ref in (part_ref, left_ref, right_ref)
+        ]
+        for c, col in enumerate(joined_x(*sides)):
+            out_ref[:, 128 * c : 128 * c + 128] = col.reshape(-1, 128)
+        if with_pair:
+            sides = [rows_of_plane(left_ref, 4, plane), rows_of_plane(refs[0], 0, plane)]
+            sides.append(rows_of_plane(right_ref, 4, plane))
+            out_ref[:, NODES:] = jnp.concatenate(sides, 0).reshape(-1, 128)
+
+
+def wide_field(part_ref, left_ref, right_ref, below_ref, above_ref):
+    sides = [
+        [blocks(ref[:, 128 * c : 128 * c + 128]) for c in range(4)]
+        for ref in (part_ref, left_ref, right_ref)
+    ]
+    result = []
+    for c, middle in enumerate(joined_x(*sides)):
+        at = slice(128 * c, 128 * c + 128)
+        result.append(joined_y(middle, blocks(below_ref[:, at], 1), blocks(above_ref[:, at], 1)))
+    return result
+
+
+def inner_rows(cols):
+    return jnp.concatenate([col[1:-1, 1:-1].reshape(ROWS, 128) for col in cols], 1)
+
+
+def smoothed_of(cols, pair, shape, rows):
+    wide = jnp.concatenate([col.reshape(-1, 128) for col in cols], 1)
+    scale = 1.0 / (pair[:, 0:1] * rows[0:1] + pair[:, 1:2])
+    table = shape()[...]
+    modes = product(wide, table) * scale
+    back = product(modes, table, 1)
+    return assemble_wide([blocks(col, EY + 2) for col in columns(back)])
+
+
+def stiffness_of(field, pair, stiff, rows):
+    return product(field, stiff()[...]) * pair[:, 0:1] + field * (rows[1:2] * pair[:, 1:2])
+
+
 def first_kernel(
-    part_ref, before_x_ref, after_x_ref, before_y_ref, after_y_ref, pair_ref, stiff_ref, rows_ref,
-    loads_ref, spread_ref, leaf_ref, column_ref, top_ref, coeff_in_ref, leaf_in_ref, source_ref,
-    search_ref, out_ref, face_x_ref, face_y_ref, coeff_ref, leaf_out_ref,
+    part_ref, left_ref, right_ref, below_ref, above_ref, pair_ref, gathered_ref, leaf_in_ref,
+    rows, shape, spread, leaf, column, top, stiff, loads,
+    source_out, search_out, wide_pair_out, out_ref, left_out_ref, right_out_ref, coeff_ref,
+    leaf_out_ref,
 ):
-    weight = weight_of(rows_ref[2:3])
-    smoothed = finish(part_ref, before_x_ref, after_x_ref, before_y_ref, after_y_ref)
-    search = smoothed * weight + coarse_of(
-        coeff_in_ref[...], leaf_in_ref[...], spread_ref[...], leaf_ref, column_ref, top_ref
-    )
-    search_ref[...] = search
-    image = stiffness_of(search, pair_ref[...], stiff_ref, rows_ref)
-    write_faces(assemble_inside(columns(image)), out_ref, face_x_ref, face_y_ref)
-    loads_of(image, loads_ref[...], leaf_ref, column_ref, top_ref, coeff_ref, leaf_out_ref)
-    source = source_ref[...]
-    coeff_ref[2:3] = numbers_row(
+    rows = rows()[...]
+    weight = weight_of(rows[2:3])
+    field = wide_field(part_ref, left_ref, right_ref, below_ref, above_ref)
+    source = inner_rows(field)
+    source_out.ref[...] = source
+    source_out.send()
+    own = pair_ref[...]
+    at = slice(NODES, NODES + 128)
+    wide_pair = jnp.concatenate([blocks(left_ref[:, at]), blocks(own), blocks(right_ref[:, at])], 0)
+    wide_pair = jnp.concatenate(
+        [blocks(below_ref[:, at], 1), wide_pair, blocks(above_ref[:, at], 1)], 1
+    ).reshape(-1, 128)
+    wide_pair_out.ref[...] = wide_pair
+    wide_pair_out.send()
+    coeffs = jnp.sum(gathered_ref[...], axis=0)
+    smoothed = smoothed_of(field, wide_pair, shape, rows)
+    search = jnp.concatenate(smoothed, 1) * weight + coarse_of(
+        coeffs, leaf_in_ref[...], spread()[...], leaf(), column(), top()
+    )
+    search_out.ref[...] = search
+    search_out.send()
+    image = stiffness_of(search, own, stiff, rows)
+    write_planes(assemble_inside(columns(image)), out_ref, left_out_ref, right_out_ref)
+    numbers = numbers_row(
         [total_of(source * source * weight), total_of(image * source), total_of(image * image)]
     )
+    loads_of(image, loads()[...], leaf(), column(), top(), coeff_ref, leaf_out_ref, numbers)
 
 
 def second_kernel(
-    part_ref, before_x_ref, after_x_ref, before_y_ref, after_y_ref, pair_ref, stiff_ref, rows_ref,
-    spread_ref, leaf_ref, column_ref, top_ref, coeff_in_ref, leaf_in_ref, source_ref, search_ref,
-    image_ref,
-    second_ref, out_ref, face_x_ref, face_y_ref, sums_ref,
+    part_ref, left_ref, right_ref, below_ref, above_ref, pair_ref, gathered_ref, leaf_in_ref,
+    rows, wide_pair, shape, spread, leaf, column, top, search, source, stiff,
+    image_out, second_out, out_ref, face_left_ref, face_right_ref, face_y_ref, sums_ref, total_ref,
 ):
-    weight = weight_of(rows_ref[2:3])
-    coeffs = coeff_in_ref[...]
+    rows = rows()[...]
+    weight = weight_of(rows[2:3])
+    coeffs = jnp.sum(gathered_ref[...], axis=0)
+    total_ref[...] = coeffs
     norm, along, size = coeffs[2:3, 0:1], coeffs[2:3, 1:2], coeffs[2:3, 2:3]
     overlap = along / norm
     scale = 1.0 / jnp.sqrt(size)
-    smoothed = finish(part_ref, before_x_ref, after_x_ref, before_y_ref, after_y_ref)
-    whole = smoothed * weight + coarse_of(
-        coeffs, leaf_in_ref[...], spread_ref[...], leaf_ref, column_ref, top_ref
-    )
-    second = (whole - overlap * search_ref[...]) * scale
-    second_ref[...] = second
-    source = source_ref[...]
-    basis = (image_ref[...] - overlap * source) * scale
-    image = stiffness_of(second, pair_ref[...], stiff_ref, rows_ref)
-    write_faces(assemble_inside(columns(image)), out_ref, face_x_ref, face_y_ref)
+    field = wide_field(part_ref, left_ref, right_ref, below_ref, above_ref)
+    first = inner_rows(field)
+    image_out.ref[...] = first
+    image_out.send()
+    smoothed = smoothed_of(field, wide_pair()[...], shape, rows)
+    whole = jnp.concatenate(smoothed, 1) * weight + coarse_of(
+        coeffs, leaf_in_ref[...], spread()[...], leaf(), column(), top()
+    )
+    second = (whole - overlap * search()[...]) * scale
+    second_out.ref[...] = second
+    second_out.send()
+    source = source()[...]
+    image = stiffness_of(second, pair_ref[...], stiff, rows)
+    write_faces(assemble_inside(columns(image)), out_ref, face_left_ref, face_right_ref, face_y_ref)
+    basis = (first - overlap * source) * scale
     sums_ref[...] = numbers_row(
         [total_of(basis * basis * weight), total_of(image * source), total_of(image * basis)]
     )
 
 
+def chooser_back(order_ref):
+    slot = lax.broadcasted_iota(jnp.int32, (ROWS, ROWS), 0)
+    return (order_ref[...] == slot).astype(F32).T.astype(BF16)
+
+
 def last_kernel(
-    part_ref, before_x_ref, after_x_ref, before_y_ref, after_y_ref, rows_ref, sums_in_ref,
+    part_ref, before_x_ref, after_x_ref, before_y_ref, after_y_ref, sums_in_ref, rows,
     image_ref, sums_ref,
 ):
     image = finish(part_ref, before_x_ref, after_x_ref, before_y_ref, after_y_ref)
     image_ref[...] = image
-    square = total_of(image * image * weight_of(rows_ref[2:3]))
-    sums_ref[...] = jnp.where(lanes() == 3, square, sums_in_ref[...])
+    square = total_of(image * image * weight_of(rows()[2:3]))
+    sums = jnp.where(lanes() == 3, square, sums_in_ref[...])
+    sums_ref[...] = jnp.broadcast_to(sums, sums_ref.shape)
 
 
 def end_kernel(
-    order_ref, sums_ref, coeff_ref, source_ref, search_one_ref, image_one_ref, search_two_ref,
-    image_two_ref,
-    pressure_ref, residual_ref,
+    sums_ref, coeff_ref, image_two_ref, order, search_one, search_two, source, image_one,
+    pressure_out, residual_out,
 ):
     sums = jnp.sum(sums_ref[...], axis=0, keepdims=True)
     squared, dot_source, dot_basis, dot_self = (sums[:, at : at + 1] for at in range(4))
@@ -446,34 +577,93 @@
     factor_one = (cosine * beta - rotated * factor_two) / first_norm
     step_one = factor_one / beta
     step_two = factor_two / basis_norm
-    slot = lax.broadcasted_iota(jnp.int32, (ROWS, ROWS), 0)
-    chooser = (order_ref[...] == slot).astype(F32).T.astype(BF16)
-    pressure_ref[...] = permuted(
-        chooser, step_one * search_one_ref[...] + step_two * search_two_ref[...]
-    )
-    residual_ref[...] = permuted(
-        chooser, source_ref[...] - step_one * image_one_ref[...] - step_two * image_two_ref[...]
-    )
-
-
-FIELD = jax.ShapeDtypeStruct((ROWS, NODES), F32)
-FACES = jax.ShapeDtypeStruct((2, 64, 128), F32)
-FACE = jax.ShapeDtypeStruct((64, 128), F32)
-COEFFS = jax.ShapeDtypeStruct((8, 128), F32)
-LEAVES = jax.ShapeDtypeStruct((1, 256), F32)
-NUMBERS = jax.ShapeDtypeStruct((1, 128), F32)
-PAIRS = jax.ShapeDtypeStruct((ROWS, 128), F32)
+    chooser = chooser_back(order())
+    pressure_out.ref[...] = permuted(
+        chooser, step_one * search_one()[...] + step_two * search_two()[...]
+    )
+    pressure_out.send()
+    residual_out.ref[...] = permuted(
+        chooser, source()[...] - step_one * image_one()[...] - step_two * image_two_ref[...]
+    )
+    residual_out.send()
+
+
+class Far:
+    def __init__(self, value):
+        self.value = value
+
+
+class Fetch:
+    def __init__(self, source, target, sem):
+        self.copy, self.target, self.waiting = pltpu.make_async_copy(source, target, sem), target, True
+        self.copy.start()
+
+    def __call__(self):
+        if self.waiting:
+            self.copy.wait()
+            self.waiting = False
+        return self.target
+
+
+class Store:
+    def __init__(self, ref, target, sem):
+        self.ref, self.copy = ref, pltpu.make_async_copy(ref, target, sem)
+
+    def send(self):
+        self.copy.start()
+
+
+def shaped(*shape):
+    return jax.ShapeDtypeStruct(shape, F32)
 
 
 def run(kernel, outs, *args):
-    vmem = pl.BlockSpec(memory_space=pltpu.VMEM)
+    vmem, far = pl.BlockSpec(memory_space=pltpu.VMEM), pl.BlockSpec(memory_space=pl.ANY)
+    far_in = [isinstance(arg, Far) for arg in args]
+    far_out = [isinstance(out, Far) for out in outs]
+    args = [arg.value if isinstance(arg, Far) else arg for arg in args]
+    outs = [out.value if isinstance(out, Far) else out for out in outs]
+    moved = [arg for arg, out_of in zip(args, far_in) if out_of]
+    moved += [out for out, out_of in zip(outs, far_out) if out_of]
+    count = len(moved)
+
+    def body(*refs):
+        ins, rest = refs[: len(args)], refs[len(args) :]
+        results, scratch = rest[: len(outs)], rest[len(outs) :]
+        at, given, stores = 0, [], []
+        for ref, is_far in zip(ins, far_in):
+            if is_far:
+                ref = Fetch(ref, scratch[at], scratch[count].at[at])
+                at += 1
+            given.append(ref)
+        for ref, is_far in zip(results, far_out):
+            if is_far:
+                ref = Store(scratch[at], ref, scratch[count].at[at])
+                stores.append(ref)
+                at += 1
+            given.append(ref)
+        kernel(*given)
+        for store in stores:
+            store.copy.wait()
+
+    scratch = [pltpu.VMEM(item.shape, item.dtype) for item in moved]
+    if count:
+        scratch.append(pltpu.SemaphoreType.DMA((count,)))
     return pl.pallas_call(
-        kernel,
-        out_shape=outs,
-        in_specs=[vmem] * len(args),
-        out_specs=tuple(vmem for _ in outs),
-        compiler_params=pltpu.CompilerParams(vmem_limit_bytes=24 * 2**20),
+        body,
+        out_shape=tuple(outs),
+        in_specs=[far if is_far else vmem for is_far in far_in],
+        out_specs=tuple(far if is_far else vmem for is_far in far_out),
+        scratch_shapes=scratch,
+        compiler_params=pltpu.CompilerParams(vmem_limit_bytes=LIMIT),
     )(*args)
+
+
+LIMIT = 28 * 2**20
+FIELD = shaped(ROWS, NODES)
+FACES = shaped(2, 64, 128)
+FACE = shaped(64, 128)
+PAIRS = shaped(ROWS, 128)
 
 
 def neighbours(low, high, axis):
@@ -483,60 +673,60 @@
     return lax.ppermute(high, axis, up), lax.ppermute(low, axis, down)
 
 
-def exchanged(face_x, face_y):
-    before_x, after_x = neighbours(face_x[0], face_x[1], "gx")
-    low, high = run(edge_kernel, (FACE, FACE), face_y, before_x, after_x)
-    before_y, after_y = neighbours(low, high, "gy")
-    return before_x, after_x, before_y, after_y
-
-
-def summed(coeffs):
-    shared = lax.psum(coeffs[:4], "gx")
-    mine = jnp.concatenate([shared, coeffs[4:]], 0)
-    peers = lax.axis_size("gy")
-    spread = jnp.broadcast_to(mine[None], (peers, 8, 128))
-    return jnp.sum(lax.all_to_all(spread, "gy", 0, 0), 0)
+def surrounded(part, left, right, coeffs, pair=None):
+    wide, across = left.shape[1], (EX + 2) * EZ
+    before, after = neighbours(left, right, "gx")
+    gathered = lax.all_to_all(coeffs, "gx", 0, 0)
+    more = () if pair is None else (pair,)
+    low, high, spread = run(
+        middle_kernel,
+        (shaped(across, wide), shaped(across, wide), shaped(lax.axis_size("gy"), 8, 128)),
+        part, before, after, coeffs, gathered, *more,
+    )
+    below, above = neighbours(low, high, "gy")
+    return part, before, after, below, above, lax.all_to_all(spread, "gy", 0, 0)
 
 
 def per_device(
     forcing, element_order, diffusivity, reaction, leaf_factor, column_factor, top_factor
 ):
-    stiff, shape, loads, spread, rows = build_tables()
-    factors = (leaf_factor[0, 0], column_factor[0, 0], top_factor[0, 0])
-    order = element_order[0]
-    part, face_x, face_y, coeffs, leaves, pair = run(
+    stiff, shape, loads, spread, rows = (Far(table) for table in build_tables())
+    factors = tuple(Far(factor[0, 0]) for factor in (leaf_factor, column_factor, top_factor))
+    order = Far(element_order[0])
+    coarse = (shaped(lax.axis_size("gx"), 8, 128), shaped(1, 256))
+    part, left, right, coeffs, leaves, pair = run(
         start_kernel,
-        (FIELD, FACES, FACES, COEFFS, LEAVES, PAIRS),
-        order, forcing[0, 0], diffusivity[0], reaction[0], *factors, loads,
-    )
-    coeffs = summed(coeffs)
-    source, part, face_x, face_y = run(
-        smooth_kernel, (FIELD, FIELD, FACES, FACES), part, *exchanged(face_x, face_y), pair, shape, rows
-    )
-    search_one, part, face_x, face_y, coeffs, leaves = run(
+        (FIELD, shaped(64, NODES + 128), shaped(64, NODES + 128), *coarse, PAIRS),
+        order, Far(forcing[0, 0]), Far(diffusivity[0]), Far(reaction[0]), loads, *factors,
+    )
+    *around, gathered = surrounded(part, left, right, coeffs, pair)
+    source, search_one, wide_pair, part, left, right, coeffs, leaves = run(
         first_kernel,
-        (FIELD, FIELD, FACES, FACES, COEFFS, LEAVES),
-        part, *exchanged(face_x, face_y), pair, stiff, rows, loads, spread, *factors, coeffs, leaves,
-        source,
-    )
-    coeffs = summed(coeffs)
-    image_one, part, face_x, face_y = run(
-        smooth_kernel, (FIELD, FIELD, FACES, FACES), part, *exchanged(face_x, face_y), pair, shape, rows
-    )
-    search_two, part, face_x, face_y, sums = run(
+        (
+            Far(FIELD), Far(FIELD), Far(shaped((EX + 2) * (EY + 2) * EZ, 128)),
+            FIELD, shaped(64, NODES), shaped(64, NODES), *coarse,
+        ),
+        *around, pair, gathered, leaves, rows, shape, spread, *factors, stiff, loads,
+    )
+    *around, gathered = surrounded(part, left, right, coeffs)
+    image_one, search_two, part, face_left, face_right, face_y, sums, coeffs = run(
         second_kernel,
-        (FIELD, FIELD, FACES, FACES, NUMBERS),
-        part, *exchanged(face_x, face_y), pair, stiff, rows, spread, *factors, coeffs, leaves, source,
-        search_one, image_one,
-    )
+        (Far(FIELD), Far(FIELD), FIELD, FACE, FACE, FACES, shaped(1, 128), shaped(8, 128)),
+        *around, pair, gathered, leaves, rows, Far(wide_pair), shape, spread, *factors,
+        Far(search_one), Far(source), stiff,
+    )
+    before_x, after_x = neighbours(face_left, face_right, "gx")
+    low, high = run(edge_kernel, (FACE, FACE), face_y, before_x, after_x)
+    before_y, after_y = neighbours(low, high, "gy")
+    peers = lax.axis_size(("gx", "gy"))
     image_two, sums = run(
-        last_kernel, (FIELD, NUMBERS), part, *exchanged(face_x, face_y), rows, sums
-    )
-    peers = lax.axis_size(("gx", "gy"))
-    sums = lax.all_to_all(jnp.broadcast_to(sums, (peers, 128)), ("gx", "gy"), 0, 0, tiled=True)
+        last_kernel, (FIELD, shaped(peers, 128)),
+        part, before_x, after_x, before_y, after_y, sums, rows,
+    )
+    sums = lax.all_to_all(sums, ("gx", "gy"), 0, 0, tiled=True)
     pressure, residual = run(
-        end_kernel, (FIELD, FIELD),
-        order, sums, coeffs, source, search_one, image_one, search_two, image_two,
+        end_kernel, (Far(FIELD), Far(FIELD)),
+        sums, coeffs, image_two, order, Far(search_one), Far(search_two), Far(source), Far(image_one),
     )
     return (pressure[None, None], residual[None, None])
 

time: 166 us -> 152 us (0.916)
  starting transfers between devices: 59.9 us -> 36.8 us
  waiting for transfers between devices: 5.29 us -> 19.7 us
  blocking collectives: 49.6 us -> 42.8 us
  Pallas kernels: 15 us -> 21.3 us
  other arithmetic: 2.49 us -> 0 us
    ppermute x20 -> x12, starting transfers between devices: 48.3 us -> 21.3 us  [neighbours(): return (lax.ppermute(high, axis, up), lax.ppermute(low, axis, down))]
    psum x2 -> x0, blocking collectives: 25.2 us -> none  [summed(): shared = lax.psum(coeffs[:4], 'gx')]
    all_to_all x1 -> x3, blocking collectives: 24.4 us -> 42.8 us  [the longest x1 22.9 us: per_device(): sums = lax.all_to_all(sums, ('gx', 'gy'), 0, 0, tiled=True)]
    ppermute x20 -> x12, waiting for transfers between devices: 5.29 us -> 19.7 us  [neighbours(): return (lax.ppermute(high, axis, up), lax.ppermute(low, axis, down))]
    pallas_call x12 -> x8, Pallas kernels: 15 us -> 21.3 us  [run(): pl.pallas_call(body, out_shape=tuple(outs), in_specs=[far if is_far else...]
    all_to_all x2, starting transfers between devices: 11.6 us -> 15.5 us  [surrounded(): lax.all_to_all(spread, 'gy', 0, 0)]
    reduce_sum x2 -> x0, other arithmetic: 2.47 us -> none  [summed(): return jnp.sum(lax.all_to_all(spread, 'gy', 0, 0), 0)]
  transfers between devices with their start and end apart: 22 -> 14, of which waited for: 9 -> 5; matrix products, arithmetic and copies ran while one was open for 3% -> 0% of each run, Pallas kernels for 3% -> 0%
where the time goes in v2:
time: 152 us; the launch traced here: 151 us
  blocking collectives  42.8 us (28%)
  starting transfers between devices  36.8 us (24%)
  local copies, waits for them, and re-layouts  29.8 us (20%)
  Pallas kernels  21.3 us (14%)
  waiting for transfers between devices  19.7 us (13%)
    unnamed x100, local copies, waits for them, and re-layouts  29.8 us
    all_to_all x1, blocking collectives, per_device(): sums = lax.all_to_all(sums, ('gx', 'gy'), 0, 0, tiled=True)  22.9 us
    pallas_call x8, Pallas kernels, run(): pl.pallas_call(body, out_shape=tuple(outs), in_specs=[far if is_far else...  21.3 us
    ppermute x12, starting transfers between devices, neighbours(): return (lax.ppermute(high, axis, up), lax.ppermute(low, axis, down))  21.3 us
    all_to_all x2, blocking collectives, surrounded(): gathered = lax.all_to_all(coeffs, 'gx', 0, 0)  19.9 us
    ppermute x12, waiting for transfers between devices, neighbours(): return (lax.ppermute(high, axis, up), lax.ppermute(low, axis, down))  19.7 us
    all_to_all x2, starting transfers between devices, surrounded(): lax.all_to_all(spread, 'gy', 0, 0)  15.5 us
  transfers between devices with their start and end apart: 14, of which 5 were waited for; matrix products, arithmetic and copies ran while one was open for 0% of the time, Pallas kernels for 0%

profile of v2, /device:TPU:1, one launch (start us, length us, event | category | flops | bytes accessed | tf_op | source)
XLA Modules:
  0.0 151.4 jit_solution(14875394988790386427)
XLA Ops:
  0.6 0.9 copy.21
  1.6 1.3 copy_bitcast_fusion
  3.0 0.6 copy-done.37
  3.6 2.7 %shard_map.131 = (f32[256,512]{1,0:T(8,128)S(1)}, f32[64,640]{1,0:T(8,128)S(1)}, f32[64,640]{1,0:T(8,128)S(1)}, f32[8,8,128]{2,1,0:T(8,128)S(1)}, f32[1,256]{1,0:T(1,128)S(1)}, /*index=5*/f32[256,128]{1,0:T(8,128)S(1)}) custom-call(s32[1,256]{1,0:T(1,128)S(1)} %bitcast.23, f32[256,512]{1,0:T(8,128)S(1)} %bitcast.21, f32[1,256]{1,0:T(1,128)S(1)} %bitcast.25, ...), custom_call_target="tpu_custom_call" | custom-call | tf_op jit(solution)/shard_map/pallas_call | solution.py:652
  6.3 0.6 copy-done.43
  6.9 2.6 %collective-permute-start = (f32[64,640]{1,0:T(8,128)S(1)}, f32[64,640]{1,0:T(8,128)S(1)}, u32[]{:S(2)}, u32[]{:S(2)}) collective-permute-start(f32[64,640]{1,0:T(8,128)S(1)} %get-tuple-element.37), channel_id=1, source_target_pairs={{0,32},{32,64},{64,96},{96,128},{128,160},{160,192},{192,224},{224... | collective-permute-start | bytes 491528 | tf_op jit(solution)/shard_map/ppermute | solution.py:673
  9.5 0.6 collective-permute-start.1
  10.1 10.0 %all_to_all.31.refs_4_ = f32[8,8,128]{2,1,0:T(8,128)S(1)} all-to-all(f32[8,8,128]{2,1,0:T(8,128)S(1)} %get-tuple-element.39.refs_3_), channel_id=1, replica_groups=mesh['gx'=8,'gy'=32] {'gx'}, dimensions={0} | all-to-all | bytes 65536 | tf_op jit(solution)/shard_map/all_to_all | solution.py:679
  20.2 0.1 shard_map.132
  20.3 0.5 copy-done.15
  20.9 0.7 copy-done.35
  21.6 0.7 copy-done.45
  22.3 0.7 copy-done.46
  23.0 10.2 %all-to-all-start.1 = ((f32[32,8,128]{2,1,0:T(8,128)}), f32[32,8,128]{2,1,0:T(8,128)}, u32[]{:S(2)}, u32[]{:S(2)}) async-start(f32[32,8,128]{2,1,0:T(8,128)} %copy-done.35), calls=%async_computation.1 | async-start | bytes 262144 | tf_op jit(solution)/shard_map/all_to_all | solution.py:687
  33.2 1.2 collective-permute-start.2
  34.5 3.6 %collective-permute-start.3 = (f32[96,640]{1,0:T(8,128)}, f32[96,640]{1,0:T(8,128)S(1)}, u32[]{:S(2)}, u32[]{:S(2)}) collective-permute-start(f32[96,640]{1,0:T(8,128)} %copy-done.45), channel_id=1, source_target_pairs={{1,0},{2,1},{3,2},{4,3},{5,4},{6,5},{7,6},{8,7},{9,8},{10,9},{11,1... | collective-permute-start | bytes 737288 | tf_op jit(solution)/shard_map/ppermute | solution.py:673
  38.1 7.9 %collective-permute-done.2.refs_3_ = f32[96,640]{1,0:T(8,128)S(1)} collective-permute-done((f32[96,640]{1,0:T(8,128)}, f32[96,640]{1,0:T(8,128)S(1)}, u32[]{:S(2)}, u32[]{:S(2)}) %collective-permute-start.2) | collective-permute-done | bytes 245792 | tf_op jit(solution)/shard_map/ppermute | solution.py:673
  46.0 0.7 copy-done.26
  46.7 0.7 copy-done.28
  47.5 0.6 copy-done.44
  48.1 1.0 copy-done.9
  49.1 0.9 copy-done.14
  50.1 0.9 copy-done.16
  51.0 0.9 copy-done.18
  51.9 0.9 copy-done.27
  52.9 0.9 copy-done.29
  53.8 7.7 %shard_map.133 = (f32[256,512]{1,0:T(8,128)S(1)}, f32[256,512]{1,0:T(8,128)S(1)}, f32[576,128]{1,0:T(8,128)S(1)}, f32[256,512]{1,0:T(8,128)S(1)}, f32[64,512]{1,...) custom-call(f32[256,512]{1,0:T(8,128)S(1)} %copy-done.9, ...), custom_call_target="tpu_custom_call" | custom-call | tf_op jit(solution)/shard_map/pallas_call | solution.py:652
  61.6 0.8 copy-done.2
  62.4 0.8 copy-done.5
  63.2 0.5 copy-done.41
  63.7 1.7 %collective-permute-start.4 = (f32[64,512]{1,0:T(8,128)S(1)}, f32[64,512]{1,0:T(8,128)S(1)}, u32[]{:S(2)}, u32[]{:S(2)}) collective-permute-start(f32[64,512]{1,0:T(8,128)S(1)} %get-tuple-element.46), channel_id=1, source_target_pairs={{0,32},{32,64},{64,96},{96,128},{128,160},{160,192},{192,224},{224... | collective-permute-start | bytes 393224 | tf_op jit(solution)/shard_map/ppermute | solution.py:673
  65.4 9.8 %all_to_all.32.refs_4_ = f32[8,8,128]{2,1,0:T(8,128)S(1)} all-to-all(f32[8,8,128]{2,1,0:T(8,128)S(1)} %get-tuple-element.48.refs_3_), channel_id=1, replica_groups=mesh['gx'=8,'gy'=32] {'gx'}, dimensions={0} | all-to-all | bytes 65536 | tf_op jit(solution)/shard_map/all_to_all | solution.py:679
  75.3 0.1 shard_map.134
  75.4 0.5 copy-done.19
  76.0 0.8 copy-done.10
  76.7 0.7 copy-done.36
  77.4 0.7 copy-done.47
  78.1 0.7 copy-done.48
  78.8 5.3 %all-to-all-start.3 = ((f32[32,8,128]{2,1,0:T(8,128)}), f32[32,8,128]{2,1,0:T(8,128)}, u32[]{:S(2)}, u32[]{:S(2)}) async-start(f32[32,8,128]{2,1,0:T(8,128)} %copy-done.36), calls=%async_computation.3 | async-start | bytes 262144 | tf_op jit(solution)/shard_map/all_to_all | solution.py:687
  84.0 1.2 collective-permute-start.6
  85.3 3.7 %collective-permute-start.7 = (f32[96,512]{1,0:T(8,128)}, f32[96,512]{1,0:T(8,128)S(1)}, u32[]{:S(2)}, u32[]{:S(2)}) collective-permute-start(f32[96,512]{1,0:T(8,128)} %copy-done.47), channel_id=1, source_target_pairs={{1,0},{2,1},{3,2},{4,3},{5,4},{6,5},{7,6},{8,7},{9,8},{10,9},{11,1... | collective-permute-start | bytes 589832 | tf_op jit(solution)/shard_map/ppermute | solution.py:673
  88.9 6.8 %collective-permute-done.6.refs_3_ = f32[96,512]{1,0:T(8,128)S(1)} collective-permute-done((f32[96,512]{1,0:T(8,128)}, f32[96,512]{1,0:T(8,128)S(1)}, u32[]{:S(2)}, u32[]{:S(2)}) %collective-permute-start.6) | collective-permute-done | bytes 196640 | tf_op jit(solution)/shard_map/ppermute | solution.py:673
  95.7 0.7 copy-done.30
  96.4 0.7 copy-done.32
  97.1 0.6 copy-done.42
  97.7 1.0 copy-done.3
  98.8 1.0 copy-done.6
  99.8 1.0 copy-done.11
  100.8 0.9 copy-done.20
  101.7 0.9 copy-done.22
  102.6 1.0 copy-done.25
  103.6 0.9 copy-done.31
  104.5 0.9 copy-done.33
  105.5 7.5 %shard_map.135 = (f32[256,512]{1,0:T(8,128)S(1)}, f32[256,512]{1,0:T(8,128)S(1)}, f32[256,512]{1,0:T(8,128)S(1)}, f32[64,128]{1,0:T(8,128)S(1)}, f32[64,128]{1,0...) custom-call(f32[256,512]{1,0:T(8,128)S(1)} %copy-done.11, ...), custom_call_target="tpu_custom_call" | custom-call | tf_op jit(solution)/shard_map/pallas_call | solution.py:652
  113.0 1.8 %collective-permute-start.8 = (f32[64,128]{1,0:T(8,128)S(1)}, f32[64,128]{1,0:T(8,128)S(1)}, u32[]{:S(2)}, u32[]{:S(2)}) collective-permute-start(f32[64,128]{1,0:T(8,128)S(1)} %get-tuple-element.57), channel_id=1, source_target_pairs={{0,32},{32,64},{64,96},{96,128},{128,160},{160,192},{192,224},{224... | collective-permute-start | bytes 98312 | tf_op jit(solution)/shard_map/ppermute | solution.py:673
  114.7 1.0 collective-permute-done.8.refs_1_
  115.8 2.6 %collective-permute-done.9.refs_2_ = f32[64,128]{1,0:T(8,128)S(1)} collective-permute-done((f32[64,128]{1,0:T(8,128)S(1)}, f32[64,128]{1,0:T(8,128)S(1)}, u32[]{:S(2)}, u32[]{:S(2)}) %collective-permute-start.9) | collective-permute-done | bytes 32800 | tf_op jit(solution)/shard_map/ppermute | solution.py:673
  118.4 0.1 shard_map.136
  118.5 4.8 %collective-permute-start.11 = (f32[64,128]{1,0:T(8,128)S(1)}, f32[64,128]{1,0:T(8,128)S(1)}, u32[]{:S(2)}, u32[]{:S(2)}) collective-permute-start(f32[64,128]{1,0:T(8,128)S(1)} %get-tuple-element.61), channel_id=1, source_target_pairs={{1,0},{2,1},{3,2},{4,3},{5,4},{6,5},{7,6},{8,7},{9,8},{10,9},{11,1... | collective-permute-start | bytes 98312 | tf_op jit(solution)/shard_map/ppermute | solution.py:673
  123.3 1.3 collective-permute-done.10.refs_3_
  124.6 0.4 shard_map.137
  125.0 22.9 %all_to_all.33 = f32[256,1,128]{2,1,0:T(1,128)S(1)} all-to-all(f32[256,1,128]{2,1,0:T(1,128)S(1)} %bitcast.22), channel_id=1, replica_groups=mesh['gx'=8,'gy'=32] {'gx','gy'}, dimensions={0} | all-to-all | bytes 262144 | tf_op jit(solution)/shard_map/all_to_all | solution.py:726
  147.9 0.7 copy-done.38
  148.6 2.7 %shard_map.138 = (f32[256,512]{1,0:T(8,128)}, f32[256,512]{1,0:T(8,128)}) custom-call(f32[256,128]{1,0:T(8,128)S(1)} %bitcast.20, f32[8,128]{1,0:T(8,128)S(1)} %get-tuple-element.64.refs_1_, f32[256,512]{1,0:T(8,128)S(1)} %get-tuple-element.65.refs_2_, s32[1,256]{1,0:T(1,128)S(1)} %bitcast.24, f32[256,512]{1,0:T(8,128)S(1)} %copy-done.7, ...), custom_call_target="tpu_custom_call" | custom-call | tf_op jit(solution)/shard_map/pallas_call | solution.py:652
  (75 shorter events, 0.3 us)
Async XLA Ops:
  1.6 1.3 copy-start.13
  1.6 1.4 copy-start.23
  1.6 1.4 copy-start.39
  1.6 1.4 copy-start.40
  2.9 0.7 copy-start.37
  3.6 43.9 %copy-start.1 = (bf16[2,512,512]{2,1,0:T(8,128)(2,1)S(1)}, bf16[2,512,512]{2,1,0:T(8,128)(2,1)}, u32[]{:S(2)}) copy-start(bf16[2,512,512]{2,1,0:T(8,128)(2,1)} %constant.10.clone.refs_14_.refs_17_) | copy-start | bytes 3145732
  6.3 0.6 copy-start.43
  6.9 13.4 %copy-start.8 = (f32[256,512]{1,0:T(8,128)}, f32[256,512]{1,0:T(8,128)S(1)}, u32[]{:S(2)}) copy-start(f32[256,512]{1,0:T(8,128)S(1)} %get-tuple-element.36.refs_0_) | copy-start | bytes 1572868
  6.9 40.5 %copy-start = (bf16[2,512,512]{2,1,0:T(8,128)(2,1)S(1)}, bf16[2,512,512]{2,1,0:T(8,128)(2,1)}, u32[]{:S(2)}) copy-start(bf16[2,512,512]{2,1,0:T(8,128)(2,1)} %constant.11.clone.refs_9_.refs_10_) | copy-start | bytes 3145732
  6.9 13.3 %collective-permute-start = (f32[64,640]{1,0:T(8,128)S(1)}, f32[64,640]{1,0:T(8,128)S(1)}, u32[]{:S(2)}, u32[]{:S(2)}) collective-permute-start(f32[64,640]{1,0:T(8,128)S(1)} %get-tuple-element.37), channel_id=1, source_target_pairs={{0,32},{32,64},{64,96},{96,128},{128,160},{160,192},{192,224},{224... | collective-permute-start | bytes 491528 | tf_op jit(solution)/shard_map/ppermute | solution.py:673
  9.5 10.7 %collective-permute-start.1 = (f32[64,640]{1,0:T(8,128)S(1)}, f32[64,640]{1,0:T(8,128)S(1)}, u32[]{:S(2)}, u32[]{:S(2)}) collective-permute-start(f32[64,640]{1,0:T(8,128)S(1)} %get-tuple-element.38), channel_id=1, source_target_pairs={{32,0},{64,32},{96,64},{128,96},{160,128},{192,160},{224,192},{0,2... | collective-permute-start | bytes 491528 | tf_op jit(solution)/shard_map/ppermute | solution.py:673
  20.2 0.7 copy-start.15
  20.2 0.7 copy-start.17
  20.2 27.3 %copy-start.34 = (f32[8,512]{1,0:T(8,128)S(1)}, f32[8,512]{1,0:T(8,128)}, u32[]{:S(2)}) copy-start(f32[8,512]{1,0:T(8,128)} %constant.14.clone.refs_8_.refs_6_) | copy-start | bytes 49156
  20.9 0.7 copy-start.35
  21.6 0.7 copy-start.45
  22.3 0.7 copy-start.46
  23.0 24.5 %copy-start.12 = (bf16[2,128,512]{2,1,0:T(8,128)(2,1)S(1)}, bf16[2,128,512]{2,1,0:T(8,128)(2,1)}, u32[]{:S(2)}) copy-start(bf16[2,128,512]{2,1,0:T(8,128)(2,1)} %constant.13.clone.refs_10_.refs_11_) | copy-start | bytes 786436
  23.0 24.5 %all-to-all-start.1 = ((f32[32,8,128]{2,1,0:T(8,128)}), f32[32,8,128]{2,1,0:T(8,128)}, u32[]{:S(2)}, u32[]{:S(2)}) async-start(f32[32,8,128]{2,1,0:T(8,128)} %copy-done.35), calls=%async_computation.1 | async-start | bytes 262144 | tf_op jit(solution)/shard_map/all_to_all | solution.py:687
  33.2 12.8 %collective-permute-start.2 = (f32[96,640]{1,0:T(8,128)}, f32[96,640]{1,0:T(8,128)S(1)}, u32[]{:S(2)}, u32[]{:S(2)}) collective-permute-start(f32[96,640]{1,0:T(8,128)} %copy-done.46), channel_id=1, source_target_pairs={{0,1},{1,2},{2,3},{3,4},{4,5},{5,6},{6,7},{7,8},{8,9},{9,10},{10,1... | collective-permute-start | bytes 737288 | tf_op jit(solution)/shard_map/ppermute | solution.py:673
  34.5 12.3 %collective-permute-start.3 = (f32[96,640]{1,0:T(8,128)}, f32[96,640]{1,0:T(8,128)S(1)}, u32[]{:S(2)}, u32[]{:S(2)}) collective-permute-start(f32[96,640]{1,0:T(8,128)} %copy-done.45), channel_id=1, source_target_pairs={{1,0},{2,1},{3,2},{4,3},{5,4},{6,5},{7,6},{8,7},{9,8},{10,9},{11,1... | collective-permute-start | bytes 737288 | tf_op jit(solution)/shard_map/ppermute | solution.py:673
  46.0 0.7 copy-start.26
  46.7 0.7 copy-start.28
  47.4 0.7 copy-start.44
  48.1 1.0 copy-start.9
  49.1 0.9 copy-start.14
  50.1 0.9 copy-start.16
  51.0 0.9 copy-start.18
  51.9 0.9 copy-start.27
  52.9 0.9 copy-start.29
  61.6 0.8 copy-start.2
  62.4 0.8 copy-start.5
  63.2 0.5 copy-start.41
  63.7 11.7 %copy-start.24 = (f32[576,128]{1,0:T(8,128)}, f32[576,128]{1,0:T(8,128)S(1)}, u32[]{:S(2)}) copy-start(f32[576,128]{1,0:T(8,128)S(1)} %get-tuple-element.53.refs_9_) | copy-start | bytes 884740
  63.7 11.6 %collective-permute-start.4 = (f32[64,512]{1,0:T(8,128)S(1)}, f32[64,512]{1,0:T(8,128)S(1)}, u32[]{:S(2)}, u32[]{:S(2)}) collective-permute-start(f32[64,512]{1,0:T(8,128)S(1)} %get-tuple-element.46), channel_id=1, source_target_pairs={{0,32},{32,64},{64,96},{96,128},{128,160},{160,192},{192,224},{224... | collective-permute-start | bytes 393224 | tf_op jit(solution)/shard_map/ppermute | solution.py:673
  65.4 9.9 %collective-permute-start.5 = (f32[64,512]{1,0:T(8,128)S(1)}, f32[64,512]{1,0:T(8,128)S(1)}, u32[]{:S(2)}, u32[]{:S(2)}) collective-permute-start(f32[64,512]{1,0:T(8,128)S(1)} %get-tuple-element.47), channel_id=1, source_target_pairs={{32,0},{64,32},{96,64},{128,96},{160,128},{192,160},{224,192},{0,2... | collective-permute-start | bytes 393224 | tf_op jit(solution)/shard_map/ppermute | solution.py:673
  75.3 0.6 copy-start.19
  75.3 0.7 copy-start.21
  76.0 0.8 copy-start.10
  76.7 0.7 copy-start.36
  77.4 0.7 copy-start.47
  78.1 0.7 copy-start.48
  78.8 18.3 %all-to-all-start.3 = ((f32[32,8,128]{2,1,0:T(8,128)}), f32[32,8,128]{2,1,0:T(8,128)}, u32[]{:S(2)}, u32[]{:S(2)}) async-start(f32[32,8,128]{2,1,0:T(8,128)} %copy-done.36), calls=%async_computation.3 | async-start | bytes 262144 | tf_op jit(solution)/shard_map/all_to_all | solution.py:687
  84.0 11.7 %collective-permute-start.6 = (f32[96,512]{1,0:T(8,128)}, f32[96,512]{1,0:T(8,128)S(1)}, u32[]{:S(2)}, u32[]{:S(2)}) collective-permute-start(f32[96,512]{1,0:T(8,128)} %copy-done.48), channel_id=1, source_target_pairs={{0,1},{1,2},{2,3},{3,4},{4,5},{5,6},{6,7},{7,8},{8,9},{9,10},{10,1... | collective-permute-start | bytes 589832 | tf_op jit(solution)/shard_map/ppermute | solution.py:673
  85.3 11.1 %collective-permute-start.7 = (f32[96,512]{1,0:T(8,128)}, f32[96,512]{1,0:T(8,128)S(1)}, u32[]{:S(2)}, u32[]{:S(2)}) collective-permute-start(f32[96,512]{1,0:T(8,128)} %copy-done.47), channel_id=1, source_target_pairs={{1,0},{2,1},{3,2},{4,3},{5,4},{6,5},{7,6},{8,7},{9,8},{10,9},{11,1... | collective-permute-start | bytes 589832 | tf_op jit(solution)/shard_map/ppermute | solution.py:673
  95.7 0.7 copy-start.30
  96.4 0.7 copy-start.32
  97.1 0.6 copy-start.42
  97.7 1.0 copy-start.3
  98.8 1.0 copy-start.6
  99.8 1.0 copy-start.11
  100.8 0.9 copy-start.20
  101.7 0.9 copy-start.22
  102.6 1.0 copy-start.25
  103.6 0.9 copy-start.31
  104.5 0.9 copy-start.33
  113.0 2.8 %collective-permute-start.8 = (f32[64,128]{1,0:T(8,128)S(1)}, f32[64,128]{1,0:T(8,128)S(1)}, u32[]{:S(2)}, u32[]{:S(2)}) collective-permute-start(f32[64,128]{1,0:T(8,128)S(1)} %get-tuple-element.57), channel_id=1, source_target_pairs={{0,32},{32,64},{64,96},{96,128},{128,160},{160,192},{192,224},{224... | collective-permute-start | bytes 98312 | tf_op jit(solution)/shard_map/ppermute | solution.py:673
  114.7 3.6 %collective-permute-start.9 = (f32[64,128]{1,0:T(8,128)S(1)}, f32[64,128]{1,0:T(8,128)S(1)}, u32[]{:S(2)}, u32[]{:S(2)}) collective-permute-start(f32[64,128]{1,0:T(8,128)S(1)} %get-tuple-element.58), channel_id=1, source_target_pairs={{32,0},{64,32},{96,64},{128,96},{160,128},{192,160},{224,192},{0,2... | collective-permute-start | bytes 98312 | tf_op jit(solution)/shard_map/ppermute | solution.py:673
  118.4 29.5 %copy-start.4 = (f32[256,512]{1,0:T(8,128)S(1)}, f32[256,512]{1,0:T(8,128)}, u32[]{:S(2)}) copy-start(f32[256,512]{1,0:T(8,128)} %copy-done.2) | copy-start | bytes 1572868
  118.4 29.5 %copy-start.7 = (f32[256,512]{1,0:T(8,128)S(1)}, f32[256,512]{1,0:T(8,128)}, u32[]{:S(2)}) copy-start(f32[256,512]{1,0:T(8,128)} %copy-done.5) | copy-start | bytes 1572868
  118.5 6.1 %collective-permute-start.10 = (f32[64,128]{1,0:T(8,128)S(1)}, f32[64,128]{1,0:T(8,128)S(1)}, u32[]{:S(2)}, u32[]{:S(2)}) collective-permute-start(f32[64,128]{1,0:T(8,128)S(1)} %get-tuple-element.60), channel_id=1, source_target_pairs={{0,1},{1,2},{2,3},{3,4},{4,5},{5,6},{6,7},{7,8},{8,9},{9,10},{10,1... | collective-permute-start | bytes 98312 | tf_op jit(solution)/shard_map/ppermute | solution.py:673
  118.5 6.1 %collective-permute-start.11 = (f32[64,128]{1,0:T(8,128)S(1)}, f32[64,128]{1,0:T(8,128)S(1)}, u32[]{:S(2)}, u32[]{:S(2)}) collective-permute-start(f32[64,128]{1,0:T(8,128)S(1)} %get-tuple-element.61), channel_id=1, source_target_pairs={{1,0},{2,1},{3,2},{4,3},{5,4},{6,5},{7,6},{8,7},{9,8},{10,9},{11,1... | collective-permute-start | bytes 98312 | tf_op jit(solution)/shard_map/ppermute | solution.py:673
  147.9 0.7 copy-start.38

commit v3 on v2

--- a/solution.py
+++ b/solution.py
@@ -4,7 +4,7 @@
 from jax import lax
 from jax.experimental import pallas as pl
 from jax.experimental.pallas import tpu as pltpu
-from jax.sharding import PartitionSpec as P
+from jax.sharding import Mesh, PartitionSpec as P
 
 NP = 8
 EX = 4
@@ -347,20 +347,17 @@
                 column_sum = column_sum + factor_rows(column_ref, at, 25) * vertex
                 if 0 < vy < EY:
                     leaf_sum = leaf_sum + factor_rows(leaf_ref, (vx - 1) * 3 + vy - 1, 9) * vertex
-    row = lax.broadcasted_iota(jnp.int32, (8, 1), 0)
-    coeffs = jnp.where(row == 2, numbers, 0.0)
-    for at, total in ((0, top_sum), (4, column_sum)):
-        total = jnp.sum(total, axis=0, keepdims=True)
-        coeffs = jnp.where(row == at, total[:, :128], coeffs)
-        coeffs = jnp.where(row == at + 1, total[:, 128:], coeffs)
+    row = lax.broadcasted_iota(jnp.int32, (4, 1), 0)
+    coeffs = jnp.where(row == 1, numbers, 0.0)
+    coeffs = jnp.where(row == 0, jnp.sum(top_sum, axis=0, keepdims=True), coeffs)
+    coeffs = jnp.where(row == 2, jnp.sum(column_sum, axis=0, keepdims=True), coeffs)
     coeff_ref[...] = jnp.broadcast_to(coeffs[None], coeff_ref.shape)
     leaf_out_ref[...] = jnp.sum(leaf_sum, axis=0, keepdims=True)
 
 
 def coarse_of(coeffs, leaf_coeffs, spread, leaf_ref, column_ref, top_ref):
     lane = lanes()
-    top = jnp.concatenate([coeffs[0:1], coeffs[1:2]], 1)
-    column = jnp.concatenate([coeffs[4:5], coeffs[5:6]], 1)
+    top, column = coeffs[0:1], coeffs[2:3]
     around = []
     for vx in range(EX + 1):
         for vy in range(EY + 1):
@@ -389,20 +386,21 @@
     return jnp.sum(jnp.sum(x, axis=0, keepdims=True), axis=1, keepdims=True)
 
 
-def numbers_row(values):
-    lane = lanes()
-    row = jnp.zeros((1, 128), F32)
+def numbers_row(values, width=256):
+    lane = lanes(width)
+    row = jnp.zeros((1, width), F32)
     for at, value in enumerate(values):
         row = jnp.where(lane == at, value, row)
     return row
 
 
 def start_kernel(
-    order, forcing, diffusivity, reaction, loads, leaf, column, top,
-    part_ref, left_ref, right_ref, coeff_ref, leaf_out_ref, pair_ref,
+    order, forcing, diffusivity, reaction, leaf, column, top, loads_ref,
+    part_ref, left_ref, right_ref, coeff_ref, leaf_out_ref, pair_ref, order_ref, *factor_refs,
 ):
     slot = lax.broadcasted_iota(jnp.int32, (ROWS, ROWS), 0)
-    chooser = (order()[...] == slot).astype(F32)
+    order_ref[...] = order()[...]
+    chooser = (order_ref[...] == slot).astype(F32)
     diffusion = jnp.sum(chooser * diffusivity()[...], axis=1, keepdims=True)
     reacting = jnp.sum(chooser * reaction()[...], axis=1, keepdims=True)
     pair = jnp.where(lanes() == 0, diffusion, reacting)
@@ -411,20 +409,25 @@
     right_ref[:, NODES:] = pair[192:]
     source = permuted(chooser.astype(BF16), forcing()[...])
     write_planes(assemble_inside(columns(source)), part_ref, left_ref, right_ref)
-    loads_of(
-        source, loads()[...], leaf(), column(), top(), coeff_ref, leaf_out_ref, numbers_row([])
-    )
+    factors = [leaf(), column(), top()]
+    loads_of(source, loads_ref[...], *factors, coeff_ref, leaf_out_ref, numbers_row([]))
+    for ref, factor in zip(factor_refs, factors):
+        ref[...] = factor[...]
 
 
 def rows_of_plane(ref, c, plane):
     return blocks(ref[:, 128 * c : 128 * c + 128])[:, plane : plane + 1]
 
 
-def middle_kernel(part_ref, left_ref, right_ref, own_ref, gathered_ref, *refs):
+def middle_kernel(part_ref, left_ref, right_ref, gathered_ref, *refs):
     with_pair = len(refs) == 4
     low_ref, high_ref, spread_ref = refs[-3:]
-    row = lax.broadcasted_iota(jnp.int32, (8, 1), 0)
-    coeffs = jnp.where(row < 4, jnp.sum(gathered_ref[...], axis=0), own_ref[0])
+    row = lax.broadcasted_iota(jnp.int32, (4, 1), 0)
+    halves_of, me = gathered_ref.shape[0] // lax.axis_size("gx"), lax.axis_index("gx")
+    gathered = gathered_ref[...]
+    source = lax.broadcasted_iota(jnp.int32, (gathered.shape[0], 1, 1), 0) // halves_of
+    mine = jnp.sum(jnp.where(source == me, gathered, 0.0), axis=0)
+    coeffs = jnp.where(row < 2, jnp.sum(gathered, axis=0), mine)
     spread_ref[...] = jnp.broadcast_to(coeffs[None], spread_ref.shape)
     for plane, out_ref in ((0, low_ref), (EY - 1, high_ref)):
         sides = [
@@ -457,80 +460,75 @@
 def smoothed_of(cols, pair, shape, rows):
     wide = jnp.concatenate([col.reshape(-1, 128) for col in cols], 1)
     scale = 1.0 / (pair[:, 0:1] * rows[0:1] + pair[:, 1:2])
-    table = shape()[...]
+    table = shape[...]
     modes = product(wide, table) * scale
     back = product(modes, table, 1)
     return assemble_wide([blocks(col, EY + 2) for col in columns(back)])
 
 
 def stiffness_of(field, pair, stiff, rows):
-    return product(field, stiff()[...]) * pair[:, 0:1] + field * (rows[1:2] * pair[:, 1:2])
+    return product(field, stiff[...]) * pair[:, 0:1] + field * (rows[1:2] * pair[:, 1:2])
 
 
 def first_kernel(
     part_ref, left_ref, right_ref, below_ref, above_ref, pair_ref, gathered_ref, leaf_in_ref,
-    rows, shape, spread, leaf, column, top, stiff, loads,
+    rows_ref, shape, spread, leaf, column, top, stiff, loads,
     source_out, search_out, wide_pair_out, out_ref, left_out_ref, right_out_ref, coeff_ref,
     leaf_out_ref,
 ):
-    rows = rows()[...]
+    rows = rows_ref[...]
     weight = weight_of(rows[2:3])
     field = wide_field(part_ref, left_ref, right_ref, below_ref, above_ref)
     source = inner_rows(field)
-    source_out.ref[...] = source
-    source_out.send()
+    source_out[...] = source
     own = pair_ref[...]
     at = slice(NODES, NODES + 128)
     wide_pair = jnp.concatenate([blocks(left_ref[:, at]), blocks(own), blocks(right_ref[:, at])], 0)
     wide_pair = jnp.concatenate(
         [blocks(below_ref[:, at], 1), wide_pair, blocks(above_ref[:, at], 1)], 1
     ).reshape(-1, 128)
-    wide_pair_out.ref[...] = wide_pair
-    wide_pair_out.send()
+    wide_pair_out[...] = wide_pair
     coeffs = jnp.sum(gathered_ref[...], axis=0)
     smoothed = smoothed_of(field, wide_pair, shape, rows)
     search = jnp.concatenate(smoothed, 1) * weight + coarse_of(
-        coeffs, leaf_in_ref[...], spread()[...], leaf(), column(), top()
-    )
-    search_out.ref[...] = search
-    search_out.send()
+        coeffs, leaf_in_ref[...], spread[...], leaf, column, top
+    )
+    search_out[...] = search
     image = stiffness_of(search, own, stiff, rows)
     write_planes(assemble_inside(columns(image)), out_ref, left_out_ref, right_out_ref)
     numbers = numbers_row(
         [total_of(source * source * weight), total_of(image * source), total_of(image * image)]
     )
-    loads_of(image, loads()[...], leaf(), column(), top(), coeff_ref, leaf_out_ref, numbers)
+    loads_of(image, loads[...], leaf, column, top, coeff_ref, leaf_out_ref, numbers)
 
 
 def second_kernel(
     part_ref, left_ref, right_ref, below_ref, above_ref, pair_ref, gathered_ref, leaf_in_ref,
-    rows, wide_pair, shape, spread, leaf, column, top, search, source, stiff,
+    rows_ref, wide_pair, shape, spread, leaf, column, top, search, source, stiff,
     image_out, second_out, out_ref, face_left_ref, face_right_ref, face_y_ref, sums_ref, total_ref,
 ):
-    rows = rows()[...]
+    rows = rows_ref[...]
     weight = weight_of(rows[2:3])
     coeffs = jnp.sum(gathered_ref[...], axis=0)
     total_ref[...] = coeffs
-    norm, along, size = coeffs[2:3, 0:1], coeffs[2:3, 1:2], coeffs[2:3, 2:3]
+    norm, along, size = coeffs[1:2, 0:1], coeffs[1:2, 1:2], coeffs[1:2, 2:3]
     overlap = along / norm
     scale = 1.0 / jnp.sqrt(size)
     field = wide_field(part_ref, left_ref, right_ref, below_ref, above_ref)
     first = inner_rows(field)
-    image_out.ref[...] = first
-    image_out.send()
-    smoothed = smoothed_of(field, wide_pair()[...], shape, rows)
+    image_out[...] = first
+    smoothed = smoothed_of(field, wide_pair[...], shape, rows)
     whole = jnp.concatenate(smoothed, 1) * weight + coarse_of(
-        coeffs, leaf_in_ref[...], spread()[...], leaf(), column(), top()
-    )
-    second = (whole - overlap * search()[...]) * scale
-    second_out.ref[...] = second
-    second_out.send()
-    source = source()[...]
+        coeffs, leaf_in_ref[...], spread[...], leaf, column, top
+    )
+    second = (whole - overlap * search[...]) * scale
+    second_out[...] = second
+    source = source[...]
     image = stiffness_of(second, pair_ref[...], stiff, rows)
     write_faces(assemble_inside(columns(image)), out_ref, face_left_ref, face_right_ref, face_y_ref)
     basis = (first - overlap * source) * scale
     sums_ref[...] = numbers_row(
-        [total_of(basis * basis * weight), total_of(image * source), total_of(image * basis)]
+        [total_of(basis * basis * weight), total_of(image * source), total_of(image * basis)], 128
     )
 
 
@@ -545,7 +543,7 @@
 ):
     image = finish(part_ref, before_x_ref, after_x_ref, before_y_ref, after_y_ref)
     image_ref[...] = image
-    square = total_of(image * image * weight_of(rows()[2:3]))
+    square = total_of(image * image * weight_of(rows[2:3]))
     sums = jnp.where(lanes() == 3, square, sums_in_ref[...])
     sums_ref[...] = jnp.broadcast_to(sums, sums_ref.shape)
 
@@ -557,7 +555,7 @@
     sums = jnp.sum(sums_ref[...], axis=0, keepdims=True)
     squared, dot_source, dot_basis, dot_self = (sums[:, at : at + 1] for at in range(4))
     coeffs = coeff_ref[...]
-    norm, along, size = coeffs[2:3, 0:1], coeffs[2:3, 1:2], coeffs[2:3, 2:3]
+    norm, along, size = coeffs[1:2, 0:1], coeffs[1:2, 1:2], coeffs[1:2, 2:3]
     beta = jnp.sqrt(norm)
     basis_norm = jnp.sqrt(squared)
     first_diag = along / norm
@@ -577,13 +575,13 @@
     factor_one = (cosine * beta - rotated * factor_two) / first_norm
     step_one = factor_one / beta
     step_two = factor_two / basis_norm
-    chooser = chooser_back(order())
+    chooser = chooser_back(order)
     pressure_out.ref[...] = permuted(
-        chooser, step_one * search_one()[...] + step_two * search_two()[...]
+        chooser, step_one * search_one[...] + step_two * search_two[...]
     )
     pressure_out.send()
     residual_out.ref[...] = permuted(
-        chooser, source()[...] - step_one * image_one()[...] - step_two * image_two_ref[...]
+        chooser, source[...] - step_one * image_one[...] - step_two * image_two_ref[...]
     )
     residual_out.send()
 
@@ -618,7 +616,7 @@
 
 
 def run(kernel, outs, *args):
-    vmem, far = pl.BlockSpec(memory_space=pltpu.VMEM), pl.BlockSpec(memory_space=pl.ANY)
+    vmem, far = pl.BlockSpec(memory_space=pltpu.VMEM), pl.BlockSpec(memory_space=pltpu.HBM)
     far_in = [isinstance(arg, Far) for arg in args]
     far_out = [isinstance(out, Far) for out in outs]
     args = [arg.value if isinstance(arg, Far) else arg for arg in args]
@@ -660,6 +658,8 @@
 
 
 LIMIT = 28 * 2**20
+GY = ("gh", "gl")
+NEAR = ("gx", "gh")
 FIELD = shaped(ROWS, NODES)
 FACES = shaped(2, 64, 128)
 FACE = shaped(64, 128)
@@ -676,64 +676,68 @@
 def surrounded(part, left, right, coeffs, pair=None):
     wide, across = left.shape[1], (EX + 2) * EZ
     before, after = neighbours(left, right, "gx")
-    gathered = lax.all_to_all(coeffs, "gx", 0, 0)
+    gathered = lax.all_to_all(coeffs, NEAR, 0, 0)
     more = () if pair is None else (pair,)
     low, high, spread = run(
         middle_kernel,
-        (shaped(across, wide), shaped(across, wide), shaped(lax.axis_size("gy"), 8, 128)),
-        part, before, after, coeffs, gathered, *more,
-    )
-    below, above = neighbours(low, high, "gy")
-    return part, before, after, below, above, lax.all_to_all(spread, "gy", 0, 0)
+        (shaped(across, wide), shaped(across, wide), shaped(lax.axis_size("gl"), 4, 256)),
+        part, before, after, gathered, *more,
+    )
+    below, above = neighbours(low, high, GY)
+    return part, before, after, below, above, lax.all_to_all(spread, "gl", 0, 0)
 
 
 def per_device(
     forcing, element_order, diffusivity, reaction, leaf_factor, column_factor, top_factor
 ):
-    stiff, shape, loads, spread, rows = (Far(table) for table in build_tables())
-    factors = tuple(Far(factor[0, 0]) for factor in (leaf_factor, column_factor, top_factor))
-    order = Far(element_order[0])
-    coarse = (shaped(lax.axis_size("gx"), 8, 128), shaped(1, 256))
-    part, left, right, coeffs, leaves, pair = run(
+    stiff, shape, loads, spread, rows = build_tables()
+    factors = [factor[0, 0] for factor in (leaf_factor, column_factor, top_factor)]
+    coarse = (shaped(lax.axis_size(NEAR), 4, 256), shaped(1, 256))
+    part, left, right, coeffs, leaves, pair, order, *factors = run(
         start_kernel,
-        (FIELD, shaped(64, NODES + 128), shaped(64, NODES + 128), *coarse, PAIRS),
-        order, Far(forcing[0, 0]), Far(diffusivity[0]), Far(reaction[0]), loads, *factors,
+        (
+            FIELD, shaped(64, NODES + 128), shaped(64, NODES + 128), *coarse, PAIRS,
+            jax.ShapeDtypeStruct((1, ROWS), jnp.int32), *(shaped(*item.shape) for item in factors),
+        ),
+        Far(element_order[0]), Far(forcing[0, 0]), Far(diffusivity[0]), Far(reaction[0]),
+        *(Far(item) for item in factors), loads,
     )
     *around, gathered = surrounded(part, left, right, coeffs, pair)
     source, search_one, wide_pair, part, left, right, coeffs, leaves = run(
         first_kernel,
         (
-            Far(FIELD), Far(FIELD), Far(shaped((EX + 2) * (EY + 2) * EZ, 128)),
-            FIELD, shaped(64, NODES), shaped(64, NODES), *coarse,
+            FIELD, FIELD, shaped((EX + 2) * (EY + 2) * EZ, 128), FIELD, shaped(64, NODES), shaped(64, NODES), *coarse,
         ),
         *around, pair, gathered, leaves, rows, shape, spread, *factors, stiff, loads,
     )
     *around, gathered = surrounded(part, left, right, coeffs)
     image_one, search_two, part, face_left, face_right, face_y, sums, coeffs = run(
         second_kernel,
-        (Far(FIELD), Far(FIELD), FIELD, FACE, FACE, FACES, shaped(1, 128), shaped(8, 128)),
-        *around, pair, gathered, leaves, rows, Far(wide_pair), shape, spread, *factors,
-        Far(search_one), Far(source), stiff,
+        (FIELD, FIELD, FIELD, FACE, FACE, FACES, shaped(1, 128), shaped(4, 256)),
+        *around, pair, gathered, leaves, rows, wide_pair, shape, spread, *factors,
+        search_one, source, stiff,
     )
     before_x, after_x = neighbours(face_left, face_right, "gx")
     low, high = run(edge_kernel, (FACE, FACE), face_y, before_x, after_x)
-    before_y, after_y = neighbours(low, high, "gy")
-    peers = lax.axis_size(("gx", "gy"))
+    before_y, after_y = neighbours(low, high, GY)
+    peers = lax.axis_size(("gx", *GY))
     image_two, sums = run(
         last_kernel, (FIELD, shaped(peers, 128)),
         part, before_x, after_x, before_y, after_y, sums, rows,
     )
-    sums = lax.all_to_all(sums, ("gx", "gy"), 0, 0, tiled=True)
+    sums = lax.all_to_all(sums, ("gx", *GY), 0, 0, tiled=True)
     pressure, residual = run(
         end_kernel, (Far(FIELD), Far(FIELD)),
-        sums, coeffs, image_two, order, Far(search_one), Far(search_two), Far(source), Far(image_one),
+        sums, coeffs, image_two, order, search_one, search_two, source, image_one,
     )
     return (pressure[None, None], residual[None, None])
 
 
 def solution(mesh):
-    field = P("gx", "gy", None, None)
-    row = P("gx", "gy", None)
+    count_x, count_y = mesh.devices.shape
+    mesh = Mesh(mesh.devices.reshape(count_x, 2, count_y // 2), ("gx", *GY))
+    field = P("gx", GY, None, None)
+    row = P("gx", GY, None)
     return jax.shard_map(
         per_device,
         mesh=mesh,

time: 152 us -> 119 us (0.78)
  blocking collectives: 42.8 us -> 73.1 us
  local copies, waits for them, and re-layouts: 29.8 us -> 2.91 us
  waiting for transfers between devices: 19.7 us -> 4.95 us
  starting transfers between devices: 36.8 us -> 23.1 us
  Pallas kernels: 21.3 us -> 14 us
    all_to_all x3 -> x5, blocking collectives: 42.8 us -> 73.1 us  [the longest x2 27.2 us: surrounded(): gathered = lax.all_to_all(coeffs, NEAR, 0, 0)]
    unnamed x100 -> x20, local copies, waits for them, and re-layouts: 29.8 us -> 2.91 us
    all_to_all x2 -> x0, starting transfers between devices: 15.5 us -> none  [surrounded(): lax.all_to_all(spread, 'gy', 0, 0)]
    ppermute x12, waiting for transfers between devices: 19.7 us -> 4.95 us  [neighbours(): return (lax.ppermute(high, axis, up), lax.ppermute(low, axis, down))]
    pallas_call x8, Pallas kernels: 21.3 us -> 14 us  [run(): pl.pallas_call(body, out_shape=tuple(outs), in_specs=[far if is_far else...]
    ppermute x12, starting transfers between devices: 21.3 us -> 23.1 us  [neighbours(): return (lax.ppermute(high, axis, up), lax.ppermute(low, axis, down))]
  transfers between devices with their start and end apart: 14 -> 12, of which waited for: 5 -> 3; matrix products, arithmetic and copies ran while one was open for 0% -> 0% of each run, Pallas kernels for 0% -> 0%
where the time goes in v3:
time: 119 us
  blocking collectives  73.1 us (61%)
  starting transfers between devices  23.1 us (19%)
  Pallas kernels  14 us (12%)
  waiting for transfers between devices  4.95 us (4%)
  local copies, waits for them, and re-layouts  2.91 us (2%)
    all_to_all x2, blocking collectives, surrounded(): gathered = lax.all_to_all(coeffs, NEAR, 0, 0)  27.2 us
    ppermute x12, starting transfers between devices, neighbours(): return (lax.ppermute(high, axis, up), lax.ppermute(low, axis, down))  23.1 us
    all_to_all x1, blocking collectives, per_device(): sums = lax.all_to_all(sums, ('gx', *GY), 0, 0, tiled=True)  23 us
    all_to_all x2, blocking collectives, surrounded(): lax.all_to_all(spread, 'gl', 0, 0)  22.9 us
    pallas_call x8, Pallas kernels, run(): pl.pallas_call(body, out_shape=tuple(outs), in_specs=[far if is_far else...  14 us
    ppermute x12, waiting for transfers between devices, neighbours(): return (lax.ppermute(high, axis, up), lax.ppermute(low, axis, down))  4.95 us
    unnamed x20, local copies, waits for them, and re-layouts  2.91 us
  transfers between devices with their start and end apart: 12, of which 3 were waited for; matrix products, arithmetic and copies ran while one was open for 0% of the time, Pallas kernels for 0%

profile of v3, /device:TPU:1, one launch (start us, length us, event | category | flops | bytes accessed | tf_op | source)
XLA Modules:
  0.0 119.1 jit_solution(13345789983334321809)
XLA Ops:
  0.6 0.9 copy.21
  1.6 0.0 copy-start.3
  1.6 0.0 copy-start.4
  1.6 0.0 copy-start.7
  1.6 0.0 copy-start.8
  1.6 1.3 %copy_bitcast_fusion = (f32[425,256]{1,0:T(8,128)S(1)}, f32[425,256]{1,0:T(8,128)S(1)}) fusion(f32[1,1,425,256]{3,1,2,0:T(1,128)} %param.18, f32[1,1,425,256]{3,1,2,0:T(1,128)} %param.17), kind=kLoop, calls=%fused_computation | loop fusion | bytes 1740800
  2.9 0.0 copy-start.6
  2.9 0.0 copy-done.3
  2.9 0.0 copy-done.4
  2.9 0.0 copy-done.7
  3.0 0.0 copy-done.8
  3.0 0.6 copy-done.6
  3.6 0.0 copy-start.1
  3.6 2.7 %shard_map.131 = (f32[256,512]{1,0:T(8,128)S(1)}, f32[64,640]{1,0:T(8,128)S(1)}, f32[64,640]{1,0:T(8,128)S(1)}, f32[16,4,256]{2,1,0:T(4,128)S(1)}, f32[1,256]{1,...) custom-call(s32[1,256]{1,0:T(1,128)S(1)} %bitcast.21, ...), custom_call_target="tpu_custom_call" | custom-call | tf_op jit(solution)/shard_map/pallas_call | solution.py:650
  6.3 0.0 copy-start
  6.3 2.6 %collective-permute-start = (f32[64,640]{1,0:T(8,128)S(1)}, f32[64,640]{1,0:T(8,128)S(1)}, u32[]{:S(2)}, u32[]{:S(2)}) collective-permute-start(f32[64,640]{1,0:T(8,128)S(1)} %get-tuple-element.41), channel_id=1, source_target_pairs={{0,32},{32,64},{64,96},{96,128},{128,160},{160,192},{192,224},{224... | collective-permute-start | bytes 491528 | tf_op jit(solution)/shard_map/ppermute | solution.py:673
  8.9 0.7 collective-permute-start.1
  9.6 14.3 %all_to_all.31.refs_3_ = f32[16,4,256]{2,1,0:T(4,128)S(1)} all-to-all(f32[16,4,256]{2,1,0:T(4,128)S(1)} %get-tuple-element.43), channel_id=1, replica_groups=mesh['gx'=8,'gh'=2,'gl'=16] {'gx','gh'}, dimensions={0} | all-to-all | bytes 131072 | tf_op jit(solution)/shard_map/all_to_all | solution.py:679
  23.9 0.0 collective-permute-done.refs_1_
  23.9 0.0 collective-permute-done.1.refs_2_
  23.9 0.0 copy-start.2
  23.9 0.1 shard_map.132
  24.0 1.7 %collective-permute-start.2 = (f32[96,640]{1,0:T(8,128)S(1)}, f32[96,640]{1,0:T(8,128)S(1)}, u32[]{:S(2)}, u32[]{:S(2)}) collective-permute-start(f32[96,640]{1,0:T(8,128)S(1)} %get-tuple-element.45), channel_id=1, source_target_pairs={{0,1},{1,2},{2,3},{3,4},{4,5},{5,6},{6,7},{7,8},{8,9},{9,10},{10,1... | collective-permute-start | bytes 737288 | tf_op jit(solution)/shard_map/ppermute | solution.py:673
  25.7 3.9 %collective-permute-start.3 = (f32[96,640]{1,0:T(8,128)S(1)}, f32[96,640]{1,0:T(8,128)S(1)}, u32[]{:S(2)}, u32[]{:S(2)}) collective-permute-start(f32[96,640]{1,0:T(8,128)S(1)} %get-tuple-element.46), channel_id=1, source_target_pairs={{1,0},{2,1},{3,2},{4,3},{5,4},{6,5},{7,6},{8,7},{9,8},{10,9},{11,1... | collective-permute-start | bytes 737288 | tf_op jit(solution)/shard_map/ppermute | solution.py:673
  29.6 0.0 copy-start.5
  29.6 13.0 %all_to_all.32.refs_6_ = f32[16,4,256]{2,1,0:T(4,128)S(1)} all-to-all(f32[16,4,256]{2,1,0:T(4,128)S(1)} %get-tuple-element.47), channel_id=1, replica_groups=mesh['gx'=8,'gh'=2,'gl'=16] {'gl'}, dimensions={0} | all-to-all | bytes 131072 | tf_op jit(solution)/shard_map/all_to_all | solution.py:687
  42.6 0.0 collective-permute-done.2.refs_3_
  42.6 0.0 collective-permute-done.3.refs_4_
  42.6 0.0 copy-done.1
  42.6 0.0 copy-done
  42.6 0.0 copy-done.2
  42.6 0.0 copy-done.5
  42.6 4.4 %shard_map.133 = (f32[256,512]{1,0:T(8,128)S(1)}, f32[256,512]{1,0:T(8,128)S(1)}, f32[576,128]{1,0:T(8,128)S(1)}, f32[256,512]{1,0:T(8,128)S(1)}, f32[64,512]{1,...) custom-call(f32[256,512]{1,0:T(8,128)S(1)} %get-tuple-element.40.refs_0_, ...), custom_call_target="tpu_custom_call" | custom-call | tf_op jit(solution)/shard_map/pallas_call | solution.py:650
  47.1 2.4 %collective-permute-start.4 = (f32[64,512]{1,0:T(8,128)S(1)}, f32[64,512]{1,0:T(8,128)S(1)}, u32[]{:S(2)}, u32[]{:S(2)}) collective-permute-start(f32[64,512]{1,0:T(8,128)S(1)} %get-tuple-element.53), channel_id=1, source_target_pairs={{0,32},{32,64},{64,96},{96,128},{128,160},{160,192},{192,224},{224... | collective-permute-start | bytes 393224 | tf_op jit(solution)/shard_map/ppermute | solution.py:673
  49.5 0.0 collective-permute-start.5
  49.5 12.9 %all_to_all.33.refs_3_ = f32[16,4,256]{2,1,0:T(4,128)S(1)} all-to-all(f32[16,4,256]{2,1,0:T(4,128)S(1)} %get-tuple-element.55), channel_id=1, replica_groups=mesh['gx'=8,'gh'=2,'gl'=16] {'gx','gh'}, dimensions={0} | all-to-all | bytes 131072 | tf_op jit(solution)/shard_map/all_to_all | solution.py:679
  62.4 0.0 collective-permute-done.4.refs_1_
  62.4 0.0 collective-permute-done.5.refs_2_
  62.4 0.1 shard_map.134
  62.5 0.8 collective-permute-start.6
  63.3 4.1 %collective-permute-start.7 = (f32[96,512]{1,0:T(8,128)S(1)}, f32[96,512]{1,0:T(8,128)S(1)}, u32[]{:S(2)}, u32[]{:S(2)}) collective-permute-start(f32[96,512]{1,0:T(8,128)S(1)} %get-tuple-element.57), channel_id=1, source_target_pairs={{1,0},{2,1},{3,2},{4,3},{5,4},{6,5},{7,6},{8,7},{9,8},{10,9},{11,1... | collective-permute-start | bytes 589832 | tf_op jit(solution)/shard_map/ppermute | solution.py:673
  67.3 9.9 %all_to_all.34.refs_6_ = f32[16,4,256]{2,1,0:T(4,128)S(1)} all-to-all(f32[16,4,256]{2,1,0:T(4,128)S(1)} %get-tuple-element.58), channel_id=1, replica_groups=mesh['gx'=8,'gh'=2,'gl'=16] {'gl'}, dimensions={0} | all-to-all | bytes 131072 | tf_op jit(solution)/shard_map/all_to_all | solution.py:687
  77.3 0.0 collective-permute-done.6.refs_3_
  77.3 0.0 collective-permute-done.7.refs_4_
  77.3 4.4 %shard_map.135 = (f32[256,512]{1,0:T(8,128)S(1)}, f32[256,512]{1,0:T(8,128)S(1)}, f32[256,512]{1,0:T(8,128)S(1)}, f32[64,128]{1,0:T(8,128)S(1)}, f32[64,128]{1,0...) custom-call(f32[256,512]{1,0:T(8,128)S(1)} %get-tuple-element.52.refs_0_, ...), custom_call_target="tpu_custom_call" | custom-call | tf_op jit(solution)/shard_map/pallas_call | solution.py:650
  81.6 2.2 %collective-permute-start.8 = (f32[64,128]{1,0:T(8,128)S(1)}, f32[64,128]{1,0:T(8,128)S(1)}, u32[]{:S(2)}, u32[]{:S(2)}) collective-permute-start(f32[64,128]{1,0:T(8,128)S(1)} %get-tuple-element.64), channel_id=1, source_target_pairs={{0,32},{32,64},{64,96},{96,128},{128,160},{160,192},{192,224},{224... | collective-permute-start | bytes 98312 | tf_op jit(solution)/shard_map/ppermute | solution.py:673
  83.9 0.0 collective-permute-start.9
  83.9 1.0 collective-permute-done.8.refs_1_
  84.9 2.6 %collective-permute-done.9.refs_2_ = f32[64,128]{1,0:T(8,128)S(1)} collective-permute-done((f32[64,128]{1,0:T(8,128)S(1)}, f32[64,128]{1,0:T(8,128)S(1)}, u32[]{:S(2)}, u32[]{:S(2)}) %collective-permute-start.9) | collective-permute-done | bytes 32800 | tf_op jit(solution)/shard_map/ppermute | solution.py:673
  87.5 0.1 shard_map.136
  87.6 0.7 collective-permute-start.10
  88.3 4.1 %collective-permute-start.11 = (f32[64,128]{1,0:T(8,128)S(1)}, f32[64,128]{1,0:T(8,128)S(1)}, u32[]{:S(2)}, u32[]{:S(2)}) collective-permute-start(f32[64,128]{1,0:T(8,128)S(1)} %get-tuple-element.68), channel_id=1, source_target_pairs={{1,0},{2,1},{3,2},{4,3},{5,4},{6,5},{7,6},{8,7},{9,8},{10,9},{11,1... | collective-permute-start | bytes 98312 | tf_op jit(solution)/shard_map/ppermute | solution.py:673
  92.4 1.3 %collective-permute-done.10.refs_3_ = f32[64,128]{1,0:T(8,128)S(1)} collective-permute-done((f32[64,128]{1,0:T(8,128)S(1)}, f32[64,128]{1,0:T(8,128)S(1)}, u32[]{:S(2)}, u32[]{:S(2)}) %collective-permute-start.10) | collective-permute-done | bytes 32800 | tf_op jit(solution)/shard_map/ppermute | solution.py:673
  93.7 0.0 collective-permute-done.11.refs_4_
  93.7 0.2 shard_map.137
  93.9 23.0 %all_to_all.35 = f32[256,1,128]{2,1,0:T(1,128)S(1)} all-to-all(f32[256,1,128]{2,1,0:T(1,128)S(1)} %bitcast.20), channel_id=1, replica_groups=mesh['gx'=8,'gh'=2,'gl'=16] {'gx','gh','gl'}, dimensions={0} | all-to-all | bytes 262144 | tf_op jit(solution)/shard_map/all_to_all | solution.py:728
  116.9 2.0 %shard_map.138 = (f32[256,512]{1,0:T(8,128)}, f32[256,512]{1,0:T(8,128)}) custom-call(f32[256,128]{1,0:T(8,128)S(1)} %bitcast.18, f32[4,256]{1,0:T(4,128)S(1)} %get-tuple-element.71.refs_1_, f32[256,512]{1,0:T(8,128)S(1)} %get-tuple-element.72.refs_2_, s32[1,256]{1,0:T(1,128)S(1)} %get-tuple-element.73.refs_3_, ...), custom_call_target="tpu_custom_call" | custom-call | tf_op jit(solution)/shard_map/pallas_call | solution.py:650
Async XLA Ops:
  1.6 1.3 %copy-start.3 = (bf16[2,512,128]{2,1,0:T(8,128)(2,1)S(1)}, bf16[2,512,128]{2,1,0:T(8,128)(2,1)}, u32[]{:S(2)}) copy-start(bf16[2,512,128]{2,1,0:T(8,128)(2,1)} %constant.12.clone.refs_7_.refs_15_) | copy-start | bytes 786436
  1.6 1.4 %copy-start.4 = (f32[1,1,256,512]{3,2,1,0:T(8,128)S(1)}, f32[1,1,256,512]{3,2,1,0:T(8,128)}, u32[]{:S(2)}) copy-start(f32[1,1,256,512]{3,2,1,0:T(8,128)} %param.12) | copy-start | bytes 1572868
  1.6 1.4 %copy-start.7 = (f32[1,1,256]{2,1,0:T(1,128)S(1)}, f32[1,1,256]{2,1,0:T(1,128)}, u32[]{:S(2)}) copy-start(f32[1,1,256]{2,1,0:T(1,128)} %param.14) | copy-start | bytes 3076
  1.6 1.4 %copy-start.8 = (f32[1,1,256]{2,1,0:T(1,128)S(1)}, f32[1,1,256]{2,1,0:T(1,128)}, u32[]{:S(2)}) copy-start(f32[1,1,256]{2,1,0:T(1,128)} %param.15) | copy-start | bytes 3076
  2.9 0.7 copy-start.6
  3.6 39.0 %copy-start.1 = (bf16[2,512,512]{2,1,0:T(8,128)(2,1)S(1)}, bf16[2,512,512]{2,1,0:T(8,128)(2,1)}, u32[]{:S(2)}) copy-start(bf16[2,512,512]{2,1,0:T(8,128)(2,1)} %constant.10.clone.refs_14_.refs_17_) | copy-start | bytes 3145732
  6.3 36.3 %copy-start = (bf16[2,512,512]{2,1,0:T(8,128)(2,1)S(1)}, bf16[2,512,512]{2,1,0:T(8,128)(2,1)}, u32[]{:S(2)}) copy-start(bf16[2,512,512]{2,1,0:T(8,128)(2,1)} %constant.11.clone.refs_9_.refs_10_) | copy-start | bytes 3145732
  6.3 17.6 %collective-permute-start = (f32[64,640]{1,0:T(8,128)S(1)}, f32[64,640]{1,0:T(8,128)S(1)}, u32[]{:S(2)}, u32[]{:S(2)}) collective-permute-start(f32[64,640]{1,0:T(8,128)S(1)} %get-tuple-element.41), channel_id=1, source_target_pairs={{0,32},{32,64},{64,96},{96,128},{128,160},{160,192},{192,224},{224... | collective-permute-start | bytes 491528 | tf_op jit(solution)/shard_map/ppermute | solution.py:673
  8.9 15.0 %collective-permute-start.1 = (f32[64,640]{1,0:T(8,128)S(1)}, f32[64,640]{1,0:T(8,128)S(1)}, u32[]{:S(2)}, u32[]{:S(2)}) collective-permute-start(f32[64,640]{1,0:T(8,128)S(1)} %get-tuple-element.42), channel_id=1, source_target_pairs={{32,0},{64,32},{96,64},{128,96},{160,128},{192,160},{224,192},{0,2... | collective-permute-start | bytes 491528 | tf_op jit(solution)/shard_map/ppermute | solution.py:673
  23.9 18.7 %copy-start.2 = (bf16[2,128,512]{2,1,0:T(8,128)(2,1)S(1)}, bf16[2,128,512]{2,1,0:T(8,128)(2,1)}, u32[]{:S(2)}) copy-start(bf16[2,128,512]{2,1,0:T(8,128)(2,1)} %constant.13.clone.refs_10_.refs_11_) | copy-start | bytes 786436
  24.0 18.6 %collective-permute-start.2 = (f32[96,640]{1,0:T(8,128)S(1)}, f32[96,640]{1,0:T(8,128)S(1)}, u32[]{:S(2)}, u32[]{:S(2)}) collective-permute-start(f32[96,640]{1,0:T(8,128)S(1)} %get-tuple-element.45), channel_id=1, source_target_pairs={{0,1},{1,2},{2,3},{3,4},{4,5},{5,6},{6,7},{7,8},{8,9},{9,10},{10,1... | collective-permute-start | bytes 737288 | tf_op jit(solution)/shard_map/ppermute | solution.py:673
  25.7 16.8 %collective-permute-start.3 = (f32[96,640]{1,0:T(8,128)S(1)}, f32[96,640]{1,0:T(8,128)S(1)}, u32[]{:S(2)}, u32[]{:S(2)}) collective-permute-start(f32[96,640]{1,0:T(8,128)S(1)} %get-tuple-element.46), channel_id=1, source_target_pairs={{1,0},{2,1},{3,2},{4,3},{5,4},{6,5},{7,6},{8,7},{9,8},{10,9},{11,1... | collective-permute-start | bytes 737288 | tf_op jit(solution)/shard_map/ppermute | solution.py:673
  29.6 13.0 %copy-start.5 = (f32[8,512]{1,0:T(8,128)S(1)}, f32[8,512]{1,0:T(8,128)}, u32[]{:S(2)}) copy-start(f32[8,512]{1,0:T(8,128)} %constant.14.clone.refs_8_.refs_6_) | copy-start | bytes 49156
  47.1 15.3 %collective-permute-start.4 = (f32[64,512]{1,0:T(8,128)S(1)}, f32[64,512]{1,0:T(8,128)S(1)}, u32[]{:S(2)}, u32[]{:S(2)}) collective-permute-start(f32[64,512]{1,0:T(8,128)S(1)} %get-tuple-element.53), channel_id=1, source_target_pairs={{0,32},{32,64},{64,96},{96,128},{128,160},{160,192},{192,224},{224... | collective-permute-start | bytes 393224 | tf_op jit(solution)/shard_map/ppermute | solution.py:673
  49.5 12.9 %collective-permute-start.5 = (f32[64,512]{1,0:T(8,128)S(1)}, f32[64,512]{1,0:T(8,128)S(1)}, u32[]{:S(2)}, u32[]{:S(2)}) collective-permute-start(f32[64,512]{1,0:T(8,128)S(1)} %get-tuple-element.54), channel_id=1, source_target_pairs={{32,0},{64,32},{96,64},{128,96},{160,128},{192,160},{224,192},{0,2... | collective-permute-start | bytes 393224 | tf_op jit(solution)/shard_map/ppermute | solution.py:673
  62.5 14.8 %collective-permute-start.6 = (f32[96,512]{1,0:T(8,128)S(1)}, f32[96,512]{1,0:T(8,128)S(1)}, u32[]{:S(2)}, u32[]{:S(2)}) collective-permute-start(f32[96,512]{1,0:T(8,128)S(1)} %get-tuple-element.56), channel_id=1, source_target_pairs={{0,1},{1,2},{2,3},{3,4},{4,5},{5,6},{6,7},{7,8},{8,9},{9,10},{10,1... | collective-permute-start | bytes 589832 | tf_op jit(solution)/shard_map/ppermute | solution.py:673
  63.3 14.0 %collective-permute-start.7 = (f32[96,512]{1,0:T(8,128)S(1)}, f32[96,512]{1,0:T(8,128)S(1)}, u32[]{:S(2)}, u32[]{:S(2)}) collective-permute-start(f32[96,512]{1,0:T(8,128)S(1)} %get-tuple-element.57), channel_id=1, source_target_pairs={{1,0},{2,1},{3,2},{4,3},{5,4},{6,5},{7,6},{8,7},{9,8},{10,9},{11,1... | collective-permute-start | bytes 589832 | tf_op jit(solution)/shard_map/ppermute | solution.py:673
  81.6 3.2 %collective-permute-start.8 = (f32[64,128]{1,0:T(8,128)S(1)}, f32[64,128]{1,0:T(8,128)S(1)}, u32[]{:S(2)}, u32[]{:S(2)}) collective-permute-start(f32[64,128]{1,0:T(8,128)S(1)} %get-tuple-element.64), channel_id=1, source_target_pairs={{0,32},{32,64},{64,96},{96,128},{128,160},{160,192},{192,224},{224... | collective-permute-start | bytes 98312 | tf_op jit(solution)/shard_map/ppermute | solution.py:673
  83.9 3.6 %collective-permute-start.9 = (f32[64,128]{1,0:T(8,128)S(1)}, f32[64,128]{1,0:T(8,128)S(1)}, u32[]{:S(2)}, u32[]{:S(2)}) collective-permute-start(f32[64,128]{1,0:T(8,128)S(1)} %get-tuple-element.65), channel_id=1, source_target_pairs={{32,0},{64,32},{96,64},{128,96},{160,128},{192,160},{224,192},{0,2... | collective-permute-start | bytes 98312 | tf_op jit(solution)/shard_map/ppermute | solution.py:673
  87.6 6.1 %collective-permute-start.10 = (f32[64,128]{1,0:T(8,128)S(1)}, f32[64,128]{1,0:T(8,128)S(1)}, u32[]{:S(2)}, u32[]{:S(2)}) collective-permute-start(f32[64,128]{1,0:T(8,128)S(1)} %get-tuple-element.67), channel_id=1, source_target_pairs={{0,1},{1,2},{2,3},{3,4},{4,5},{5,6},{6,7},{7,8},{8,9},{9,10},{10,1... | collective-permute-start | bytes 98312 | tf_op jit(solution)/shard_map/ppermute | solution.py:673
  88.3 5.4 %collective-permute-start.11 = (f32[64,128]{1,0:T(8,128)S(1)}, f32[64,128]{1,0:T(8,128)S(1)}, u32[]{:S(2)}, u32[]{:S(2)}) collective-permute-start(f32[64,128]{1,0:T(8,128)S(1)} %get-tuple-element.68), channel_id=1, source_target_pairs={{1,0},{2,1},{3,2},{4,3},{5,4},{6,5},{7,6},{8,7},{9,8},{10,9},{11,1... | collective-permute-start | bytes 98312 | tf_op jit(solution)/shard_map/ppermute | solution.py:673

commit v4 on v3

--- a/solution.py
+++ b/solution.py
@@ -103,9 +103,15 @@
         + np.kron(np.kron(filler, eigvals), filler)
         + np.kron(np.kron(filler, filler), eigvals)
     )
-    shape_full = np.kron(np.kron(modes, modes), modes)
     linear = np.stack([(1.0 - points) / 2.0, (1.0 + points) / 2.0], 1)
     trilinear = np.kron(np.kron(linear, linear), linear)
+    even_first = np.argsort([np.sign(modes[0, m]) != np.sign(modes[7, m]) for m in range(8)], kind="stable")
+    first = np.kron(np.kron(modes[:4, even_first], modes), modes)
+    shape_full = np.stack([first[:, :256], first[:, 256:]])
+    eigen_full = eigen_full.reshape(8, 64)[even_first].reshape(-1)
+    tiles = stiff_full.reshape(8, 64, 8, 64)
+    near, mirrored = tiles[:4, :, :4], tiles[:4, :, :3:-1]
+    stiff_full = np.stack([near + mirrored, near - mirrored]).reshape(2, 256, 256) / 2.0
     ends = np.where((np.arange(8) == 0) | (np.arange(8) == 7), 0.5, 1.0)
     share = np.kron(np.kron(ends, ends), ends)
     rows = np.zeros((8, NODES), np.float32)
@@ -138,6 +144,22 @@
         return lax.dot_general(p, q, dims, preferred_element_type=F32)
 
     return dot(high, table[0]) + (dot(low, table[0]) + dot(high, table[1]))
+
+
+def fold(cols):
+    far, near = pltpu.roll(cols[3], 64, 1), pltpu.roll(cols[2], 64, 1)
+    even = jnp.concatenate([cols[0] + far, cols[1] + near], 1)
+    return even, jnp.concatenate([cols[0] - far, cols[1] - near], 1)
+
+
+def unfold(even, odd):
+    total, rest = even + odd, even - odd
+    last, third = pltpu.roll(rest[:, :128], 64, 1), pltpu.roll(rest[:, 128:], 64, 1)
+    return [total[:, :128], total[:, 128:], third, last]
+
+
+def part_of(table, at):
+    return table[0, at], table[1, at]
 
 
 def permuted(chooser, x):
@@ -221,15 +243,15 @@
     return result
 
 
-def joined_x(own, left, right):
-    own, left, right = list(own), list(left), list(right)
-    low, high = own[0], own[3]
-    tail = jnp.zeros_like(low[1:])
-    own[0] = low + jnp.concatenate([first_plane(left[3]), tail], 0)
-    own[3] = high + jnp.concatenate([tail, last_plane(right[0])], 0)
+def joined_x(middle, left, right):
+    middle, left, right = list(middle), list(left), list(right)
+    low, high = middle[0], middle[3]
+    hole = jnp.zeros_like(low[1:])
+    middle[0] = low + jnp.concatenate([first_plane(left[3]), hole], 0)
+    middle[3] = high + jnp.concatenate([hole, last_plane(right[0])], 0)
     left[3] = left[3] + last_plane(low[:1])
     right[0] = right[0] + first_plane(high[EX - 1 :])
-    return [jnp.concatenate(parts, 0) for parts in zip(left, own, right)]
+    return [jnp.concatenate(parts, 0) for parts in zip(left, middle, right)]
 
 
 def joined_y(middle, below, above):
@@ -252,7 +274,7 @@
     ]
 
 
-def write_faces(cols, part_ref, face_left_ref, face_right_ref, face_y_ref):
+def write_faces(cols, part_ref, face_left_ref, face_right_ref, face_low_ref, face_high_ref):
     row_y = lanes() // NP % NP
     for c in range(4):
         part_ref[:, 128 * c : 128 * c + 128] = cols[c]
@@ -266,51 +288,73 @@
         last = jnp.where(row_y == NP - 1, split[:, EY - 1].reshape(64, 128), 0.0)
         low = low + (pltpu.roll(first, 8 * c, 1) if c else first)
         high = high + pltpu.roll(last, (72 + 8 * c) % 128, 1)
-    face_y_ref[0] = low
-    face_y_ref[1] = high
-
-
-def write_planes(cols, part_ref, left_ref, right_ref):
+    face_low_ref[...] = low
+    face_high_ref[...] = high
+
+
+def write_planes(cols, part_ref, below_ref, above_ref):
     for c in range(4):
         at = slice(128 * c, 128 * c + 128)
         part_ref[:, at] = cols[c]
-        left_ref[:, at] = cols[c][:64]
-        right_ref[:, at] = cols[c][192:]
-
-
-def edge_kernel(face_y_ref, before_ref, after_ref, out_low_ref, out_high_ref):
-    lane = lanes()
-    first = lane < 8
-    last = (lane >= 88) & (lane < 96)
-    out_low_ref[...] = face_y_ref[0]
-    out_high_ref[...] = face_y_ref[1]
-    out_low_ref[0:16] += jnp.where(first, pltpu.roll(before_ref[0:16], 64, 1), 0.0)
-    out_high_ref[0:16] += jnp.where(first, pltpu.roll(before_ref[48:64], 8, 1), 0.0)
-    out_low_ref[48:64] += jnp.where(last, pltpu.roll(after_ref[0:16], 88, 1), 0.0)
-    out_high_ref[48:64] += jnp.where(last, pltpu.roll(after_ref[48:64], 32, 1), 0.0)
-
-
-def finish(part_ref, before_x_ref, after_x_ref, before_y_ref, after_y_ref):
+        below_ref[:, at] = blocks(cols[c])[:, 0].reshape(64, 128)
+        above_ref[:, at] = blocks(cols[c])[:, EY - 1].reshape(64, 128)
+
+
+def faces_added(part_ref, before_x_ref, after_x_ref, before_y_ref, after_y_ref):
     lane = lanes()
     row_y = lane // NP % NP
     rest = jnp.zeros((192, 128), F32)
     before = jnp.where(lane < 64, pltpu.roll(before_x_ref[...], 64, 1), 0.0)
     after = jnp.where(lane >= 64, pltpu.roll(after_x_ref[...], 64, 1), 0.0)
+    none = jnp.zeros((ROWS, 128), F32)
+    over_x = [jnp.concatenate([before, rest], 0), none, none, jnp.concatenate([rest, after], 0)]
     before_y, after_y = before_y_ref[...], after_y_ref[...]
     hole = jnp.zeros((EX, EY - 2, EZ, 128), F32)
-    result = []
+    own, over_y = [], []
     for c in range(4):
-        col = part_ref[:, 128 * c : 128 * c + 128]
-        if c == 0:
-            col = col + jnp.concatenate([before, rest], 0)
-        if c == 3:
-            col = col + jnp.concatenate([rest, after], 0)
+        own.append(part_ref[:, 128 * c : 128 * c + 128])
         low = pltpu.roll(before_y, (128 - 8 * c) % 128, 1) if c else before_y
         low = jnp.where(row_y == 0, low, 0.0).reshape(EX, 1, EZ, 128)
         high = jnp.where(row_y == NP - 1, pltpu.roll(after_y, 56 - 8 * c, 1), 0.0)
         high = high.reshape(EX, 1, EZ, 128)
-        result.append(col + jnp.concatenate([low, hole, high], 1).reshape(ROWS, 128))
-    return jnp.concatenate(result, 1)
+        over_y.append(jnp.concatenate([low, hole, high], 1).reshape(ROWS, 128))
+    return own, over_x, over_y
+
+
+EDGES = ((-1, -1, 0, 0, 0), (-1, 1, 48, 0, 56), (1, -1, 192, 3, 64), (1, 1, 240, 3, 120))
+
+
+def over_lanes(x):
+    for shift in (8, 16, 32, 64):
+        x = x + pltpu.roll(x, shift, 1)
+    return x
+
+
+def diagonal_of(side_x, side_y):
+    count_x, count_y = lax.axis_size("gx"), lax.axis_size(GY)
+    at_y = lax.axis_index("gh") * lax.axis_size("gl") + lax.axis_index("gl")
+    at_x = lax.rem(lax.axis_index("gx") + count_x + side_x, count_x)
+    return at_x * count_y + lax.rem(at_y + count_y + side_y, count_y)
+
+
+def edge_out(part_ref, row, block, first):
+    lane = lanes()
+    piece = part_ref[row : row + EZ, 128 * block : 128 * block + 128]
+    piece = over_lanes(jnp.where((lane >= first) & (lane < first + NP), piece, 0.0))
+    level = lax.broadcasted_iota(jnp.int32, (EZ, 1), 0)
+    return jnp.sum(jnp.where(lane // NP == level, piece, 0.0), axis=0, keepdims=True)
+
+
+def edge_in(line, first):
+    lane = lanes()
+    line = jnp.where(is_number(lane), pltpu.roll(line, 127, 1), line)
+    level = lax.broadcasted_iota(jnp.int32, (EZ, 1), 0)
+    spread = over_lanes(jnp.where(lane // NP == level, line, 0.0))
+    return jnp.where((lane >= first) & (lane < first + NP), spread, 0.0)
+
+
+def is_number(lane):
+    return (lane % NP == NP - 1) & (lane < 4 * NP)
 
 
 def factor_rows(ref, at, count):
@@ -386,40 +430,42 @@
     return jnp.sum(jnp.sum(x, axis=0, keepdims=True), axis=1, keepdims=True)
 
 
-def numbers_row(values, width=256):
+def numbers_row(values, width=256, step=1):
     lane = lanes(width)
     row = jnp.zeros((1, width), F32)
     for at, value in enumerate(values):
-        row = jnp.where(lane == at, value, row)
+        row = jnp.where(lane == step * (at + 1) - 1, value, row)
     return row
 
 
 def start_kernel(
-    order, forcing, diffusivity, reaction, leaf, column, top, loads_ref,
-    part_ref, left_ref, right_ref, coeff_ref, leaf_out_ref, pair_ref, order_ref, *factor_refs,
+    order_ref, forcing_ref, diffusivity_ref, reaction_ref, leaf_ref, column_ref, top_ref, loads_ref,
+    part_ref, below_ref, above_ref, coeff_ref, leaf_out_ref, pair_ref,
 ):
     slot = lax.broadcasted_iota(jnp.int32, (ROWS, ROWS), 0)
-    order_ref[...] = order()[...]
     chooser = (order_ref[...] == slot).astype(F32)
-    diffusion = jnp.sum(chooser * diffusivity()[...], axis=1, keepdims=True)
-    reacting = jnp.sum(chooser * reaction()[...], axis=1, keepdims=True)
+    diffusion = jnp.sum(chooser * diffusivity_ref[...], axis=1, keepdims=True)
+    reacting = jnp.sum(chooser * reaction_ref[...], axis=1, keepdims=True)
     pair = jnp.where(lanes() == 0, diffusion, reacting)
     pair_ref[...] = pair
-    left_ref[:, NODES:] = pair[:64]
-    right_ref[:, NODES:] = pair[192:]
-    source = permuted(chooser.astype(BF16), forcing()[...])
-    write_planes(assemble_inside(columns(source)), part_ref, left_ref, right_ref)
-    factors = [leaf(), column(), top()]
-    loads_of(source, loads_ref[...], *factors, coeff_ref, leaf_out_ref, numbers_row([]))
-    for ref, factor in zip(factor_refs, factors):
-        ref[...] = factor[...]
-
-
-def rows_of_plane(ref, c, plane):
-    return blocks(ref[:, 128 * c : 128 * c + 128])[:, plane : plane + 1]
-
-
-def middle_kernel(part_ref, left_ref, right_ref, gathered_ref, *refs):
+    below_ref[:, NODES:] = blocks(pair)[:, 0].reshape(64, 128)
+    above_ref[:, NODES:] = blocks(pair)[:, EY - 1].reshape(64, 128)
+    source = permuted(chooser.astype(BF16), forcing_ref[...])
+    write_planes(assemble_inside(columns(source)), part_ref, below_ref, above_ref)
+    loads_of(
+        source, loads_ref[...], leaf_ref, column_ref, top_ref, coeff_ref, leaf_out_ref, numbers_row([])
+    )
+
+
+def own_plane(ref, c, plane):
+    return blocks(ref[EY * EZ * plane : EY * EZ * (plane + 1), 128 * c : 128 * c + 128])
+
+
+def got_plane(ref, c, plane):
+    return blocks(ref[EZ * plane : EZ * (plane + 1), 128 * c : 128 * c + 128], 1)
+
+
+def middle_kernel(part_ref, below_ref, above_ref, gathered_ref, *refs):
     with_pair = len(refs) == 4
     low_ref, high_ref, spread_ref = refs[-3:]
     row = lax.broadcasted_iota(jnp.int32, (4, 1), 0)
@@ -429,73 +475,77 @@
     mine = jnp.sum(jnp.where(source == me, gathered, 0.0), axis=0)
     coeffs = jnp.where(row < 2, jnp.sum(gathered, axis=0), mine)
     spread_ref[...] = jnp.broadcast_to(coeffs[None], spread_ref.shape)
-    for plane, out_ref in ((0, low_ref), (EY - 1, high_ref)):
-        sides = [
-            [rows_of_plane(ref, c, plane) for c in range(4)] for ref in (part_ref, left_ref, right_ref)
-        ]
-        for c, col in enumerate(joined_x(*sides)):
+    for plane, out_ref in ((0, low_ref), (EX - 1, high_ref)):
+        for c in range(4):
+            sides = got_plane(below_ref, c, plane), got_plane(above_ref, c, plane)
+            col = joined_y(own_plane(part_ref, c, plane), *sides)
             out_ref[:, 128 * c : 128 * c + 128] = col.reshape(-1, 128)
         if with_pair:
-            sides = [rows_of_plane(left_ref, 4, plane), rows_of_plane(refs[0], 0, plane)]
-            sides.append(rows_of_plane(right_ref, 4, plane))
-            out_ref[:, NODES:] = jnp.concatenate(sides, 0).reshape(-1, 128)
-
-
-def wide_field(part_ref, left_ref, right_ref, below_ref, above_ref):
-    sides = [
-        [blocks(ref[:, 128 * c : 128 * c + 128]) for c in range(4)]
-        for ref in (part_ref, left_ref, right_ref)
-    ]
-    result = []
-    for c, middle in enumerate(joined_x(*sides)):
+            sides = [got_plane(below_ref, 4, plane), own_plane(refs[0], 0, plane)]
+            sides.append(got_plane(above_ref, 4, plane))
+            out_ref[:, NODES:] = jnp.concatenate(sides, 1).reshape(-1, 128)
+
+
+def wide_field(part_ref, below_ref, above_ref, left_ref, right_ref):
+    middle, left, right = [], [], []
+    for c in range(4):
         at = slice(128 * c, 128 * c + 128)
-        result.append(joined_y(middle, blocks(below_ref[:, at], 1), blocks(above_ref[:, at], 1)))
-    return result
+        middle.append(
+            joined_y(blocks(part_ref[:, at]), blocks(below_ref[:, at], 1), blocks(above_ref[:, at], 1))
+        )
+        left.append(blocks(left_ref[:, at], EY + 2))
+        right.append(blocks(right_ref[:, at], EY + 2))
+    return joined_x(middle, left, right)
 
 
 def inner_rows(cols):
     return jnp.concatenate([col[1:-1, 1:-1].reshape(ROWS, 128) for col in cols], 1)
 
 
-def smoothed_of(cols, pair, shape, rows):
-    wide = jnp.concatenate([col.reshape(-1, 128) for col in cols], 1)
-    scale = 1.0 / (pair[:, 0:1] * rows[0:1] + pair[:, 1:2])
-    table = shape[...]
-    modes = product(wide, table) * scale
-    back = product(modes, table, 1)
-    return assemble_wide([blocks(col, EY + 2) for col in columns(back)])
+def smoothed_of(cols, scale, shape):
+    halves_of = fold([col.reshape(-1, 128) for col in cols])
+    back = []
+    for at, half in enumerate(halves_of):
+        table = part_of(shape, at)
+        modes = product(half, table) * scale[:, 256 * at : 256 * at + 256]
+        back.append(product(modes, table, 1))
+    return assemble_wide([blocks(col, EY + 2) for col in unfold(*back)])
 
 
 def stiffness_of(field, pair, stiff, rows):
-    return product(field, stiff[...]) * pair[:, 0:1] + field * (rows[1:2] * pair[:, 1:2])
+    halves_of = fold(columns(field))
+    done = [product(half, part_of(stiff, at)) for at, half in enumerate(halves_of)]
+    stiffened = jnp.concatenate(unfold(*done), 1)
+    return stiffened * pair[:, 0:1] + field * (rows[1:2] * pair[:, 1:2])
 
 
 def first_kernel(
-    part_ref, left_ref, right_ref, below_ref, above_ref, pair_ref, gathered_ref, leaf_in_ref,
+    part_ref, below_ref, above_ref, left_ref, right_ref, pair_ref, gathered_ref, leaf_in_ref,
     rows_ref, shape, spread, leaf, column, top, stiff, loads,
-    source_out, search_out, wide_pair_out, out_ref, left_out_ref, right_out_ref, coeff_ref,
+    source_out, search_out, scale_out, out_ref, below_out_ref, above_out_ref, coeff_ref,
     leaf_out_ref,
 ):
     rows = rows_ref[...]
     weight = weight_of(rows[2:3])
-    field = wide_field(part_ref, left_ref, right_ref, below_ref, above_ref)
+    field = wide_field(part_ref, below_ref, above_ref, left_ref, right_ref)
     source = inner_rows(field)
     source_out[...] = source
     own = pair_ref[...]
     at = slice(NODES, NODES + 128)
-    wide_pair = jnp.concatenate([blocks(left_ref[:, at]), blocks(own), blocks(right_ref[:, at])], 0)
     wide_pair = jnp.concatenate(
-        [blocks(below_ref[:, at], 1), wide_pair, blocks(above_ref[:, at], 1)], 1
+        [blocks(below_ref[:, at], 1), blocks(own), blocks(above_ref[:, at], 1)], 1
     ).reshape(-1, 128)
-    wide_pair_out[...] = wide_pair
+    wide_pair = jnp.concatenate([left_ref[:, at], wide_pair, right_ref[:, at]], 0)
     coeffs = jnp.sum(gathered_ref[...], axis=0)
-    smoothed = smoothed_of(field, wide_pair, shape, rows)
+    scale = 1.0 / (wide_pair[:, 0:1] * rows[0:1] + wide_pair[:, 1:2])
+    scale_out[...] = scale
+    smoothed = smoothed_of(field, scale, shape)
     search = jnp.concatenate(smoothed, 1) * weight + coarse_of(
         coeffs, leaf_in_ref[...], spread[...], leaf, column, top
     )
     search_out[...] = search
     image = stiffness_of(search, own, stiff, rows)
-    write_planes(assemble_inside(columns(image)), out_ref, left_out_ref, right_out_ref)
+    write_planes(assemble_inside(columns(image)), out_ref, below_out_ref, above_out_ref)
     numbers = numbers_row(
         [total_of(source * source * weight), total_of(image * source), total_of(image * image)]
     )
@@ -503,9 +553,9 @@
 
 
 def second_kernel(
-    part_ref, left_ref, right_ref, below_ref, above_ref, pair_ref, gathered_ref, leaf_in_ref,
-    rows_ref, wide_pair, shape, spread, leaf, column, top, search, source, stiff,
-    image_out, second_out, out_ref, face_left_ref, face_right_ref, face_y_ref, sums_ref, total_ref,
+    part_ref, below_ref, above_ref, left_ref, right_ref, pair_ref, gathered_ref, leaf_in_ref,
+    rows_ref, smoother_scale, shape, spread, leaf, column, top, search, source, stiff,
+    image_out, second_out, out_ref, face_left_ref, face_right_ref, face_low_ref, face_high_ref, sums_ref, total_ref,
 ):
     rows = rows_ref[...]
     weight = weight_of(rows[2:3])
@@ -514,10 +564,10 @@
     norm, along, size = coeffs[1:2, 0:1], coeffs[1:2, 1:2], coeffs[1:2, 2:3]
     overlap = along / norm
     scale = 1.0 / jnp.sqrt(size)
-    field = wide_field(part_ref, left_ref, right_ref, below_ref, above_ref)
+    field = wide_field(part_ref, below_ref, above_ref, left_ref, right_ref)
     first = inner_rows(field)
     image_out[...] = first
-    smoothed = smoothed_of(field, wide_pair[...], shape, rows)
+    smoothed = smoothed_of(field, smoother_scale[...], shape)
     whole = jnp.concatenate(smoothed, 1) * weight + coarse_of(
         coeffs, leaf_in_ref[...], spread[...], leaf, column, top
     )
@@ -525,10 +575,10 @@
     second_out[...] = second
     source = source[...]
     image = stiffness_of(second, pair_ref[...], stiff, rows)
-    write_faces(assemble_inside(columns(image)), out_ref, face_left_ref, face_right_ref, face_y_ref)
+    write_faces(assemble_inside(columns(image)), out_ref, face_left_ref, face_right_ref, face_low_ref, face_high_ref)
     basis = (first - overlap * source) * scale
     sums_ref[...] = numbers_row(
-        [total_of(basis * basis * weight), total_of(image * source), total_of(image * basis)], 128
+        [total_of(basis * basis * weight), total_of(image * source), total_of(image * basis)], 128, NP
     )
 
 
@@ -541,19 +591,50 @@
     part_ref, before_x_ref, after_x_ref, before_y_ref, after_y_ref, sums_in_ref, rows,
     image_ref, sums_ref,
 ):
-    image = finish(part_ref, before_x_ref, after_x_ref, before_y_ref, after_y_ref)
-    image_ref[...] = image
-    square = total_of(image * image * weight_of(rows[2:3]))
-    sums = jnp.where(lanes() == 3, square, sums_in_ref[...])
-    sums_ref[...] = jnp.broadcast_to(sums, sums_ref.shape)
+    lane = lanes()
+    weight = columns(weight_of(rows[2:3]))
+    row = lax.broadcasted_iota(jnp.int32, (ROWS, 1), 0)
+    at_y = row // EZ % EY
+    row_y = lane // NP % NP
+    face_y = ((row_y == 0) & (at_y == 0)) | ((row_y == NP - 1) & (at_y == EY - 1))
+    face_x = {0: (lane < 64) & (row < 64), 3: (lane >= 64) & (row >= 192)}
+    square = jnp.zeros((ROWS, 128), F32)
+    fields = faces_added(part_ref, before_x_ref, after_x_ref, before_y_ref, after_y_ref)
+    for c, (own, over_x, over_y) in enumerate(zip(*fields)):
+        image = own + over_x + over_y
+        image_ref[:, 128 * c : 128 * c + 128] = image
+        term = image * image
+        if c in face_x:
+            both = 4.0 * (own + over_x) * (own + over_y)
+            term = jnp.where(face_x[c] & face_y, both, term)
+        square = square + term * weight[c]
+    sums = jnp.where(lane == 4 * NP - 1, total_of(square), sums_in_ref[...])
+    device = lax.broadcasted_iota(jnp.int32, (sums_ref.shape[0], 1), 0)
+    sent = jnp.zeros(sums_ref.shape, F32)
+    for side_x, side_y, first_row, block, first in EDGES:
+        edge = edge_out(part_ref, first_row, block, first)
+        sent = jnp.where(device == diagonal_of(side_x, side_y), edge, sent)
+    sums_ref[...] = jnp.where(is_number(lane), sums, sent)
 
 
 def end_kernel(
     sums_ref, coeff_ref, image_two_ref, order, search_one, search_two, source, image_one,
     pressure_out, residual_out,
 ):
-    sums = jnp.sum(sums_ref[...], axis=0, keepdims=True)
-    squared, dot_source, dot_basis, dot_self = (sums[:, at : at + 1] for at in range(4))
+    got = sums_ref[...]
+    sums = jnp.sum(got, axis=0, keepdims=True)
+    squared, dot_source, dot_basis, dot_self = (
+        sums[:, NP * at + NP - 1 : NP * at + NP] for at in range(4)
+    )
+    device = lax.broadcasted_iota(jnp.int32, (got.shape[0], 1), 0)
+    image_two = columns(image_two_ref[...])
+    for side_x, side_y, first_row, block, first in EDGES:
+        line = jnp.where(device == diagonal_of(side_x, side_y), got, 0.0)
+        edge = edge_in(jnp.sum(line, axis=0, keepdims=True), first)
+        above, below = jnp.zeros((first_row, 128), F32), jnp.zeros((ROWS - EZ - first_row, 128), F32)
+        parts = [part for part in (above, edge, below) if part.shape[0]]
+        image_two[block] = image_two[block] + jnp.concatenate(parts, 0)
+    image_two = jnp.concatenate(image_two, 1)
     coeffs = coeff_ref[...]
     norm, along, size = coeffs[1:2, 0:1], coeffs[1:2, 1:2], coeffs[1:2, 2:3]
     beta = jnp.sqrt(norm)
@@ -581,7 +662,7 @@
     )
     pressure_out.send()
     residual_out.ref[...] = permuted(
-        chooser, source[...] - step_one * image_one[...] - step_two * image_two_ref[...]
+        chooser, source[...] - step_one * image_one[...] - step_two * image_two
     )
     residual_out.send()
 
@@ -661,7 +742,6 @@
 GY = ("gh", "gl")
 NEAR = ("gx", "gh")
 FIELD = shaped(ROWS, NODES)
-FACES = shaped(2, 64, 128)
 FACE = shaped(64, 128)
 PAIRS = shaped(ROWS, 128)
 
@@ -673,18 +753,18 @@
     return lax.ppermute(high, axis, up), lax.ppermute(low, axis, down)
 
 
-def surrounded(part, left, right, coeffs, pair=None):
-    wide, across = left.shape[1], (EX + 2) * EZ
-    before, after = neighbours(left, right, "gx")
+def surrounded(part, low, high, coeffs, pair=None):
+    wide, across = low.shape[1], (EY + 2) * EZ
+    below, above = neighbours(low, high, GY)
     gathered = lax.all_to_all(coeffs, NEAR, 0, 0)
     more = () if pair is None else (pair,)
     low, high, spread = run(
         middle_kernel,
         (shaped(across, wide), shaped(across, wide), shaped(lax.axis_size("gl"), 4, 256)),
-        part, before, after, gathered, *more,
-    )
-    below, above = neighbours(low, high, GY)
-    return part, before, after, below, above, lax.all_to_all(spread, "gl", 0, 0)
+        part, below, above, gathered, *more,
+    )
+    left, right = neighbours(low, high, "gx")
+    return part, below, above, left, right, lax.all_to_all(spread, "gl", 0, 0)
 
 
 def per_device(
@@ -693,33 +773,29 @@
     stiff, shape, loads, spread, rows = build_tables()
     factors = [factor[0, 0] for factor in (leaf_factor, column_factor, top_factor)]
     coarse = (shaped(lax.axis_size(NEAR), 4, 256), shaped(1, 256))
-    part, left, right, coeffs, leaves, pair, order, *factors = run(
+    order = element_order[0]
+    part, low, high, coeffs, leaves, pair = run(
         start_kernel,
-        (
-            FIELD, shaped(64, NODES + 128), shaped(64, NODES + 128), *coarse, PAIRS,
-            jax.ShapeDtypeStruct((1, ROWS), jnp.int32), *(shaped(*item.shape) for item in factors),
-        ),
-        Far(element_order[0]), Far(forcing[0, 0]), Far(diffusivity[0]), Far(reaction[0]),
-        *(Far(item) for item in factors), loads,
-    )
-    *around, gathered = surrounded(part, left, right, coeffs, pair)
-    source, search_one, wide_pair, part, left, right, coeffs, leaves = run(
+        (FIELD, shaped(64, NODES + 128), shaped(64, NODES + 128), *coarse, PAIRS),
+        order, forcing[0, 0], diffusivity[0], reaction[0], *factors, loads,
+    )
+    *around, gathered = surrounded(part, low, high, coeffs, pair)
+    source, search_one, scale, part, low, high, coeffs, leaves = run(
         first_kernel,
         (
-            FIELD, FIELD, shaped((EX + 2) * (EY + 2) * EZ, 128), FIELD, shaped(64, NODES), shaped(64, NODES), *coarse,
+            FIELD, FIELD, shaped((EX + 2) * (EY + 2) * EZ, NODES), FIELD, shaped(64, NODES), shaped(64, NODES), *coarse,
         ),
         *around, pair, gathered, leaves, rows, shape, spread, *factors, stiff, loads,
     )
-    *around, gathered = surrounded(part, left, right, coeffs)
-    image_one, search_two, part, face_left, face_right, face_y, sums, coeffs = run(
+    *around, gathered = surrounded(part, low, high, coeffs)
+    image_one, search_two, part, face_left, face_right, face_low, face_high, sums, coeffs = run(
         second_kernel,
-        (FIELD, FIELD, FIELD, FACE, FACE, FACES, shaped(1, 128), shaped(4, 256)),
-        *around, pair, gathered, leaves, rows, wide_pair, shape, spread, *factors,
+        (FIELD, FIELD, FIELD, FACE, FACE, FACE, FACE, shaped(1, 128), shaped(4, 256)),
+        *around, pair, gathered, leaves, rows, scale, shape, spread, *factors,
         search_one, source, stiff,
     )
     before_x, after_x = neighbours(face_left, face_right, "gx")
-    low, high = run(edge_kernel, (FACE, FACE), face_y, before_x, after_x)
-    before_y, after_y = neighbours(low, high, GY)
+    before_y, after_y = neighbours(face_low, face_high, GY)
     peers = lax.axis_size(("gx", *GY))
     image_two, sums = run(
         last_kernel, (FIELD, shaped(peers, 128)),

time: 119 us -> 115 us (0.966)
  waiting for transfers between devices: 4.95 us -> 1.32 us
  Pallas kernels: 14 us -> 12.2 us
  blocking collectives: 73.1 us -> 74.6 us
    ppermute x12, waiting for transfers between devices: 4.95 us -> 1.32 us  [neighbours(): return (lax.ppermute(high, axis, up), lax.ppermute(low, axis, down))]
    pallas_call x8 -> x7, Pallas kernels: 14 us -> 12.2 us  [run(): pl.pallas_call(body, out_shape=tuple(outs), in_specs=[far if is_far else...]
  transfers between devices with their start and end apart: 12 -> 12, of which waited for: 3 -> 1; matrix products, arithmetic and copies ran while one was open for 0% -> 0% of each run, Pallas kernels for 0% -> 0%
where the time goes in v4:
time: 115 us
  blocking collectives  74.6 us (65%)
  starting transfers between devices  23.7 us (21%)
  Pallas kernels  12.2 us (11%)
  local copies, waits for them, and re-layouts  2.24 us (2%)
  waiting for transfers between devices  1.32 us (1%)
    all_to_all x2, blocking collectives, surrounded(): gathered = lax.all_to_all(coeffs, NEAR, 0, 0)  27.6 us
    all_to_all x1, blocking collectives, per_device(): sums = lax.all_to_all(sums, ('gx', *GY), 0, 0, tiled=True)  24.2 us
    ppermute x12, starting transfers between devices, neighbours(): return (lax.ppermute(high, axis, up), lax.ppermute(low, axis, down))  23.7 us
    all_to_all x2, blocking collectives, surrounded(): return (part, below, above, left, right, lax.all_to_all(spread, 'gl', 0, 0))  22.9 us
    pallas_call x7, Pallas kernels, run(): pl.pallas_call(body, out_shape=tuple(outs), in_specs=[far if is_far else...  12.2 us
  transfers between devices with their start and end apart: 12, of which 1 were waited for; matrix products, arithmetic and copies ran while one was open for 0% of the time, Pallas kernels for 0%

profile of v4, /device:TPU:1, one launch (start us, length us, event | category | flops | bytes accessed | tf_op | source)
XLA Modules:
  0.0 115.1 jit_solution(14429815077448094951)
XLA Ops:
  0.6 0.0 copy-start.3
  0.6 0.0 copy-start.8
  0.7 0.0 copy-start.7
  0.7 0.0 copy-start.6
  0.7 0.0 copy-start.4
  0.7 1.0 copy.21
  1.7 1.2 %copy_bitcast_fusion = (f32[425,256]{1,0:T(8,128)S(1)}, f32[425,256]{1,0:T(8,128)S(1)}) fusion(f32[1,1,425,256]{3,1,2,0:T(1,128)} %param.18, f32[1,1,425,256]{3,1,2,0:T(1,128)} %param.17), kind=kLoop, calls=%fused_computation | loop fusion | bytes 1740800
  2.9 0.0 copy-done.3
  2.9 0.0 copy-done.8
  2.9 0.0 copy-done.7
  2.9 0.0 copy-done.6
  2.9 0.0 copy-done.4
  2.9 0.0 copy-start
  2.9 0.0 copy-start.1
  3.0 0.0 copy-start.2
  3.0 0.0 copy-start.5
  3.0 1.4 %shard_map.131 = (f32[256,512]{1,0:T(8,128)S(1)}, f32[64,640]{1,0:T(8,128)S(1)}, f32[64,640]{1,0:T(8,128)S(1)}, f32[16,4,256]{2,1,0:T(4,128)S(1)}, f32[1,256]{1,0:T(1,128)S(1)}, /*index=5*/f32[256,128]{1,0:T(8,128)S(1)}) custom-call(s32[1,256]{1,0:T(1,128)S(1)} %bitcast.23, f32[256,512]{1,0:T(8,128)S(1)} %bitcast.21, f32[1,256]{1,0:T(1,128)S(1)} %bitcast.25, ...), custom_call_target="tpu_custom_call" | custom-call | tf_op jit(solution)/shard_map/pallas_call | solution.py:731
  4.4 2.5 %collective-permute-start = (f32[64,640]{1,0:T(8,128)S(1)}, f32[64,640]{1,0:T(8,128)S(1)}, u32[]{:S(2)}, u32[]{:S(2)}) collective-permute-start(f32[64,640]{1,0:T(8,128)S(1)} %get-tuple-element.36), channel_id=1, source_target_pairs={{0,1},{1,2},{2,3},{3,4},{4,5},{5,6},{6,7},{7,8},{8,9},{9,10},{10,1... | collective-permute-start | bytes 491528 | tf_op jit(solution)/shard_map/ppermute | solution.py:753
  6.9 6.5 %collective-permute-start.1 = (f32[64,640]{1,0:T(8,128)S(1)}, f32[64,640]{1,0:T(8,128)S(1)}, u32[]{:S(2)}, u32[]{:S(2)}) collective-permute-start(f32[64,640]{1,0:T(8,128)S(1)} %get-tuple-element.37), channel_id=1, source_target_pairs={{1,0},{2,1},{3,2},{4,3},{5,4},{6,5},{7,6},{8,7},{9,8},{10,9},{11,1... | collective-permute-start | bytes 491528 | tf_op jit(solution)/shard_map/ppermute | solution.py:753
  13.4 12.7 %all_to_all.31.refs_3_ = f32[16,4,256]{2,1,0:T(4,128)S(1)} all-to-all(f32[16,4,256]{2,1,0:T(4,128)S(1)} %get-tuple-element.38), channel_id=1, replica_groups=mesh['gx'=8,'gh'=2,'gl'=16] {'gx','gh'}, dimensions={0} | all-to-all | bytes 131072 | tf_op jit(solution)/shard_map/all_to_all | solution.py:759
  26.1 0.0 collective-permute-done.refs_1_
  26.1 0.0 collective-permute-done.1.refs_2_
  26.1 0.1 shard_map.132
  26.2 0.5 collective-permute-start.2
  26.7 0.0 collective-permute-start.3
  26.8 13.0 %all_to_all.32.refs_6_ = f32[16,4,256]{2,1,0:T(4,128)S(1)} all-to-all(f32[16,4,256]{2,1,0:T(4,128)S(1)} %get-tuple-element.42), channel_id=1, replica_groups=mesh['gx'=8,'gh'=2,'gl'=16] {'gl'}, dimensions={0} | all-to-all | bytes 131072 | tf_op jit(solution)/shard_map/all_to_all | solution.py:767
  39.7 0.0 collective-permute-done.2.refs_3_
  39.7 0.0 collective-permute-done.3.refs_4_
  39.7 0.0 copy-done
  39.7 0.0 copy-done.1
  39.8 0.0 copy-done.2
  39.8 0.0 copy-done.5
  39.8 4.0 %shard_map.133 = (f32[256,512]{1,0:T(8,128)S(1)}, f32[256,512]{1,0:T(8,128)S(1)}, f32[576,512]{1,0:T(8,128)S(1)}, f32[256,512]{1,0:T(8,128)S(1)}, f32[64,512]{1,...) custom-call(f32[256,512]{1,0:T(8,128)S(1)} %get-tuple-element.35.refs_0_, ...), custom_call_target="tpu_custom_call" | custom-call | tf_op jit(solution)/shard_map/pallas_call | solution.py:731
  43.8 0.8 collective-permute-start.4
  44.6 4.1 %collective-permute-start.5 = (f32[64,512]{1,0:T(8,128)S(1)}, f32[64,512]{1,0:T(8,128)S(1)}, u32[]{:S(2)}, u32[]{:S(2)}) collective-permute-start(f32[64,512]{1,0:T(8,128)S(1)} %get-tuple-element.46), channel_id=1, source_target_pairs={{1,0},{2,1},{3,2},{4,3},{5,4},{6,5},{7,6},{8,7},{9,8},{10,9},{11,1... | collective-permute-start | bytes 393224 | tf_op jit(solution)/shard_map/ppermute | solution.py:753
  48.7 14.9 %all_to_all.33.refs_3_ = f32[16,4,256]{2,1,0:T(4,128)S(1)} all-to-all(f32[16,4,256]{2,1,0:T(4,128)S(1)} %get-tuple-element.47), channel_id=1, replica_groups=mesh['gx'=8,'gh'=2,'gl'=16] {'gx','gh'}, dimensions={0} | all-to-all | bytes 131072 | tf_op jit(solution)/shard_map/all_to_all | solution.py:759
  63.5 0.0 collective-permute-done.4.refs_1_
  63.6 0.0 collective-permute-done.5.refs_2_
  63.6 0.1 shard_map.134
  63.7 0.5 collective-permute-start.6
  64.2 0.0 collective-permute-start.7
  64.2 9.9 %all_to_all.34.refs_6_ = f32[16,4,256]{2,1,0:T(4,128)S(1)} all-to-all(f32[16,4,256]{2,1,0:T(4,128)S(1)} %get-tuple-element.50), channel_id=1, replica_groups=mesh['gx'=8,'gh'=2,'gl'=16] {'gl'}, dimensions={0} | all-to-all | bytes 131072 | tf_op jit(solution)/shard_map/all_to_all | solution.py:767
  74.2 0.0 collective-permute-done.6.refs_3_
  74.2 0.0 collective-permute-done.7.refs_4_
  74.2 4.0 %shard_map.135 = (f32[256,512]{1,0:T(8,128)S(1)}, f32[256,512]{1,0:T(8,128)S(1)}, f32[256,512]{1,0:T(8,128)S(1)}, f32[64,128]{1,0:T(8,128)S(1)}, f32[64,128]{1,0...) custom-call(f32[256,512]{1,0:T(8,128)S(1)} %get-tuple-element.44.ref, ...), custom_call_target="tpu_custom_call" | custom-call | tf_op jit(solution)/shard_map/pallas_call | solution.py:731
  78.2 2.9 %collective-permute-start.8 = (f32[64,128]{1,0:T(8,128)S(1)}, f32[64,128]{1,0:T(8,128)S(1)}, u32[]{:S(2)}, u32[]{:S(2)}) collective-permute-start(f32[64,128]{1,0:T(8,128)S(1)} %get-tuple-element.56), channel_id=1, source_target_pairs={{0,32},{32,64},{64,96},{96,128},{128,160},{160,192},{192,224},{224... | collective-permute-start | bytes 98312 | tf_op jit(solution)/shard_map/ppermute | solution.py:753
  81.1 1.1 collective-permute-start.9
  82.2 0.7 collective-permute-start.10
  82.9 4.1 %collective-permute-start.11 = (f32[64,128]{1,0:T(8,128)S(1)}, f32[64,128]{1,0:T(8,128)S(1)}, u32[]{:S(2)}, u32[]{:S(2)}) collective-permute-start(f32[64,128]{1,0:T(8,128)S(1)} %get-tuple-element.59), channel_id=1, source_target_pairs={{1,0},{2,1},{3,2},{4,3},{5,4},{6,5},{7,6},{8,7},{9,8},{10,9},{11,1... | collective-permute-start | bytes 98312 | tf_op jit(solution)/shard_map/ppermute | solution.py:753
  87.0 0.0 collective-permute-done.8.refs_1_
  87.0 0.0 collective-permute-done.9.refs_2_
  87.0 1.3 %collective-permute-done.10.refs_3_ = f32[64,128]{1,0:T(8,128)S(1)} collective-permute-done((f32[64,128]{1,0:T(8,128)S(1)}, f32[64,128]{1,0:T(8,128)S(1)}, u32[]{:S(2)}, u32[]{:S(2)}) %collective-permute-start.10) | collective-permute-done | bytes 32800 | tf_op jit(solution)/shard_map/ppermute | solution.py:753
  88.3 0.0 collective-permute-done.11.refs_4_
  88.3 0.4 shard_map.136
  88.7 24.2 %all_to_all.35 = f32[256,1,128]{2,1,0:T(1,128)S(1)} all-to-all(f32[256,1,128]{2,1,0:T(1,128)S(1)} %bitcast.22), channel_id=1, replica_groups=mesh['gx'=8,'gh'=2,'gl'=16] {'gx','gh','gl'}, dimensions={0} | all-to-all | bytes 262144 | tf_op jit(solution)/shard_map/all_to_all | solution.py:804
  112.9 2.1 %shard_map.137 = (f32[256,512]{1,0:T(8,128)}, f32[256,512]{1,0:T(8,128)}) custom-call(f32[256,128]{1,0:T(8,128)S(1)} %bitcast.20, f32[4,256]{1,0:T(4,128)S(1)} %get-tuple-element.62.refs_1_, f32[256,512]{1,0:T(8,128)S(1)} %get-tuple-element.63.refs_2_, s32[1,256]{1,0:T(1,128)S(1)} %bitcast.24, f32[256,512]{1,0:T(8,128)S(1)} %get-tuple-element.53.refs_15_.refs_4_, ...), custom_call_target="tpu_custom_call" | custom-call | tf_op jit(solution)/shard_map/pallas_call | solution.py:731
Async XLA Ops:
  0.6 2.3 %copy-start.3 = (bf16[2,512,128]{2,1,0:T(8,128)(2,1)S(1)}, bf16[2,512,128]{2,1,0:T(8,128)(2,1)}, u32[]{:S(2)}) copy-start(bf16[2,512,128]{2,1,0:T(8,128)(2,1)} %constant.12.clone.refs_7_.refs_15_) | copy-start | bytes 786436
  0.6 2.3 %copy-start.8 = (f32[1,1,256]{2,1,0:T(1,128)S(1)}, f32[1,1,256]{2,1,0:T(1,128)}, u32[]{:S(2)}) copy-start(f32[1,1,256]{2,1,0:T(1,128)} %param.15) | copy-start | bytes 3076
  0.7 2.3 %copy-start.7 = (f32[1,1,256]{2,1,0:T(1,128)S(1)}, f32[1,1,256]{2,1,0:T(1,128)}, u32[]{:S(2)}) copy-start(f32[1,1,256]{2,1,0:T(1,128)} %param.14) | copy-start | bytes 3076
  0.7 2.3 %copy-start.6 = (s32[1,1,256]{2,1,0:T(1,128)S(1)}, s32[1,1,256]{2,1,0:T(1,128)}, u32[]{:S(2)}) copy-start(s32[1,1,256]{2,1,0:T(1,128)} %param.13) | copy-start | bytes 3076
  0.7 2.3 %copy-start.4 = (f32[1,1,256,512]{3,2,1,0:T(8,128)S(1)}, f32[1,1,256,512]{3,2,1,0:T(8,128)}, u32[]{:S(2)}) copy-start(f32[1,1,256,512]{3,2,1,0:T(8,128)} %param.12) | copy-start | bytes 1572868
  2.9 36.8 %copy-start = (bf16[2,2,256,256]{3,2,1,0:T(8,128)(2,1)S(1)}, bf16[2,2,256,256]{3,2,1,0:T(8,128)(2,1)}, u32[]{:S(2)}) copy-start(bf16[2,2,256,256]{3,2,1,0:T(8,128)(2,1)} %constant.11.clone.refs_9_.refs_10_) | copy-start | bytes 1572868
  2.9 36.8 %copy-start.1 = (bf16[2,2,256,256]{3,2,1,0:T(8,128)(2,1)S(1)}, bf16[2,2,256,256]{3,2,1,0:T(8,128)(2,1)}, u32[]{:S(2)}) copy-start(bf16[2,2,256,256]{3,2,1,0:T(8,128)(2,1)} %constant.10.clone.refs_14_.refs_17_) | copy-start | bytes 1572868
  3.0 36.8 %copy-start.2 = (bf16[2,128,512]{2,1,0:T(8,128)(2,1)S(1)}, bf16[2,128,512]{2,1,0:T(8,128)(2,1)}, u32[]{:S(2)}) copy-start(bf16[2,128,512]{2,1,0:T(8,128)(2,1)} %constant.13.clone.refs_10_.refs_11_) | copy-start | bytes 786436
  3.0 36.8 %copy-start.5 = (f32[8,512]{1,0:T(8,128)S(1)}, f32[8,512]{1,0:T(8,128)}, u32[]{:S(2)}) copy-start(f32[8,512]{1,0:T(8,128)} %constant.14.clone.refs_8_.refs_6_) | copy-start | bytes 49156
  4.4 21.7 %collective-permute-start = (f32[64,640]{1,0:T(8,128)S(1)}, f32[64,640]{1,0:T(8,128)S(1)}, u32[]{:S(2)}, u32[]{:S(2)}) collective-permute-start(f32[64,640]{1,0:T(8,128)S(1)} %get-tuple-element.36), channel_id=1, source_target_pairs={{0,1},{1,2},{2,3},{3,4},{4,5},{5,6},{6,7},{7,8},{8,9},{9,10},{10,1... | collective-permute-start | bytes 491528 | tf_op jit(solution)/shard_map/ppermute | solution.py:753
  6.9 19.2 %collective-permute-start.1 = (f32[64,640]{1,0:T(8,128)S(1)}, f32[64,640]{1,0:T(8,128)S(1)}, u32[]{:S(2)}, u32[]{:S(2)}) collective-permute-start(f32[64,640]{1,0:T(8,128)S(1)} %get-tuple-element.37), channel_id=1, source_target_pairs={{1,0},{2,1},{3,2},{4,3},{5,4},{6,5},{7,6},{8,7},{9,8},{10,9},{11,1... | collective-permute-start | bytes 491528 | tf_op jit(solution)/shard_map/ppermute | solution.py:753
  26.2 13.5 %collective-permute-start.2 = (f32[96,640]{1,0:T(8,128)S(1)}, f32[96,640]{1,0:T(8,128)S(1)}, u32[]{:S(2)}, u32[]{:S(2)}) collective-permute-start(f32[96,640]{1,0:T(8,128)S(1)} %get-tuple-element.40), channel_id=1, source_target_pairs={{0,32},{32,64},{64,96},{96,128},{128,160},{160,192},{192,224},{224... | collective-permute-start | bytes 737288 | tf_op jit(solution)/shard_map/ppermute | solution.py:753
  26.7 13.0 %collective-permute-start.3 = (f32[96,640]{1,0:T(8,128)S(1)}, f32[96,640]{1,0:T(8,128)S(1)}, u32[]{:S(2)}, u32[]{:S(2)}) collective-permute-start(f32[96,640]{1,0:T(8,128)S(1)} %get-tuple-element.41), channel_id=1, source_target_pairs={{32,0},{64,32},{96,64},{128,96},{160,128},{192,160},{224,192},{0,2... | collective-permute-start | bytes 737288 | tf_op jit(solution)/shard_map/ppermute | solution.py:753
  43.8 19.7 %collective-permute-start.4 = (f32[64,512]{1,0:T(8,128)S(1)}, f32[64,512]{1,0:T(8,128)S(1)}, u32[]{:S(2)}, u32[]{:S(2)}) collective-permute-start(f32[64,512]{1,0:T(8,128)S(1)} %get-tuple-element.45), channel_id=1, source_target_pairs={{0,1},{1,2},{2,3},{3,4},{4,5},{5,6},{6,7},{7,8},{8,9},{9,10},{10,1... | collective-permute-start | bytes 393224 | tf_op jit(solution)/shard_map/ppermute | solution.py:753
  44.6 18.9 %collective-permute-start.5 = (f32[64,512]{1,0:T(8,128)S(1)}, f32[64,512]{1,0:T(8,128)S(1)}, u32[]{:S(2)}, u32[]{:S(2)}) collective-permute-start(f32[64,512]{1,0:T(8,128)S(1)} %get-tuple-element.46), channel_id=1, source_target_pairs={{1,0},{2,1},{3,2},{4,3},{5,4},{6,5},{7,6},{8,7},{9,8},{10,9},{11,1... | collective-permute-start | bytes 393224 | tf_op jit(solution)/shard_map/ppermute | solution.py:753
  63.7 10.5 %collective-permute-start.6 = (f32[96,512]{1,0:T(8,128)S(1)}, f32[96,512]{1,0:T(8,128)S(1)}, u32[]{:S(2)}, u32[]{:S(2)}) collective-permute-start(f32[96,512]{1,0:T(8,128)S(1)} %get-tuple-element.48), channel_id=1, source_target_pairs={{0,32},{32,64},{64,96},{96,128},{128,160},{160,192},{192,224},{224... | collective-permute-start | bytes 589832 | tf_op jit(solution)/shard_map/ppermute | solution.py:753
  64.2 10.0 %collective-permute-start.7 = (f32[96,512]{1,0:T(8,128)S(1)}, f32[96,512]{1,0:T(8,128)S(1)}, u32[]{:S(2)}, u32[]{:S(2)}) collective-permute-start(f32[96,512]{1,0:T(8,128)S(1)} %get-tuple-element.49), channel_id=1, source_target_pairs={{32,0},{64,32},{96,64},{128,96},{160,128},{192,160},{224,192},{0,2... | collective-permute-start | bytes 589832 | tf_op jit(solution)/shard_map/ppermute | solution.py:753
  78.2 8.8 %collective-permute-start.8 = (f32[64,128]{1,0:T(8,128)S(1)}, f32[64,128]{1,0:T(8,128)S(1)}, u32[]{:S(2)}, u32[]{:S(2)}) collective-permute-start(f32[64,128]{1,0:T(8,128)S(1)} %get-tuple-element.56), channel_id=1, source_target_pairs={{0,32},{32,64},{64,96},{96,128},{128,160},{160,192},{192,224},{224... | collective-permute-start | bytes 98312 | tf_op jit(solution)/shard_map/ppermute | solution.py:753
  81.1 5.9 %collective-permute-start.9 = (f32[64,128]{1,0:T(8,128)S(1)}, f32[64,128]{1,0:T(8,128)S(1)}, u32[]{:S(2)}, u32[]{:S(2)}) collective-permute-start(f32[64,128]{1,0:T(8,128)S(1)} %get-tuple-element.57), channel_id=1, source_target_pairs={{32,0},{64,32},{96,64},{128,96},{160,128},{192,160},{224,192},{0,2... | collective-permute-start | bytes 98312 | tf_op jit(solution)/shard_map/ppermute | solution.py:753
  82.2 6.1 %collective-permute-start.10 = (f32[64,128]{1,0:T(8,128)S(1)}, f32[64,128]{1,0:T(8,128)S(1)}, u32[]{:S(2)}, u32[]{:S(2)}) collective-permute-start(f32[64,128]{1,0:T(8,128)S(1)} %get-tuple-element.58), channel_id=1, source_target_pairs={{0,1},{1,2},{2,3},{3,4},{4,5},{5,6},{6,7},{7,8},{8,9},{9,10},{10,1... | collective-permute-start | bytes 98312 | tf_op jit(solution)/shard_map/ppermute | solution.py:753
  82.9 5.4 %collective-permute-start.11 = (f32[64,128]{1,0:T(8,128)S(1)}, f32[64,128]{1,0:T(8,128)S(1)}, u32[]{:S(2)}, u32[]{:S(2)}) collective-permute-start(f32[64,128]{1,0:T(8,128)S(1)} %get-tuple-element.59), channel_id=1, source_target_pairs={{1,0},{2,1},{3,2},{4,3},{5,4},{6,5},{7,6},{8,7},{9,8},{10,9},{11,1... | collective-permute-start | bytes 98312 | tf_op jit(solution)/shard_map/ppermute | solution.py:753

commit v5 on v4

--- a/solution.py
+++ b/solution.py
@@ -274,12 +274,34 @@
     ]
 
 
+def is_even(axis):
+    return lax.rem(lax.axis_index("gx" if axis == "gx" else "gl"), 2) == 0
+
+
+def write_sides(axis, first_ref, second_ref, at, low, high):
+    even = is_even(axis)
+    first_ref[at] = jnp.where(even, high, low)
+    second_ref[at] = jnp.where(even, low, high)
+
+
+class Side:
+    def __init__(self, axis, even_ref, odd_ref):
+        self.even, self.refs = is_even(axis), (even_ref, odd_ref)
+        self.shape = even_ref.shape
+
+    def __getitem__(self, at):
+        return jnp.where(self.even, self.refs[0][at], self.refs[1][at])
+
+
+def sides_of(axis, first_ref, second_ref):
+    return Side(axis, second_ref, first_ref), Side(axis, first_ref, second_ref)
+
+
 def write_faces(cols, part_ref, face_left_ref, face_right_ref, face_low_ref, face_high_ref):
     row_y = lanes() // NP % NP
     for c in range(4):
         part_ref[:, 128 * c : 128 * c + 128] = cols[c]
-    face_left_ref[...] = cols[0][:64]
-    face_right_ref[...] = cols[3][192:]
+    write_sides("gx", face_left_ref, face_right_ref, ..., cols[0][:64], cols[3][192:])
     low = jnp.zeros((64, 128), F32)
     high = jnp.zeros((64, 128), F32)
     for c in range(4):
@@ -288,16 +310,19 @@
         last = jnp.where(row_y == NP - 1, split[:, EY - 1].reshape(64, 128), 0.0)
         low = low + (pltpu.roll(first, 8 * c, 1) if c else first)
         high = high + pltpu.roll(last, (72 + 8 * c) % 128, 1)
-    face_low_ref[...] = low
-    face_high_ref[...] = high
+    write_sides("gy", face_low_ref, face_high_ref, ..., low, high)
 
 
 def write_planes(cols, part_ref, below_ref, above_ref):
     for c in range(4):
         at = slice(128 * c, 128 * c + 128)
         part_ref[:, at] = cols[c]
-        below_ref[:, at] = blocks(cols[c])[:, 0].reshape(64, 128)
-        above_ref[:, at] = blocks(cols[c])[:, EY - 1].reshape(64, 128)
+        write_plane_pair(cols[c], below_ref, above_ref, at)
+
+
+def write_plane_pair(col, first_ref, second_ref, at):
+    low, high = blocks(col)[:, 0].reshape(64, 128), blocks(col)[:, EY - 1].reshape(64, 128)
+    write_sides("gy", first_ref, second_ref, (slice(None), at), low, high)
 
 
 def faces_added(part_ref, before_x_ref, after_x_ref, before_y_ref, after_y_ref):
@@ -448,8 +473,7 @@
     reacting = jnp.sum(chooser * reaction_ref[...], axis=1, keepdims=True)
     pair = jnp.where(lanes() == 0, diffusion, reacting)
     pair_ref[...] = pair
-    below_ref[:, NODES:] = blocks(pair)[:, 0].reshape(64, 128)
-    above_ref[:, NODES:] = blocks(pair)[:, EY - 1].reshape(64, 128)
+    write_plane_pair(pair, below_ref, above_ref, slice(NODES, NODES + 128))
     source = permuted(chooser.astype(BF16), forcing_ref[...])
     write_planes(assemble_inside(columns(source)), part_ref, below_ref, above_ref)
     loads_of(
@@ -466,6 +490,7 @@
 
 
 def middle_kernel(part_ref, below_ref, above_ref, gathered_ref, *refs):
+    below_ref, above_ref = sides_of("gy", below_ref, above_ref)
     with_pair = len(refs) == 4
     low_ref, high_ref, spread_ref = refs[-3:]
     row = lax.broadcasted_iota(jnp.int32, (4, 1), 0)
@@ -475,15 +500,16 @@
     mine = jnp.sum(jnp.where(source == me, gathered, 0.0), axis=0)
     coeffs = jnp.where(row < 2, jnp.sum(gathered, axis=0), mine)
     spread_ref[...] = jnp.broadcast_to(coeffs[None], spread_ref.shape)
-    for plane, out_ref in ((0, low_ref), (EX - 1, high_ref)):
-        for c in range(4):
+    for c in range(4 + with_pair):
+        found = []
+        for plane in (0, EX - 1):
             sides = got_plane(below_ref, c, plane), got_plane(above_ref, c, plane)
-            col = joined_y(own_plane(part_ref, c, plane), *sides)
-            out_ref[:, 128 * c : 128 * c + 128] = col.reshape(-1, 128)
-        if with_pair:
-            sides = [got_plane(below_ref, 4, plane), own_plane(refs[0], 0, plane)]
-            sides.append(got_plane(above_ref, 4, plane))
-            out_ref[:, NODES:] = jnp.concatenate(sides, 1).reshape(-1, 128)
+            if c < 4:
+                col = joined_y(own_plane(part_ref, c, plane), *sides)
+            else:
+                col = jnp.concatenate([sides[0], own_plane(refs[0], 0, plane), sides[1]], 1)
+            found.append(col.reshape(-1, 128))
+        write_sides("gx", low_ref, high_ref, (slice(None), slice(128 * c, 128 * c + 128)), *found)
 
 
 def wide_field(part_ref, below_ref, above_ref, left_ref, right_ref):
@@ -527,6 +553,8 @@
 ):
     rows = rows_ref[...]
     weight = weight_of(rows[2:3])
+    below_ref, above_ref = sides_of("gy", below_ref, above_ref)
+    left_ref, right_ref = sides_of("gx", left_ref, right_ref)
     field = wide_field(part_ref, below_ref, above_ref, left_ref, right_ref)
     source = inner_rows(field)
     source_out[...] = source
@@ -564,6 +592,8 @@
     norm, along, size = coeffs[1:2, 0:1], coeffs[1:2, 1:2], coeffs[1:2, 2:3]
     overlap = along / norm
     scale = 1.0 / jnp.sqrt(size)
+    below_ref, above_ref = sides_of("gy", below_ref, above_ref)
+    left_ref, right_ref = sides_of("gx", left_ref, right_ref)
     field = wide_field(part_ref, below_ref, above_ref, left_ref, right_ref)
     first = inner_rows(field)
     image_out[...] = first
@@ -588,7 +618,7 @@
 
 
 def last_kernel(
-    part_ref, before_x_ref, after_x_ref, before_y_ref, after_y_ref, sums_in_ref, rows,
+    part_ref, after_y_ref, before_y_ref, after_x_ref, before_x_ref, sums_in_ref, rows,
     image_ref, sums_ref,
 ):
     lane = lanes()
@@ -599,6 +629,8 @@
     face_y = ((row_y == 0) & (at_y == 0)) | ((row_y == NP - 1) & (at_y == EY - 1))
     face_x = {0: (lane < 64) & (row < 64), 3: (lane >= 64) & (row >= 192)}
     square = jnp.zeros((ROWS, 128), F32)
+    before_x_ref, after_x_ref = sides_of("gx", before_x_ref, after_x_ref)
+    before_y_ref, after_y_ref = sides_of("gy", before_y_ref, after_y_ref)
     fields = faces_added(part_ref, before_x_ref, after_x_ref, before_y_ref, after_y_ref)
     for c, (own, over_x, over_y) in enumerate(zip(*fields)):
         image = own + over_x + over_y
@@ -746,11 +778,11 @@
 PAIRS = shaped(ROWS, 128)
 
 
-def neighbours(low, high, axis):
+def neighbours(first, second, axis):
     peers = lax.axis_size(axis)
-    up = [(i, (i + 1) % peers) for i in range(peers)]
-    down = [(j, i) for i, j in up]
-    return lax.ppermute(high, axis, up), lax.ppermute(low, axis, down)
+    pairs = [(i, i ^ 1) for i in range(peers)]
+    others = [(i, (i + 2 * (i % 2) - 1) % peers) for i in range(peers)]
+    return lax.ppermute(first, axis, pairs), lax.ppermute(second, axis, others)
 
 
 def surrounded(part, low, high, coeffs, pair=None):
@@ -799,7 +831,7 @@
     peers = lax.axis_size(("gx", *GY))
     image_two, sums = run(
         last_kernel, (FIELD, shaped(peers, 128)),
-        part, before_x, after_x, before_y, after_y, sums, rows,
+        part, after_y, before_y, after_x, before_x, sums, rows,
     )
     sums = lax.all_to_all(sums, ("gx", *GY), 0, 0, tiled=True)
     pressure, residual = run(

time: 115 us -> 106 us (0.922)
  starting transfers between devices: 23.7 us -> 16.8 us
  blocking collectives: 74.6 us -> 72.1 us
    ppermute x12, starting transfers between devices: 23.7 us -> 16.8 us  [the longest x6 12.4 us: neighbours(): lax.ppermute(second, axis, others)]
    all_to_all x1, blocking collectives: 24.2 us -> 22.3 us  [per_device(): sums = lax.all_to_all(sums, ('gx', *GY), 0, 0, tiled=True)]
where the time goes in v5:
time: 106 us
  blocking collectives  72.1 us (68%)
  starting transfers between devices  16.8 us (16%)
  Pallas kernels  12.2 us (12%)
  local copies, waits for them, and re-layouts  2.24 us (2%)
  waiting for transfers between devices  1.68 us (2%)
    all_to_all x2, blocking collectives, surrounded(): gathered = lax.all_to_all(coeffs, NEAR, 0, 0)  27.6 us
    all_to_all x1, blocking collectives, per_device(): sums = lax.all_to_all(sums, ('gx', *GY), 0, 0, tiled=True)  22.3 us
    all_to_all x2, blocking collectives, surrounded(): return (part, below, above, left, right, lax.all_to_all(spread, 'gl', 0, 0))  22.2 us
    ppermute x6, starting transfers between devices, neighbours(): lax.ppermute(second, axis, others)  12.4 us
    pallas_call x7, Pallas kernels, run(): pl.pallas_call(body, out_shape=tuple(outs), in_specs=[far if is_far else...  12.2 us
    ppermute x6, starting transfers between devices, neighbours(): lax.ppermute(first, axis, pairs)  4.35 us
    unnamed x20, local copies, waits for them, and re-layouts  2.24 us
  transfers between devices with their start and end apart: 12, of which 1 were waited for; matrix products, arithmetic and copies ran while one was open for 0% of the time, Pallas kernels for 0%

profile of v5, /device:TPU:1, one launch (start us, length us, event | category | flops | bytes accessed | tf_op | source)
XLA Modules:
  0.0 106.0 jit_solution(4291950514526371290)
XLA Ops:
  0.6 0.0 copy-start.3
  0.6 0.0 copy-start.8
  0.7 0.0 copy-start.7
  0.7 0.0 copy-start.6
  0.7 0.0 copy-start.4
  0.7 1.0 copy.21
  1.7 1.2 %copy_bitcast_fusion = (f32[425,256]{1,0:T(8,128)S(1)}, f32[425,256]{1,0:T(8,128)S(1)}) fusion(f32[1,1,425,256]{3,1,2,0:T(1,128)} %param.18, f32[1,1,425,256]{3,1,2,0:T(1,128)} %param.17), kind=kLoop, calls=%fused_computation | loop fusion | bytes 1740800
  2.9 0.0 copy-done.3
  2.9 0.0 copy-done.8
  2.9 0.0 copy-done.7
  2.9 0.0 copy-done.6
  2.9 0.0 copy-done.4
  2.9 0.0 copy-start
  2.9 0.0 copy-start.1
  3.0 0.0 copy-start.2
  3.0 0.0 copy-start.5
  3.0 1.4 %shard_map.131 = (f32[256,512]{1,0:T(8,128)S(1)}, f32[64,640]{1,0:T(8,128)S(1)}, f32[64,640]{1,0:T(8,128)S(1)}, f32[16,4,256]{2,1,0:T(4,128)S(1)}, f32[1,256]{1,0:T(1,128)S(1)}, /*index=5*/f32[256,128]{1,0:T(8,128)S(1)}) custom-call(s32[1,256]{1,0:T(1,128)S(1)} %bitcast.23, f32[256,512]{1,0:T(8,128)S(1)} %bitcast.21, f32[1,256]{1,0:T(1,128)S(1)} %bitcast.25, ...), custom_call_target="tpu_custom_call" | custom-call | tf_op jit(solution)/shard_map/pallas_call | solution.py:763
  4.4 2.6 %collective-permute-start = (f32[64,640]{1,0:T(8,128)S(1)}, f32[64,640]{1,0:T(8,128)S(1)}, u32[]{:S(2)}, u32[]{:S(2)}) collective-permute-start(f32[64,640]{1,0:T(8,128)S(1)} %get-tuple-element.36), channel_id=1, source_target_pairs={{0,1},{1,0},{2,3},{3,2},{4,5},{5,4},{6,7},{7,6},{8,9},{9,8},{10,11... | collective-permute-start | bytes 491528 | tf_op jit(solution)/shard_map/ppermute | solution.py:785
  6.9 7.1 %collective-permute-start.1 = (f32[64,640]{1,0:T(8,128)S(1)}, f32[64,640]{1,0:T(8,128)S(1)}, u32[]{:S(2)}, u32[]{:S(2)}) collective-permute-start(f32[64,640]{1,0:T(8,128)S(1)} %get-tuple-element.37), channel_id=1, source_target_pairs={{0,31},{1,2},{2,1},{3,4},{4,3},{5,6},{6,5},{7,8},{8,7},{9,10},{10,... | collective-permute-start | bytes 491528 | tf_op jit(solution)/shard_map/ppermute | solution.py:785
  14.0 13.0 %all_to_all.31.refs_3_ = f32[16,4,256]{2,1,0:T(4,128)S(1)} all-to-all(f32[16,4,256]{2,1,0:T(4,128)S(1)} %get-tuple-element.38), channel_id=1, replica_groups=mesh['gx'=8,'gh'=2,'gl'=16] {'gx','gh'}, dimensions={0} | all-to-all | bytes 131072 | tf_op jit(solution)/shard_map/all_to_all | solution.py:791
  27.0 0.0 collective-permute-done.refs_1_
  27.0 0.0 collective-permute-done.1.refs_2_
  27.0 0.1 shard_map.132
  27.2 0.5 collective-permute-start.2
  27.7 0.2 collective-permute-start.3
  27.9 10.5 %all_to_all.32.refs_6_ = f32[16,4,256]{2,1,0:T(4,128)S(1)} all-to-all(f32[16,4,256]{2,1,0:T(4,128)S(1)} %get-tuple-element.42), channel_id=1, replica_groups=mesh['gx'=8,'gh'=2,'gl'=16] {'gl'}, dimensions={0} | all-to-all | bytes 131072 | tf_op jit(solution)/shard_map/all_to_all | solution.py:799
  38.4 0.0 collective-permute-done.2.refs_3_
  38.4 0.0 collective-permute-done.3.refs_4_
  38.4 0.0 copy-done
  38.4 0.0 copy-done.1
  38.4 0.0 copy-done.2
  38.4 0.0 copy-done.5
  38.4 4.0 %shard_map.133 = (f32[256,512]{1,0:T(8,128)S(1)}, f32[256,512]{1,0:T(8,128)S(1)}, f32[576,512]{1,0:T(8,128)S(1)}, f32[256,512]{1,0:T(8,128)S(1)}, f32[64,512]{1,...) custom-call(f32[256,512]{1,0:T(8,128)S(1)} %get-tuple-element.35.refs_0_, ...), custom_call_target="tpu_custom_call" | custom-call | tf_op jit(solution)/shard_map/pallas_call | solution.py:763
  42.5 0.7 collective-permute-start.4
  43.2 0.5 collective-permute-start.5
  43.7 14.6 %all_to_all.33.refs_3_ = f32[16,4,256]{2,1,0:T(4,128)S(1)} all-to-all(f32[16,4,256]{2,1,0:T(4,128)S(1)} %get-tuple-element.47), channel_id=1, replica_groups=mesh['gx'=8,'gh'=2,'gl'=16] {'gx','gh'}, dimensions={0} | all-to-all | bytes 131072 | tf_op jit(solution)/shard_map/all_to_all | solution.py:791
  58.3 0.0 collective-permute-done.4.refs_1_
  58.3 0.0 collective-permute-done.5.refs_2_
  58.3 0.1 shard_map.134
  58.4 0.5 collective-permute-start.6
  58.9 0.2 collective-permute-start.7
  59.1 11.7 %all_to_all.34.refs_6_ = f32[16,4,256]{2,1,0:T(4,128)S(1)} all-to-all(f32[16,4,256]{2,1,0:T(4,128)S(1)} %get-tuple-element.50), channel_id=1, replica_groups=mesh['gx'=8,'gh'=2,'gl'=16] {'gl'}, dimensions={0} | all-to-all | bytes 131072 | tf_op jit(solution)/shard_map/all_to_all | solution.py:799
  70.8 0.0 collective-permute-done.6.refs_3_
  70.8 0.0 collective-permute-done.7.refs_4_
  70.8 4.1 %shard_map.135 = (f32[256,512]{1,0:T(8,128)S(1)}, f32[256,512]{1,0:T(8,128)S(1)}, f32[256,512]{1,0:T(8,128)S(1)}, f32[64,128]{1,0:T(8,128)S(1)}, f32[64,128]{1,0...) custom-call(f32[256,512]{1,0:T(8,128)S(1)} %get-tuple-element.44.ref, ...), custom_call_target="tpu_custom_call" | custom-call | tf_op jit(solution)/shard_map/pallas_call | solution.py:763
  74.9 0.9 collective-permute-start.8
  75.8 0.1 collective-permute-start.9
  75.9 3.5 %collective-permute-start.10 = (f32[64,128]{1,0:T(8,128)S(1)}, f32[64,128]{1,0:T(8,128)S(1)}, u32[]{:S(2)}, u32[]{:S(2)}) collective-permute-start(f32[64,128]{1,0:T(8,128)S(1)} %get-tuple-element.58), channel_id=1, source_target_pairs={{0,224},{32,64},{64,32},{96,128},{128,96},{160,192},{192,160},{224... | collective-permute-start | bytes 98312 | tf_op jit(solution)/shard_map/ppermute | solution.py:785
  79.4 0.0 collective-permute-start.11
  79.4 1.7 %collective-permute-done.8.refs_1_ = f32[64,128]{1,0:T(8,128)S(1)} collective-permute-done((f32[64,128]{1,0:T(8,128)S(1)}, f32[64,128]{1,0:T(8,128)S(1)}, u32[]{:S(2)}, u32[]{:S(2)}) %collective-permute-start.8) | collective-permute-done | bytes 32800 | tf_op jit(solution)/shard_map/ppermute | solution.py:785
  81.1 0.0 collective-permute-done.9.refs_2_
  81.1 0.0 collective-permute-done.10.refs_3_
  81.1 0.0 collective-permute-done.11.refs_4_
  81.1 0.4 shard_map.136
  81.5 22.3 %all_to_all.35 = f32[256,1,128]{2,1,0:T(1,128)S(1)} all-to-all(f32[256,1,128]{2,1,0:T(1,128)S(1)} %bitcast.22), channel_id=1, replica_groups=mesh['gx'=8,'gh'=2,'gl'=16] {'gx','gh','gl'}, dimensions={0} | all-to-all | bytes 262144 | tf_op jit(solution)/shard_map/all_to_all | solution.py:836
  103.8 2.1 %shard_map.137 = (f32[256,512]{1,0:T(8,128)}, f32[256,512]{1,0:T(8,128)}) custom-call(f32[256,128]{1,0:T(8,128)S(1)} %bitcast.20, f32[4,256]{1,0:T(4,128)S(1)} %get-tuple-element.62.refs_1_, f32[256,512]{1,0:T(8,128)S(1)} %get-tuple-element.63.refs_2_, s32[1,256]{1,0:T(1,128)S(1)} %bitcast.24, f32[256,512]{1,0:T(8,128)S(1)} %get-tuple-element.53.refs_15_.refs_4_, ...), custom_call_target="tpu_custom_call" | custom-call | tf_op jit(solution)/shard_map/pallas_call | solution.py:763
Async XLA Ops:
  0.6 2.3 %copy-start.3 = (bf16[2,512,128]{2,1,0:T(8,128)(2,1)S(1)}, bf16[2,512,128]{2,1,0:T(8,128)(2,1)}, u32[]{:S(2)}) copy-start(bf16[2,512,128]{2,1,0:T(8,128)(2,1)} %constant.12.clone.refs_7_.refs_15_) | copy-start | bytes 786436
  0.6 2.3 %copy-start.8 = (f32[1,1,256]{2,1,0:T(1,128)S(1)}, f32[1,1,256]{2,1,0:T(1,128)}, u32[]{:S(2)}) copy-start(f32[1,1,256]{2,1,0:T(1,128)} %param.15) | copy-start | bytes 3076
  0.7 2.3 %copy-start.7 = (f32[1,1,256]{2,1,0:T(1,128)S(1)}, f32[1,1,256]{2,1,0:T(1,128)}, u32[]{:S(2)}) copy-start(f32[1,1,256]{2,1,0:T(1,128)} %param.14) | copy-start | bytes 3076
  0.7 2.3 %copy-start.6 = (s32[1,1,256]{2,1,0:T(1,128)S(1)}, s32[1,1,256]{2,1,0:T(1,128)}, u32[]{:S(2)}) copy-start(s32[1,1,256]{2,1,0:T(1,128)} %param.13) | copy-start | bytes 3076
  0.7 2.3 %copy-start.4 = (f32[1,1,256,512]{3,2,1,0:T(8,128)S(1)}, f32[1,1,256,512]{3,2,1,0:T(8,128)}, u32[]{:S(2)}) copy-start(f32[1,1,256,512]{3,2,1,0:T(8,128)} %param.12) | copy-start | bytes 1572868
  2.9 35.5 %copy-start = (bf16[2,2,256,256]{3,2,1,0:T(8,128)(2,1)S(1)}, bf16[2,2,256,256]{3,2,1,0:T(8,128)(2,1)}, u32[]{:S(2)}) copy-start(bf16[2,2,256,256]{3,2,1,0:T(8,128)(2,1)} %constant.11.clone.refs_9_.refs_10_) | copy-start | bytes 1572868
  2.9 35.4 %copy-start.1 = (bf16[2,2,256,256]{3,2,1,0:T(8,128)(2,1)S(1)}, bf16[2,2,256,256]{3,2,1,0:T(8,128)(2,1)}, u32[]{:S(2)}) copy-start(bf16[2,2,256,256]{3,2,1,0:T(8,128)(2,1)} %constant.10.clone.refs_14_.refs_17_) | copy-start | bytes 1572868
  3.0 35.4 %copy-start.2 = (bf16[2,128,512]{2,1,0:T(8,128)(2,1)S(1)}, bf16[2,128,512]{2,1,0:T(8,128)(2,1)}, u32[]{:S(2)}) copy-start(bf16[2,128,512]{2,1,0:T(8,128)(2,1)} %constant.13.clone.refs_10_.refs_11_) | copy-start | bytes 786436
  3.0 35.4 %copy-start.5 = (f32[8,512]{1,0:T(8,128)S(1)}, f32[8,512]{1,0:T(8,128)}, u32[]{:S(2)}) copy-start(f32[8,512]{1,0:T(8,128)} %constant.14.clone.refs_8_.refs_6_) | copy-start | bytes 49156
  4.4 22.7 %collective-permute-start = (f32[64,640]{1,0:T(8,128)S(1)}, f32[64,640]{1,0:T(8,128)S(1)}, u32[]{:S(2)}, u32[]{:S(2)}) collective-permute-start(f32[64,640]{1,0:T(8,128)S(1)} %get-tuple-element.36), channel_id=1, source_target_pairs={{0,1},{1,0},{2,3},{3,2},{4,5},{5,4},{6,7},{7,6},{8,9},{9,8},{10,11... | collective-permute-start | bytes 491528 | tf_op jit(solution)/shard_map/ppermute | solution.py:785
  6.9 20.1 %collective-permute-start.1 = (f32[64,640]{1,0:T(8,128)S(1)}, f32[64,640]{1,0:T(8,128)S(1)}, u32[]{:S(2)}, u32[]{:S(2)}) collective-permute-start(f32[64,640]{1,0:T(8,128)S(1)} %get-tuple-element.37), channel_id=1, source_target_pairs={{0,31},{1,2},{2,1},{3,4},{4,3},{5,6},{6,5},{7,8},{8,7},{9,10},{10,... | collective-permute-start | bytes 491528 | tf_op jit(solution)/shard_map/ppermute | solution.py:785
  27.2 11.2 %collective-permute-start.2 = (f32[96,640]{1,0:T(8,128)S(1)}, f32[96,640]{1,0:T(8,128)S(1)}, u32[]{:S(2)}, u32[]{:S(2)}) collective-permute-start(f32[96,640]{1,0:T(8,128)S(1)} %get-tuple-element.40), channel_id=1, source_target_pairs={{0,32},{32,0},{64,96},{96,64},{128,160},{160,128},{192,224},{224,1... | collective-permute-start | bytes 737288 | tf_op jit(solution)/shard_map/ppermute | solution.py:785
  27.7 10.7 %collective-permute-start.3 = (f32[96,640]{1,0:T(8,128)S(1)}, f32[96,640]{1,0:T(8,128)S(1)}, u32[]{:S(2)}, u32[]{:S(2)}) collective-permute-start(f32[96,640]{1,0:T(8,128)S(1)} %get-tuple-element.41), channel_id=1, source_target_pairs={{0,224},{32,64},{64,32},{96,128},{128,96},{160,192},{192,160},{224... | collective-permute-start | bytes 737288 | tf_op jit(solution)/shard_map/ppermute | solution.py:785
  42.5 15.8 %collective-permute-start.4 = (f32[64,512]{1,0:T(8,128)S(1)}, f32[64,512]{1,0:T(8,128)S(1)}, u32[]{:S(2)}, u32[]{:S(2)}) collective-permute-start(f32[64,512]{1,0:T(8,128)S(1)} %get-tuple-element.45), channel_id=1, source_target_pairs={{0,1},{1,0},{2,3},{3,2},{4,5},{5,4},{6,7},{7,6},{8,9},{9,8},{10,11... | collective-permute-start | bytes 393224 | tf_op jit(solution)/shard_map/ppermute | solution.py:785
  43.2 15.1 %collective-permute-start.5 = (f32[64,512]{1,0:T(8,128)S(1)}, f32[64,512]{1,0:T(8,128)S(1)}, u32[]{:S(2)}, u32[]{:S(2)}) collective-permute-start(f32[64,512]{1,0:T(8,128)S(1)} %get-tuple-element.46), channel_id=1, source_target_pairs={{0,31},{1,2},{2,1},{3,4},{4,3},{5,6},{6,5},{7,8},{8,7},{9,10},{10,... | collective-permute-start | bytes 393224 | tf_op jit(solution)/shard_map/ppermute | solution.py:785
  58.4 12.4 %collective-permute-start.6 = (f32[96,512]{1,0:T(8,128)S(1)}, f32[96,512]{1,0:T(8,128)S(1)}, u32[]{:S(2)}, u32[]{:S(2)}) collective-permute-start(f32[96,512]{1,0:T(8,128)S(1)} %get-tuple-element.48), channel_id=1, source_target_pairs={{0,32},{32,0},{64,96},{96,64},{128,160},{160,128},{192,224},{224,1... | collective-permute-start | bytes 589832 | tf_op jit(solution)/shard_map/ppermute | solution.py:785
  58.9 11.9 %collective-permute-start.7 = (f32[96,512]{1,0:T(8,128)S(1)}, f32[96,512]{1,0:T(8,128)S(1)}, u32[]{:S(2)}, u32[]{:S(2)}) collective-permute-start(f32[96,512]{1,0:T(8,128)S(1)} %get-tuple-element.49), channel_id=1, source_target_pairs={{0,224},{32,64},{64,32},{96,128},{128,96},{160,192},{192,160},{224... | collective-permute-start | bytes 589832 | tf_op jit(solution)/shard_map/ppermute | solution.py:785
  74.9 6.2 %collective-permute-start.8 = (f32[64,128]{1,0:T(8,128)S(1)}, f32[64,128]{1,0:T(8,128)S(1)}, u32[]{:S(2)}, u32[]{:S(2)}) collective-permute-start(f32[64,128]{1,0:T(8,128)S(1)} %get-tuple-element.56), channel_id=1, source_target_pairs={{0,31},{1,2},{2,1},{3,4},{4,3},{5,6},{6,5},{7,8},{8,7},{9,10},{10,... | collective-permute-start | bytes 98312 | tf_op jit(solution)/shard_map/ppermute | solution.py:785
  75.8 5.3 %collective-permute-start.9 = (f32[64,128]{1,0:T(8,128)S(1)}, f32[64,128]{1,0:T(8,128)S(1)}, u32[]{:S(2)}, u32[]{:S(2)}) collective-permute-start(f32[64,128]{1,0:T(8,128)S(1)} %get-tuple-element.57), channel_id=1, source_target_pairs={{0,1},{1,0},{2,3},{3,2},{4,5},{5,4},{6,7},{7,6},{8,9},{9,8},{10,11... | collective-permute-start | bytes 98312 | tf_op jit(solution)/shard_map/ppermute | solution.py:785
  75.9 5.2 %collective-permute-start.10 = (f32[64,128]{1,0:T(8,128)S(1)}, f32[64,128]{1,0:T(8,128)S(1)}, u32[]{:S(2)}, u32[]{:S(2)}) collective-permute-start(f32[64,128]{1,0:T(8,128)S(1)} %get-tuple-element.58), channel_id=1, source_target_pairs={{0,224},{32,64},{64,32},{96,128},{128,96},{160,192},{192,160},{224... | collective-permute-start | bytes 98312 | tf_op jit(solution)/shard_map/ppermute | solution.py:785
  79.4 1.7 %collective-permute-start.11 = (f32[64,128]{1,0:T(8,128)S(1)}, f32[64,128]{1,0:T(8,128)S(1)}, u32[]{:S(2)}, u32[]{:S(2)}) collective-permute-start(f32[64,128]{1,0:T(8,128)S(1)} %get-tuple-element.59), channel_id=1, source_target_pairs={{0,32},{32,0},{64,96},{96,64},{128,160},{160,128},{192,224},{224,1... | collective-permute-start | bytes 98312 | tf_op jit(solution)/shard_map/ppermute | solution.py:785

commit v6 on v5

--- a/solution.py
+++ b/solution.py
@@ -201,6 +201,21 @@
     return jnp.where(lanes() // NP % NP == NP - 1, roll_lanes(x, 56), 0.0)
 
 
+def swap_lanes(x, step):
+    flat = x.reshape(-1, 128)
+    lane = lax.broadcasted_iota(jnp.int32, flat.shape, 1)
+    place = lane // step % NP
+    move = jnp.where(place == 0, 7 * step, jnp.where(place == NP - 1, -7 * step, 0))
+    return jnp.take_along_axis(flat, lane + move, axis=1, mode="promise_in_bounds").reshape(x.shape)
+
+
+def from_rows(before, after):
+    row_y = lanes() // NP % NP
+    return swap_lanes(
+        jnp.where(row_y == NP - 1, before, jnp.where(row_y == 0, after, 0.0)), NP
+    )
+
+
 def roll_lanes(x, shift):
     return pltpu.roll(x.reshape(-1, 128), shift, 1).reshape(x.shape)
 
@@ -209,13 +224,13 @@
     rows = col.shape[0]
     row_z = lanes() % NP
     level = lax.broadcasted_iota(jnp.int32, (rows, 1), 0) % EZ
-    up = pltpu.roll(pltpu.roll(col, 121, 1), 1, 0)
-    down = pltpu.roll(pltpu.roll(col, 7, 1), rows - 1, 0)
-    return (
-        col
-        + jnp.where((row_z == 0) & (level > 0), up, 0.0)
-        + jnp.where((row_z == NP - 1) & (level < EZ - 1), down, 0.0)
-    )
+    swapped = swap_lanes(col, 1)
+    up = pltpu.roll(swapped, 1, 0)
+    down = pltpu.roll(swapped, rows - 1, 0)
+    kept = jnp.where(
+        (row_z == 0) & (level > 0), up, jnp.where((row_z == NP - 1) & (level < EZ - 1), down, 0.0)
+    )
+    return col + kept
 
 
 def blocks(col, length=EY):
@@ -234,12 +249,9 @@
     edge = jnp.zeros((EX, 1, EZ, 128), F32)
     result = []
     for col in cols:
-        col = (
-            col
-            + jnp.concatenate([edge, first_row(col[:, : EY - 1])], 1)
-            + jnp.concatenate([last_row(col[:, 1:]), edge], 1)
-        )
-        result.append(sum_levels(col.reshape(ROWS, 128)))
+        before = jnp.concatenate([edge, col[:, : EY - 1]], 1)
+        after = jnp.concatenate([col[:, 1:], edge], 1)
+        result.append(sum_levels((col + from_rows(before, after)).reshape(ROWS, 128)))
     return result
 
 
@@ -269,7 +281,7 @@
         cols[3][1:-1] + last_plane(cols[0][2:]),
     ]
     return [
-        sum_levels((col[:, 1:-1] + first_row(col[:, :-2]) + last_row(col[:, 2:])).reshape(ROWS, 128))
+        sum_levels((col[:, 1:-1] + from_rows(col[:, :-2], col[:, 2:])).reshape(ROWS, 128))
         for col in cols
     ]
 

time: 106 us -> 106 us (level)
  no operation moved by 1% of the time
where the time goes in v6:
time: 106 us
  blocking collectives  72.1 us (68%)
  starting transfers between devices  16.8 us (16%)
  Pallas kernels  11.8 us (11%)
  local copies, waits for them, and re-layouts  2.24 us (2%)
  waiting for transfers between devices  1.67 us (2%)
    all_to_all x2, blocking collectives, surrounded(): gathered = lax.all_to_all(coeffs, NEAR, 0, 0)  27.6 us
    all_to_all x1, blocking collectives, per_device(): sums = lax.all_to_all(sums, ('gx', *GY), 0, 0, tiled=True)  22.3 us
    all_to_all x2, blocking collectives, surrounded(): return (part, below, above, left, right, lax.all_to_all(spread, 'gl', 0, 0))  22.2 us
    ppermute x6, starting transfers between devices, neighbours(): lax.ppermute(second, axis, others)  12.4 us
    pallas_call x7, Pallas kernels, run(): pl.pallas_call(body, out_shape=tuple(outs), in_specs=[far if is_far else...  11.8 us
    ppermute x6, starting transfers between devices, neighbours(): lax.ppermute(first, axis, pairs)  4.34 us
    unnamed x20, local copies, waits for them, and re-layouts  2.24 us
  transfers between devices with their start and end apart: 12, of which 1 were waited for; matrix products, arithmetic and copies ran while one was open for 0% of the time, Pallas kernels for 0%

profile of v6, /device:TPU:1, one launch (start us, length us, event | category | flops | bytes accessed | tf_op | source)
XLA Modules:
  0.0 105.6 jit_solution(8599904389061107991)
XLA Ops:
  0.6 0.0 copy-start.3
  0.6 0.0 copy-start.8
  0.7 0.0 copy-start.7
  0.7 0.0 copy-start.6
  0.7 0.0 copy-start.4
  0.7 1.0 copy.21
  1.7 1.2 %copy_bitcast_fusion = (f32[425,256]{1,0:T(8,128)S(1)}, f32[425,256]{1,0:T(8,128)S(1)}) fusion(f32[1,1,425,256]{3,1,2,0:T(1,128)} %param.18, f32[1,1,425,256]{3,1,2,0:T(1,128)} %param.17), kind=kLoop, calls=%fused_computation | loop fusion | bytes 1740800
  2.9 0.0 copy-done.3
  2.9 0.0 copy-done.8
  2.9 0.0 copy-done.7
  2.9 0.0 copy-done.6
  2.9 0.0 copy-done.4
  2.9 0.0 copy-start
  2.9 0.0 copy-start.1
  3.0 0.0 copy-start.2
  3.0 0.0 copy-start.5
  3.0 1.2 %shard_map.131 = (f32[256,512]{1,0:T(8,128)S(1)}, f32[64,640]{1,0:T(8,128)S(1)}, f32[64,640]{1,0:T(8,128)S(1)}, f32[16,4,256]{2,1,0:T(4,128)S(1)}, f32[1,256]{1,0:T(1,128)S(1)}, /*index=5*/f32[256,128]{1,0:T(8,128)S(1)}) custom-call(s32[1,256]{1,0:T(1,128)S(1)} %bitcast.23, f32[256,512]{1,0:T(8,128)S(1)} %bitcast.21, f32[1,256]{1,0:T(1,128)S(1)} %bitcast.25, ...), custom_call_target="tpu_custom_call" | custom-call | tf_op jit(solution)/shard_map/pallas_call | solution.py:775
  4.2 2.6 %collective-permute-start = (f32[64,640]{1,0:T(8,128)S(1)}, f32[64,640]{1,0:T(8,128)S(1)}, u32[]{:S(2)}, u32[]{:S(2)}) collective-permute-start(f32[64,640]{1,0:T(8,128)S(1)} %get-tuple-element.36), channel_id=1, source_target_pairs={{0,1},{1,0},{2,3},{3,2},{4,5},{5,4},{6,7},{7,6},{8,9},{9,8},{10,11... | collective-permute-start | bytes 491528 | tf_op jit(solution)/shard_map/ppermute | solution.py:797
  6.8 7.1 %collective-permute-start.1 = (f32[64,640]{1,0:T(8,128)S(1)}, f32[64,640]{1,0:T(8,128)S(1)}, u32[]{:S(2)}, u32[]{:S(2)}) collective-permute-start(f32[64,640]{1,0:T(8,128)S(1)} %get-tuple-element.37), channel_id=1, source_target_pairs={{0,31},{1,2},{2,1},{3,4},{4,3},{5,6},{6,5},{7,8},{8,7},{9,10},{10,... | collective-permute-start | bytes 491528 | tf_op jit(solution)/shard_map/ppermute | solution.py:797
  13.9 13.0 %all_to_all.31.refs_3_ = f32[16,4,256]{2,1,0:T(4,128)S(1)} all-to-all(f32[16,4,256]{2,1,0:T(4,128)S(1)} %get-tuple-element.38), channel_id=1, replica_groups=mesh['gx'=8,'gh'=2,'gl'=16] {'gx','gh'}, dimensions={0} | all-to-all | bytes 131072 | tf_op jit(solution)/shard_map/all_to_all | solution.py:803
  26.9 0.0 collective-permute-done.refs_1_
  26.9 0.0 collective-permute-done.1.refs_2_
  26.9 0.1 shard_map.132
  27.1 0.5 collective-permute-start.2
  27.5 0.2 collective-permute-start.3
  27.7 10.5 %all_to_all.32.refs_6_ = f32[16,4,256]{2,1,0:T(4,128)S(1)} all-to-all(f32[16,4,256]{2,1,0:T(4,128)S(1)} %get-tuple-element.42), channel_id=1, replica_groups=mesh['gx'=8,'gh'=2,'gl'=16] {'gl'}, dimensions={0} | all-to-all | bytes 131072 | tf_op jit(solution)/shard_map/all_to_all | solution.py:811
  38.2 0.0 collective-permute-done.2.refs_3_
  38.2 0.0 collective-permute-done.3.refs_4_
  38.2 0.0 copy-done
  38.3 0.0 copy-done.1
  38.3 0.0 copy-done.2
  38.3 0.0 copy-done.5
  38.3 3.9 %shard_map.133 = (f32[256,512]{1,0:T(8,128)S(1)}, f32[256,512]{1,0:T(8,128)S(1)}, f32[576,512]{1,0:T(8,128)S(1)}, f32[256,512]{1,0:T(8,128)S(1)}, f32[64,512]{1,...) custom-call(f32[256,512]{1,0:T(8,128)S(1)} %get-tuple-element.35.refs_0_, ...), custom_call_target="tpu_custom_call" | custom-call | tf_op jit(solution)/shard_map/pallas_call | solution.py:775
  42.2 0.7 collective-permute-start.4
  42.9 0.5 collective-permute-start.5
  43.4 14.6 %all_to_all.33.refs_3_ = f32[16,4,256]{2,1,0:T(4,128)S(1)} all-to-all(f32[16,4,256]{2,1,0:T(4,128)S(1)} %get-tuple-element.47), channel_id=1, replica_groups=mesh['gx'=8,'gh'=2,'gl'=16] {'gx','gh'}, dimensions={0} | all-to-all | bytes 131072 | tf_op jit(solution)/shard_map/all_to_all | solution.py:803
  58.0 0.0 collective-permute-done.4.refs_1_
  58.0 0.0 collective-permute-done.5.refs_2_
  58.0 0.1 shard_map.134
  58.2 0.5 collective-permute-start.6
  58.7 0.2 collective-permute-start.7
  58.9 11.7 %all_to_all.34.refs_6_ = f32[16,4,256]{2,1,0:T(4,128)S(1)} all-to-all(f32[16,4,256]{2,1,0:T(4,128)S(1)} %get-tuple-element.50), channel_id=1, replica_groups=mesh['gx'=8,'gh'=2,'gl'=16] {'gl'}, dimensions={0} | all-to-all | bytes 131072 | tf_op jit(solution)/shard_map/all_to_all | solution.py:811
  70.6 0.0 collective-permute-done.6.refs_3_
  70.6 0.0 collective-permute-done.7.refs_4_
  70.6 3.9 %shard_map.135 = (f32[256,512]{1,0:T(8,128)S(1)}, f32[256,512]{1,0:T(8,128)S(1)}, f32[256,512]{1,0:T(8,128)S(1)}, f32[64,128]{1,0:T(8,128)S(1)}, f32[64,128]{1,0...) custom-call(f32[256,512]{1,0:T(8,128)S(1)} %get-tuple-element.44.ref, ...), custom_call_target="tpu_custom_call" | custom-call | tf_op jit(solution)/shard_map/pallas_call | solution.py:775
  74.5 0.9 collective-permute-start.8
  75.3 0.1 collective-permute-start.9
  75.4 3.5 %collective-permute-start.10 = (f32[64,128]{1,0:T(8,128)S(1)}, f32[64,128]{1,0:T(8,128)S(1)}, u32[]{:S(2)}, u32[]{:S(2)}) collective-permute-start(f32[64,128]{1,0:T(8,128)S(1)} %get-tuple-element.58), channel_id=1, source_target_pairs={{0,224},{32,64},{64,32},{96,128},{128,96},{160,192},{192,160},{224... | collective-permute-start | bytes 98312 | tf_op jit(solution)/shard_map/ppermute | solution.py:797
  79.0 0.0 collective-permute-start.11
  79.0 1.6 %collective-permute-done.8.refs_1_ = f32[64,128]{1,0:T(8,128)S(1)} collective-permute-done((f32[64,128]{1,0:T(8,128)S(1)}, f32[64,128]{1,0:T(8,128)S(1)}, u32[]{:S(2)}, u32[]{:S(2)}) %collective-permute-start.8) | collective-permute-done | bytes 32800 | tf_op jit(solution)/shard_map/ppermute | solution.py:797
  80.6 0.0 collective-permute-done.9.refs_2_
  80.6 0.0 collective-permute-done.10.refs_3_
  80.6 0.0 collective-permute-done.11.refs_4_
  80.6 0.4 shard_map.136
  81.0 22.3 %all_to_all.35 = f32[256,1,128]{2,1,0:T(1,128)S(1)} all-to-all(f32[256,1,128]{2,1,0:T(1,128)S(1)} %bitcast.22), channel_id=1, replica_groups=mesh['gx'=8,'gh'=2,'gl'=16] {'gx','gh','gl'}, dimensions={0} | all-to-all | bytes 262144 | tf_op jit(solution)/shard_map/all_to_all | solution.py:848
  103.4 2.1 %shard_map.137 = (f32[256,512]{1,0:T(8,128)}, f32[256,512]{1,0:T(8,128)}) custom-call(f32[256,128]{1,0:T(8,128)S(1)} %bitcast.20, f32[4,256]{1,0:T(4,128)S(1)} %get-tuple-element.62.refs_1_, f32[256,512]{1,0:T(8,128)S(1)} %get-tuple-element.63.refs_2_, s32[1,256]{1,0:T(1,128)S(1)} %bitcast.24, f32[256,512]{1,0:T(8,128)S(1)} %get-tuple-element.53.refs_15_.refs_4_, ...), custom_call_target="tpu_custom_call" | custom-call | tf_op jit(solution)/shard_map/pallas_call | solution.py:775
Async XLA Ops:
  0.6 2.3 %copy-start.3 = (bf16[2,512,128]{2,1,0:T(8,128)(2,1)S(1)}, bf16[2,512,128]{2,1,0:T(8,128)(2,1)}, u32[]{:S(2)}) copy-start(bf16[2,512,128]{2,1,0:T(8,128)(2,1)} %constant.12.clone.refs_7_.refs_15_) | copy-start | bytes 786436
  0.6 2.3 %copy-start.8 = (f32[1,1,256]{2,1,0:T(1,128)S(1)}, f32[1,1,256]{2,1,0:T(1,128)}, u32[]{:S(2)}) copy-start(f32[1,1,256]{2,1,0:T(1,128)} %param.15) | copy-start | bytes 3076
  0.7 2.3 %copy-start.7 = (f32[1,1,256]{2,1,0:T(1,128)S(1)}, f32[1,1,256]{2,1,0:T(1,128)}, u32[]{:S(2)}) copy-start(f32[1,1,256]{2,1,0:T(1,128)} %param.14) | copy-start | bytes 3076
  0.7 2.3 %copy-start.6 = (s32[1,1,256]{2,1,0:T(1,128)S(1)}, s32[1,1,256]{2,1,0:T(1,128)}, u32[]{:S(2)}) copy-start(s32[1,1,256]{2,1,0:T(1,128)} %param.13) | copy-start | bytes 3076
  0.7 2.3 %copy-start.4 = (f32[1,1,256,512]{3,2,1,0:T(8,128)S(1)}, f32[1,1,256,512]{3,2,1,0:T(8,128)}, u32[]{:S(2)}) copy-start(f32[1,1,256,512]{3,2,1,0:T(8,128)} %param.12) | copy-start | bytes 1572868
  2.9 35.3 %copy-start = (bf16[2,2,256,256]{3,2,1,0:T(8,128)(2,1)S(1)}, bf16[2,2,256,256]{3,2,1,0:T(8,128)(2,1)}, u32[]{:S(2)}) copy-start(bf16[2,2,256,256]{3,2,1,0:T(8,128)(2,1)} %constant.11.clone.refs_9_.refs_10_) | copy-start | bytes 1572868
  2.9 35.3 %copy-start.1 = (bf16[2,2,256,256]{3,2,1,0:T(8,128)(2,1)S(1)}, bf16[2,2,256,256]{3,2,1,0:T(8,128)(2,1)}, u32[]{:S(2)}) copy-start(bf16[2,2,256,256]{3,2,1,0:T(8,128)(2,1)} %constant.10.clone.refs_14_.refs_17_) | copy-start | bytes 1572868
  3.0 35.3 %copy-start.2 = (bf16[2,128,512]{2,1,0:T(8,128)(2,1)S(1)}, bf16[2,128,512]{2,1,0:T(8,128)(2,1)}, u32[]{:S(2)}) copy-start(bf16[2,128,512]{2,1,0:T(8,128)(2,1)} %constant.13.clone.refs_10_.refs_11_) | copy-start | bytes 786436
  3.0 35.3 %copy-start.5 = (f32[8,512]{1,0:T(8,128)S(1)}, f32[8,512]{1,0:T(8,128)}, u32[]{:S(2)}) copy-start(f32[8,512]{1,0:T(8,128)} %constant.14.clone.refs_8_.refs_6_) | copy-start | bytes 49156
  4.2 22.7 %collective-permute-start = (f32[64,640]{1,0:T(8,128)S(1)}, f32[64,640]{1,0:T(8,128)S(1)}, u32[]{:S(2)}, u32[]{:S(2)}) collective-permute-start(f32[64,640]{1,0:T(8,128)S(1)} %get-tuple-element.36), channel_id=1, source_target_pairs={{0,1},{1,0},{2,3},{3,2},{4,5},{5,4},{6,7},{7,6},{8,9},{9,8},{10,11... | collective-permute-start | bytes 491528 | tf_op jit(solution)/shard_map/ppermute | solution.py:797
  6.8 20.1 %collective-permute-start.1 = (f32[64,640]{1,0:T(8,128)S(1)}, f32[64,640]{1,0:T(8,128)S(1)}, u32[]{:S(2)}, u32[]{:S(2)}) collective-permute-start(f32[64,640]{1,0:T(8,128)S(1)} %get-tuple-element.37), channel_id=1, source_target_pairs={{0,31},{1,2},{2,1},{3,4},{4,3},{5,6},{6,5},{7,8},{8,7},{9,10},{10,... | collective-permute-start | bytes 491528 | tf_op jit(solution)/shard_map/ppermute | solution.py:797
  27.1 11.2 %collective-permute-start.2 = (f32[96,640]{1,0:T(8,128)S(1)}, f32[96,640]{1,0:T(8,128)S(1)}, u32[]{:S(2)}, u32[]{:S(2)}) collective-permute-start(f32[96,640]{1,0:T(8,128)S(1)} %get-tuple-element.40), channel_id=1, source_target_pairs={{0,32},{32,0},{64,96},{96,64},{128,160},{160,128},{192,224},{224,1... | collective-permute-start | bytes 737288 | tf_op jit(solution)/shard_map/ppermute | solution.py:797
  27.5 10.7 %collective-permute-start.3 = (f32[96,640]{1,0:T(8,128)S(1)}, f32[96,640]{1,0:T(8,128)S(1)}, u32[]{:S(2)}, u32[]{:S(2)}) collective-permute-start(f32[96,640]{1,0:T(8,128)S(1)} %get-tuple-element.41), channel_id=1, source_target_pairs={{0,224},{32,64},{64,32},{96,128},{128,96},{160,192},{192,160},{224... | collective-permute-start | bytes 737288 | tf_op jit(solution)/shard_map/ppermute | solution.py:797
  42.2 15.8 %collective-permute-start.4 = (f32[64,512]{1,0:T(8,128)S(1)}, f32[64,512]{1,0:T(8,128)S(1)}, u32[]{:S(2)}, u32[]{:S(2)}) collective-permute-start(f32[64,512]{1,0:T(8,128)S(1)} %get-tuple-element.45), channel_id=1, source_target_pairs={{0,1},{1,0},{2,3},{3,2},{4,5},{5,4},{6,7},{7,6},{8,9},{9,8},{10,11... | collective-permute-start | bytes 393224 | tf_op jit(solution)/shard_map/ppermute | solution.py:797
  42.9 15.1 %collective-permute-start.5 = (f32[64,512]{1,0:T(8,128)S(1)}, f32[64,512]{1,0:T(8,128)S(1)}, u32[]{:S(2)}, u32[]{:S(2)}) collective-permute-start(f32[64,512]{1,0:T(8,128)S(1)} %get-tuple-element.46), channel_id=1, source_target_pairs={{0,31},{1,2},{2,1},{3,4},{4,3},{5,6},{6,5},{7,8},{8,7},{9,10},{10,... | collective-permute-start | bytes 393224 | tf_op jit(solution)/shard_map/ppermute | solution.py:797
  58.2 12.4 %collective-permute-start.6 = (f32[96,512]{1,0:T(8,128)S(1)}, f32[96,512]{1,0:T(8,128)S(1)}, u32[]{:S(2)}, u32[]{:S(2)}) collective-permute-start(f32[96,512]{1,0:T(8,128)S(1)} %get-tuple-element.48), channel_id=1, source_target_pairs={{0,32},{32,0},{64,96},{96,64},{128,160},{160,128},{192,224},{224,1... | collective-permute-start | bytes 589832 | tf_op jit(solution)/shard_map/ppermute | solution.py:797
  58.7 11.9 %collective-permute-start.7 = (f32[96,512]{1,0:T(8,128)S(1)}, f32[96,512]{1,0:T(8,128)S(1)}, u32[]{:S(2)}, u32[]{:S(2)}) collective-permute-start(f32[96,512]{1,0:T(8,128)S(1)} %get-tuple-element.49), channel_id=1, source_target_pairs={{0,224},{32,64},{64,32},{96,128},{128,96},{160,192},{192,160},{224... | collective-permute-start | bytes 589832 | tf_op jit(solution)/shard_map/ppermute | solution.py:797
  74.5 6.2 %collective-permute-start.8 = (f32[64,128]{1,0:T(8,128)S(1)}, f32[64,128]{1,0:T(8,128)S(1)}, u32[]{:S(2)}, u32[]{:S(2)}) collective-permute-start(f32[64,128]{1,0:T(8,128)S(1)} %get-tuple-element.56), channel_id=1, source_target_pairs={{0,31},{1,2},{2,1},{3,4},{4,3},{5,6},{6,5},{7,8},{8,7},{9,10},{10,... | collective-permute-start | bytes 98312 | tf_op jit(solution)/shard_map/ppermute | solution.py:797
  75.3 5.3 %collective-permute-start.9 = (f32[64,128]{1,0:T(8,128)S(1)}, f32[64,128]{1,0:T(8,128)S(1)}, u32[]{:S(2)}, u32[]{:S(2)}) collective-permute-start(f32[64,128]{1,0:T(8,128)S(1)} %get-tuple-element.57), channel_id=1, source_target_pairs={{0,1},{1,0},{2,3},{3,2},{4,5},{5,4},{6,7},{7,6},{8,9},{9,8},{10,11... | collective-permute-start | bytes 98312 | tf_op jit(solution)/shard_map/ppermute | solution.py:797
  75.4 5.2 %collective-permute-start.10 = (f32[64,128]{1,0:T(8,128)S(1)}, f32[64,128]{1,0:T(8,128)S(1)}, u32[]{:S(2)}, u32[]{:S(2)}) collective-permute-start(f32[64,128]{1,0:T(8,128)S(1)} %get-tuple-element.58), channel_id=1, source_target_pairs={{0,224},{32,64},{64,32},{96,128},{128,96},{160,192},{192,160},{224... | collective-permute-start | bytes 98312 | tf_op jit(solution)/shard_map/ppermute | solution.py:797
  79.0 1.7 %collective-permute-start.11 = (f32[64,128]{1,0:T(8,128)S(1)}, f32[64,128]{1,0:T(8,128)S(1)}, u32[]{:S(2)}, u32[]{:S(2)}) collective-permute-start(f32[64,128]{1,0:T(8,128)S(1)} %get-tuple-element.59), channel_id=1, source_target_pairs={{0,32},{32,0},{64,96},{96,64},{128,160},{160,128},{192,224},{224,1... | collective-permute-start | bytes 98312 | tf_op jit(solution)/shard_map/ppermute | solution.py:797

commit v7 on v6

--- a/solution.py
+++ b/solution.py
@@ -394,10 +394,18 @@
     return (lane % NP == NP - 1) & (lane < 4 * NP)
 
 
-def factor_rows(ref, at, count):
-    if at < count - 1:
-        return ref[pl.ds(LEVELS * at, 24), :]
-    return pltpu.roll(ref[pl.ds(LEVELS * count - 24, 24), :], LEVELS, 0)
+def factor_rows(ref, at):
+    return ref[24 * at : 24 * at + 24, :]
+
+
+def align_rows(ref, out_ref):
+    count = out_ref.shape[0] // 24
+    for at in range(count):
+        if at < count - 1:
+            block = ref[pl.ds(LEVELS * at, 24), :]
+        else:
+            block = pltpu.roll(ref[pl.ds(LEVELS * count - 24, 24), :], LEVELS, 0)
+        out_ref[24 * at : 24 * at + 24, :] = block
 
 
 def loads_of(unassembled, loads, leaf_ref, column_ref, top_ref, coeff_ref, leaf_out_ref, numbers):
@@ -423,11 +431,11 @@
                         total = total + jnp.where(lane // 2 == sx * 2 + sy, piece, 0.0)
             vertex = jnp.sum(total, axis=1, keepdims=True)
             at = vx * (EY + 1) + vy
-            top_sum = top_sum + factor_rows(top_ref, at, 25) * vertex
+            top_sum = top_sum + factor_rows(top_ref, at) * vertex
             if 0 < vx < EX:
-                column_sum = column_sum + factor_rows(column_ref, at, 25) * vertex
+                column_sum = column_sum + factor_rows(column_ref, at) * vertex
                 if 0 < vy < EY:
-                    leaf_sum = leaf_sum + factor_rows(leaf_ref, (vx - 1) * 3 + vy - 1, 9) * vertex
+                    leaf_sum = leaf_sum + factor_rows(leaf_ref, (vx - 1) * 3 + vy - 1) * vertex
     row = lax.broadcasted_iota(jnp.int32, (4, 1), 0)
     coeffs = jnp.where(row == 1, numbers, 0.0)
     coeffs = jnp.where(row == 0, jnp.sum(top_sum, axis=0, keepdims=True), coeffs)
@@ -443,11 +451,11 @@
     for vx in range(EX + 1):
         for vy in range(EY + 1):
             at = vx * (EY + 1) + vy
-            total = factor_rows(top_ref, at, 25) * top
+            total = factor_rows(top_ref, at) * top
             if 0 < vx < EX:
-                total = total + factor_rows(column_ref, at, 25) * column
+                total = total + factor_rows(column_ref, at) * column
                 if 0 < vy < EY:
-                    total = total + factor_rows(leaf_ref, (vx - 1) * 3 + vy - 1, 9) * leaf_coeffs
+                    total = total + factor_rows(leaf_ref, (vx - 1) * 3 + vy - 1) * leaf_coeffs
             vertex = jnp.sum(total, axis=1, keepdims=True)
             same = jnp.broadcast_to(vertex, (24, 128))
             around.append(jnp.where(lane % 2 == 0, same, pltpu.roll(same, 23, 0))[:16])
@@ -476,9 +484,13 @@
 
 
 def start_kernel(
-    order_ref, forcing_ref, diffusivity_ref, reaction_ref, leaf_ref, column_ref, top_ref, loads_ref,
-    part_ref, below_ref, above_ref, coeff_ref, leaf_out_ref, pair_ref,
+    order_ref, forcing_ref, diffusivity_ref, reaction_ref, leaf_in_ref, column_in_ref, top_in_ref,
+    loads_ref,
+    part_ref, below_ref, above_ref, coeff_ref, leaf_out_ref, pair_ref, leaf_ref, column_ref, top_ref,
 ):
+    align_rows(leaf_in_ref, leaf_ref)
+    align_rows(column_in_ref, column_ref)
+    align_rows(top_in_ref, top_ref)
     slot = lax.broadcasted_iota(jnp.int32, (ROWS, ROWS), 0)
     chooser = (order_ref[...] == slot).astype(F32)
     diffusion = jnp.sum(chooser * diffusivity_ref[...], axis=1, keepdims=True)
@@ -818,9 +830,12 @@
     factors = [factor[0, 0] for factor in (leaf_factor, column_factor, top_factor)]
     coarse = (shaped(lax.axis_size(NEAR), 4, 256), shaped(1, 256))
     order = element_order[0]
-    part, low, high, coeffs, leaves, pair = run(
+    part, low, high, coeffs, leaves, pair, *factors = run(
         start_kernel,
-        (FIELD, shaped(64, NODES + 128), shaped(64, NODES + 128), *coarse, PAIRS),
+        (
+            FIELD, shaped(64, NODES + 128), shaped(64, NODES + 128), *coarse, PAIRS,
+            *(shaped(item.shape[0] // LEVELS * 24, 256) for item in factors),
+        ),
         order, forcing[0, 0], diffusivity[0], reaction[0], *factors, loads,
     )
     *around, gathered = surrounded(part, low, high, coeffs, pair)

time: 106 us -> 106 us (level)
  no operation moved by 1% of the time
where the time goes in v7:
time: 106 us; the launch traced here: 105 us
  blocking collectives  72.1 us (68%)
  starting transfers between devices  16.8 us (16%)
  Pallas kernels  11.5 us (11%)
  local copies, waits for them, and re-layouts  2.24 us (2%)
  waiting for transfers between devices  1.68 us (2%)
    all_to_all x2, blocking collectives, surrounded(): gathered = lax.all_to_all(coeffs, NEAR, 0, 0)  27.6 us
    all_to_all x1, blocking collectives, per_device(): sums = lax.all_to_all(sums, ('gx', *GY), 0, 0, tiled=True)  22.3 us
    all_to_all x2, blocking collectives, surrounded(): return (part, below, above, left, right, lax.all_to_all(spread, 'gl', 0, 0))  22.2 us
    ppermute x6, starting transfers between devices, neighbours(): lax.ppermute(second, axis, others)  12.4 us
    pallas_call x7, Pallas kernels, run(): pl.pallas_call(body, out_shape=tuple(outs), in_specs=[far if is_far else...  11.5 us
    ppermute x6, starting transfers between devices, neighbours(): lax.ppermute(first, axis, pairs)  4.32 us
    unnamed x20, local copies, waits for them, and re-layouts  2.24 us
  transfers between devices with their start and end apart: 12, of which 1 were waited for; matrix products, arithmetic and copies ran while one was open for 0% of the time, Pallas kernels for 0%

profile of v7, /device:TPU:1, one launch (start us, length us, event | category | flops | bytes accessed | tf_op | source)
XLA Modules:
  0.0 105.3 jit_solution(16450636591123390329)
XLA Ops:
  0.6 0.0 copy-start.2
  0.6 0.0 copy-start.8
  0.7 0.0 copy-start.7
  0.7 0.0 copy-start.6
  0.7 0.0 copy-start.4
  0.7 1.0 copy.21
  1.7 1.2 %copy_bitcast_fusion = (f32[425,256]{1,0:T(8,128)S(1)}, f32[425,256]{1,0:T(8,128)S(1)}) fusion(f32[1,1,425,256]{3,1,2,0:T(1,128)} %param.18, f32[1,1,425,256]{3,1,2,0:T(1,128)} %param.17), kind=kLoop, calls=%fused_computation | loop fusion | bytes 1740800
  2.9 0.0 copy-done.2
  2.9 0.0 copy-done.8
  2.9 0.0 copy-done.7
  2.9 0.0 copy-done.6
  2.9 0.0 copy-done.4
  2.9 0.0 copy-start
  2.9 0.0 copy-start.1
  3.0 0.0 copy-start.3
  3.0 0.0 copy-start.5
  3.0 1.3 %shard_map.131 = (f32[256,512]{1,0:T(8,128)S(1)}, f32[64,640]{1,0:T(8,128)S(1)}, f32[64,640]{1,0:T(8,128)S(1)}, f32[16,4,256]{2,1,0:T(4,128)S(1)}, f32[1,256]{1,...) custom-call(s32[1,256]{1,0:T(1,128)S(1)} %bitcast.21, ...), custom_call_target="tpu_custom_call" | custom-call | tf_op jit(solution)/shard_map/pallas_call | solution.py:787
  4.3 2.5 %collective-permute-start = (f32[64,640]{1,0:T(8,128)S(1)}, f32[64,640]{1,0:T(8,128)S(1)}, u32[]{:S(2)}, u32[]{:S(2)}) collective-permute-start(f32[64,640]{1,0:T(8,128)S(1)} %get-tuple-element.39), channel_id=1, source_target_pairs={{0,1},{1,0},{2,3},{3,2},{4,5},{5,4},{6,7},{7,6},{8,9},{9,8},{10,11... | collective-permute-start | bytes 491528 | tf_op jit(solution)/shard_map/ppermute | solution.py:809
  6.8 7.1 %collective-permute-start.1 = (f32[64,640]{1,0:T(8,128)S(1)}, f32[64,640]{1,0:T(8,128)S(1)}, u32[]{:S(2)}, u32[]{:S(2)}) collective-permute-start(f32[64,640]{1,0:T(8,128)S(1)} %get-tuple-element.40), channel_id=1, source_target_pairs={{0,31},{1,2},{2,1},{3,4},{4,3},{5,6},{6,5},{7,8},{8,7},{9,10},{10,... | collective-permute-start | bytes 491528 | tf_op jit(solution)/shard_map/ppermute | solution.py:809
  13.9 13.0 %all_to_all.31.refs_3_ = f32[16,4,256]{2,1,0:T(4,128)S(1)} all-to-all(f32[16,4,256]{2,1,0:T(4,128)S(1)} %get-tuple-element.41), channel_id=1, replica_groups=mesh['gx'=8,'gh'=2,'gl'=16] {'gx','gh'}, dimensions={0} | all-to-all | bytes 131072 | tf_op jit(solution)/shard_map/all_to_all | solution.py:815
  26.9 0.0 collective-permute-done.refs_1_
  26.9 0.0 collective-permute-done.1.refs_2_
  26.9 0.1 shard_map.132
  27.1 0.5 collective-permute-start.2
  27.6 0.2 collective-permute-start.3
  27.8 10.5 %all_to_all.32.refs_6_ = f32[16,4,256]{2,1,0:T(4,128)S(1)} all-to-all(f32[16,4,256]{2,1,0:T(4,128)S(1)} %get-tuple-element.45), channel_id=1, replica_groups=mesh['gx'=8,'gh'=2,'gl'=16] {'gl'}, dimensions={0} | all-to-all | bytes 131072 | tf_op jit(solution)/shard_map/all_to_all | solution.py:823
  38.3 0.0 collective-permute-done.2.refs_3_
  38.3 0.0 collective-permute-done.3.refs_4_
  38.3 0.0 copy-done
  38.3 0.0 copy-done.1
  38.3 0.0 copy-done.3
  38.3 0.0 copy-done.5
  38.3 3.7 %shard_map.133 = (f32[256,512]{1,0:T(8,128)S(1)}, f32[256,512]{1,0:T(8,128)S(1)}, f32[576,512]{1,0:T(8,128)S(1)}, f32[256,512]{1,0:T(8,128)S(1)}, f32[64,512]{1,...) custom-call(f32[256,512]{1,0:T(8,128)S(1)} %get-tuple-element.38.refs_0_, ...), custom_call_target="tpu_custom_call" | custom-call | tf_op jit(solution)/shard_map/pallas_call | solution.py:787
  42.1 0.7 collective-permute-start.4
  42.8 0.5 collective-permute-start.5
  43.3 14.6 %all_to_all.33.refs_3_ = f32[16,4,256]{2,1,0:T(4,128)S(1)} all-to-all(f32[16,4,256]{2,1,0:T(4,128)S(1)} %get-tuple-element.53), channel_id=1, replica_groups=mesh['gx'=8,'gh'=2,'gl'=16] {'gx','gh'}, dimensions={0} | all-to-all | bytes 131072 | tf_op jit(solution)/shard_map/all_to_all | solution.py:815
  57.9 0.0 collective-permute-done.4.refs_1_
  57.9 0.0 collective-permute-done.5.refs_2_
  57.9 0.2 shard_map.134
  58.0 0.5 collective-permute-start.6
  58.5 0.2 collective-permute-start.7
  58.7 11.7 %all_to_all.34.refs_6_ = f32[16,4,256]{2,1,0:T(4,128)S(1)} all-to-all(f32[16,4,256]{2,1,0:T(4,128)S(1)} %get-tuple-element.56), channel_id=1, replica_groups=mesh['gx'=8,'gh'=2,'gl'=16] {'gl'}, dimensions={0} | all-to-all | bytes 131072 | tf_op jit(solution)/shard_map/all_to_all | solution.py:823
  70.4 0.0 collective-permute-done.6.refs_3_
  70.4 0.0 collective-permute-done.7.refs_4_
  70.4 3.7 %shard_map.135 = (f32[256,512]{1,0:T(8,128)S(1)}, f32[256,512]{1,0:T(8,128)S(1)}, f32[256,512]{1,0:T(8,128)S(1)}, f32[64,128]{1,0:T(8,128)S(1)}, f32[64,128]{1,0...) custom-call(f32[256,512]{1,0:T(8,128)S(1)} %get-tuple-element.50.ref, ...), custom_call_target="tpu_custom_call" | custom-call | tf_op jit(solution)/shard_map/pallas_call | solution.py:787
  74.1 0.9 collective-permute-start.8
  75.0 0.1 collective-permute-start.9
  75.1 3.5 %collective-permute-start.10 = (f32[64,128]{1,0:T(8,128)S(1)}, f32[64,128]{1,0:T(8,128)S(1)}, u32[]{:S(2)}, u32[]{:S(2)}) collective-permute-start(f32[64,128]{1,0:T(8,128)S(1)} %get-tuple-element.64), channel_id=1, source_target_pairs={{0,224},{32,64},{64,32},{96,128},{128,96},{160,192},{192,160},{224... | collective-permute-start | bytes 98312 | tf_op jit(solution)/shard_map/ppermute | solution.py:809
  78.6 0.0 collective-permute-start.11
  78.7 1.7 %collective-permute-done.8.refs_1_ = f32[64,128]{1,0:T(8,128)S(1)} collective-permute-done((f32[64,128]{1,0:T(8,128)S(1)}, f32[64,128]{1,0:T(8,128)S(1)}, u32[]{:S(2)}, u32[]{:S(2)}) %collective-permute-start.8) | collective-permute-done | bytes 32800 | tf_op jit(solution)/shard_map/ppermute | solution.py:809
  80.3 0.0 collective-permute-done.9.refs_2_
  80.3 0.0 collective-permute-done.10.refs_3_
  80.3 0.0 collective-permute-done.11.refs_4_
  80.3 0.4 shard_map.136
  80.7 22.3 %all_to_all.35 = f32[256,1,128]{2,1,0:T(1,128)S(1)} all-to-all(f32[256,1,128]{2,1,0:T(1,128)S(1)} %bitcast.20), channel_id=1, replica_groups=mesh['gx'=8,'gh'=2,'gl'=16] {'gx','gh','gl'}, dimensions={0} | all-to-all | bytes 262144 | tf_op jit(solution)/shard_map/all_to_all | solution.py:863
  103.0 2.1 %shard_map.137 = (f32[256,512]{1,0:T(8,128)}, f32[256,512]{1,0:T(8,128)}) custom-call(f32[256,128]{1,0:T(8,128)S(1)} %bitcast.18, f32[4,256]{1,0:T(4,128)S(1)} %get-tuple-element.68.refs_1_, f32[256,512]{1,0:T(8,128)S(1)} %get-tuple-element.69.refs_2_, s32[1,256]{1,0:T(1,128)S(1)} %bitcast.22, f32[256,512]{1,0:T(8,128)S(1)} %get-tuple-element.59.refs_15_.refs_4_, ...), custom_call_target="tpu_custom_call" | custom-call | tf_op jit(solution)/shard_map/pallas_call | solution.py:787
Async XLA Ops:
  0.6 2.3 %copy-start.2 = (bf16[2,512,128]{2,1,0:T(8,128)(2,1)S(1)}, bf16[2,512,128]{2,1,0:T(8,128)(2,1)}, u32[]{:S(2)}) copy-start(bf16[2,512,128]{2,1,0:T(8,128)(2,1)} %constant.12.clone.refs_7_.refs_15_) | copy-start | bytes 786436
  0.6 2.3 %copy-start.8 = (f32[1,1,256]{2,1,0:T(1,128)S(1)}, f32[1,1,256]{2,1,0:T(1,128)}, u32[]{:S(2)}) copy-start(f32[1,1,256]{2,1,0:T(1,128)} %param.15) | copy-start | bytes 3076
  0.7 2.3 %copy-start.7 = (f32[1,1,256]{2,1,0:T(1,128)S(1)}, f32[1,1,256]{2,1,0:T(1,128)}, u32[]{:S(2)}) copy-start(f32[1,1,256]{2,1,0:T(1,128)} %param.14) | copy-start | bytes 3076
  0.7 2.3 %copy-start.6 = (s32[1,1,256]{2,1,0:T(1,128)S(1)}, s32[1,1,256]{2,1,0:T(1,128)}, u32[]{:S(2)}) copy-start(s32[1,1,256]{2,1,0:T(1,128)} %param.13) | copy-start | bytes 3076
  0.7 2.3 %copy-start.4 = (f32[1,1,256,512]{3,2,1,0:T(8,128)S(1)}, f32[1,1,256,512]{3,2,1,0:T(8,128)}, u32[]{:S(2)}) copy-start(f32[1,1,256,512]{3,2,1,0:T(8,128)} %param.12) | copy-start | bytes 1572868
  2.9 35.3 %copy-start = (bf16[2,2,256,256]{3,2,1,0:T(8,128)(2,1)S(1)}, bf16[2,2,256,256]{3,2,1,0:T(8,128)(2,1)}, u32[]{:S(2)}) copy-start(bf16[2,2,256,256]{3,2,1,0:T(8,128)(2,1)} %constant.11.clone.refs_9_.refs_10_) | copy-start | bytes 1572868
  2.9 35.3 %copy-start.1 = (bf16[2,2,256,256]{3,2,1,0:T(8,128)(2,1)S(1)}, bf16[2,2,256,256]{3,2,1,0:T(8,128)(2,1)}, u32[]{:S(2)}) copy-start(bf16[2,2,256,256]{3,2,1,0:T(8,128)(2,1)} %constant.10.clone.refs_14_.refs_17_) | copy-start | bytes 1572868
  3.0 35.3 %copy-start.3 = (bf16[2,128,512]{2,1,0:T(8,128)(2,1)S(1)}, bf16[2,128,512]{2,1,0:T(8,128)(2,1)}, u32[]{:S(2)}) copy-start(bf16[2,128,512]{2,1,0:T(8,128)(2,1)} %constant.13.clone.refs_10_.refs_11_) | copy-start | bytes 786436
  3.0 35.3 %copy-start.5 = (f32[8,512]{1,0:T(8,128)S(1)}, f32[8,512]{1,0:T(8,128)}, u32[]{:S(2)}) copy-start(f32[8,512]{1,0:T(8,128)} %constant.14.clone.refs_8_.refs_6_) | copy-start | bytes 49156
  4.3 22.7 %collective-permute-start = (f32[64,640]{1,0:T(8,128)S(1)}, f32[64,640]{1,0:T(8,128)S(1)}, u32[]{:S(2)}, u32[]{:S(2)}) collective-permute-start(f32[64,640]{1,0:T(8,128)S(1)} %get-tuple-element.39), channel_id=1, source_target_pairs={{0,1},{1,0},{2,3},{3,2},{4,5},{5,4},{6,7},{7,6},{8,9},{9,8},{10,11... | collective-permute-start | bytes 491528 | tf_op jit(solution)/shard_map/ppermute | solution.py:809
  6.8 20.1 %collective-permute-start.1 = (f32[64,640]{1,0:T(8,128)S(1)}, f32[64,640]{1,0:T(8,128)S(1)}, u32[]{:S(2)}, u32[]{:S(2)}) collective-permute-start(f32[64,640]{1,0:T(8,128)S(1)} %get-tuple-element.40), channel_id=1, source_target_pairs={{0,31},{1,2},{2,1},{3,4},{4,3},{5,6},{6,5},{7,8},{8,7},{9,10},{10,... | collective-permute-start | bytes 491528 | tf_op jit(solution)/shard_map/ppermute | solution.py:809
  27.1 11.2 %collective-permute-start.2 = (f32[96,640]{1,0:T(8,128)S(1)}, f32[96,640]{1,0:T(8,128)S(1)}, u32[]{:S(2)}, u32[]{:S(2)}) collective-permute-start(f32[96,640]{1,0:T(8,128)S(1)} %get-tuple-element.43), channel_id=1, source_target_pairs={{0,32},{32,0},{64,96},{96,64},{128,160},{160,128},{192,224},{224,1... | collective-permute-start | bytes 737288 | tf_op jit(solution)/shard_map/ppermute | solution.py:809
  27.6 10.7 %collective-permute-start.3 = (f32[96,640]{1,0:T(8,128)S(1)}, f32[96,640]{1,0:T(8,128)S(1)}, u32[]{:S(2)}, u32[]{:S(2)}) collective-permute-start(f32[96,640]{1,0:T(8,128)S(1)} %get-tuple-element.44), channel_id=1, source_target_pairs={{0,224},{32,64},{64,32},{96,128},{128,96},{160,192},{192,160},{224... | collective-permute-start | bytes 737288 | tf_op jit(solution)/shard_map/ppermute | solution.py:809
  42.1 15.8 %collective-permute-start.4 = (f32[64,512]{1,0:T(8,128)S(1)}, f32[64,512]{1,0:T(8,128)S(1)}, u32[]{:S(2)}, u32[]{:S(2)}) collective-permute-start(f32[64,512]{1,0:T(8,128)S(1)} %get-tuple-element.51), channel_id=1, source_target_pairs={{0,1},{1,0},{2,3},{3,2},{4,5},{5,4},{6,7},{7,6},{8,9},{9,8},{10,11... | collective-permute-start | bytes 393224 | tf_op jit(solution)/shard_map/ppermute | solution.py:809
  42.8 15.1 %collective-permute-start.5 = (f32[64,512]{1,0:T(8,128)S(1)}, f32[64,512]{1,0:T(8,128)S(1)}, u32[]{:S(2)}, u32[]{:S(2)}) collective-permute-start(f32[64,512]{1,0:T(8,128)S(1)} %get-tuple-element.52), channel_id=1, source_target_pairs={{0,31},{1,2},{2,1},{3,4},{4,3},{5,6},{6,5},{7,8},{8,7},{9,10},{10,... | collective-permute-start | bytes 393224 | tf_op jit(solution)/shard_map/ppermute | solution.py:809
  58.0 12.4 %collective-permute-start.6 = (f32[96,512]{1,0:T(8,128)S(1)}, f32[96,512]{1,0:T(8,128)S(1)}, u32[]{:S(2)}, u32[]{:S(2)}) collective-permute-start(f32[96,512]{1,0:T(8,128)S(1)} %get-tuple-element.54), channel_id=1, source_target_pairs={{0,32},{32,0},{64,96},{96,64},{128,160},{160,128},{192,224},{224,1... | collective-permute-start | bytes 589832 | tf_op jit(solution)/shard_map/ppermute | solution.py:809
  58.5 11.9 %collective-permute-start.7 = (f32[96,512]{1,0:T(8,128)S(1)}, f32[96,512]{1,0:T(8,128)S(1)}, u32[]{:S(2)}, u32[]{:S(2)}) collective-permute-start(f32[96,512]{1,0:T(8,128)S(1)} %get-tuple-element.55), channel_id=1, source_target_pairs={{0,224},{32,64},{64,32},{96,128},{128,96},{160,192},{192,160},{224... | collective-permute-start | bytes 589832 | tf_op jit(solution)/shard_map/ppermute | solution.py:809
  74.1 6.2 %collective-permute-start.8 = (f32[64,128]{1,0:T(8,128)S(1)}, f32[64,128]{1,0:T(8,128)S(1)}, u32[]{:S(2)}, u32[]{:S(2)}) collective-permute-start(f32[64,128]{1,0:T(8,128)S(1)} %get-tuple-element.62), channel_id=1, source_target_pairs={{0,31},{1,2},{2,1},{3,4},{4,3},{5,6},{6,5},{7,8},{8,7},{9,10},{10,... | collective-permute-start | bytes 98312 | tf_op jit(solution)/shard_map/ppermute | solution.py:809
  75.0 5.3 %collective-permute-start.9 = (f32[64,128]{1,0:T(8,128)S(1)}, f32[64,128]{1,0:T(8,128)S(1)}, u32[]{:S(2)}, u32[]{:S(2)}) collective-permute-start(f32[64,128]{1,0:T(8,128)S(1)} %get-tuple-element.63), channel_id=1, source_target_pairs={{0,1},{1,0},{2,3},{3,2},{4,5},{5,4},{6,7},{7,6},{8,9},{9,8},{10,11... | collective-permute-start | bytes 98312 | tf_op jit(solution)/shard_map/ppermute | solution.py:809
  75.1 5.2 %collective-permute-start.10 = (f32[64,128]{1,0:T(8,128)S(1)}, f32[64,128]{1,0:T(8,128)S(1)}, u32[]{:S(2)}, u32[]{:S(2)}) collective-permute-start(f32[64,128]{1,0:T(8,128)S(1)} %get-tuple-element.64), channel_id=1, source_target_pairs={{0,224},{32,64},{64,32},{96,128},{128,96},{160,192},{192,160},{224... | collective-permute-start | bytes 98312 | tf_op jit(solution)/shard_map/ppermute | solution.py:809
  78.6 1.7 %collective-permute-start.11 = (f32[64,128]{1,0:T(8,128)S(1)}, f32[64,128]{1,0:T(8,128)S(1)}, u32[]{:S(2)}, u32[]{:S(2)}) collective-permute-start(f32[64,128]{1,0:T(8,128)S(1)} %get-tuple-element.65), channel_id=1, source_target_pairs={{0,32},{32,0},{64,96},{96,64},{128,160},{160,128},{192,224},{224,1... | collective-permute-start | bytes 98312 | tf_op jit(solution)/shard_map/ppermute | solution.py:809

commit v8 on v7

--- a/solution.py
+++ b/solution.py
@@ -713,14 +713,12 @@
     step_one = factor_one / beta
     step_two = factor_two / basis_norm
     chooser = chooser_back(order)
-    pressure_out.ref[...] = permuted(
-        chooser, step_one * search_one[...] + step_two * search_two[...]
-    )
-    pressure_out.send()
-    residual_out.ref[...] = permuted(
-        chooser, source[...] - step_one * image_one[...] - step_two * image_two
-    )
-    residual_out.send()
+    pressure = step_one * search_one[...] + step_two * search_two[...]
+    residual = source[...] - step_one * image_one[...] - step_two * image_two
+    for field, out in ((pressure, pressure_out), (residual, residual_out)):
+        for at in range(QUARTERS):
+            rows = ROWS // QUARTERS
+            out.send(at, permuted(chooser[rows * at : rows * (at + 1)], field))
 
 
 class Far:
@@ -741,11 +739,16 @@
 
 
 class Store:
-    def __init__(self, ref, target, sem):
-        self.ref, self.copy = ref, pltpu.make_async_copy(ref, target, sem)
-
-    def send(self):
-        self.copy.start()
+    def __init__(self, ref, target, sems):
+        self.ref, self.rows = ref, ref.shape[0] // QUARTERS
+        spans = [pl.ds(self.rows * at, self.rows) for at in range(QUARTERS)]
+        self.copies = [
+            pltpu.make_async_copy(ref.at[span], target.at[span], sems[at]) for at, span in enumerate(spans)
+        ]
+
+    def send(self, at, value):
+        self.ref[self.rows * at : self.rows * (at + 1)] = value
+        self.copies[at].start()
 
 
 def shaped(*shape):
@@ -768,22 +771,24 @@
         at, given, stores = 0, [], []
         for ref, is_far in zip(ins, far_in):
             if is_far:
-                ref = Fetch(ref, scratch[at], scratch[count].at[at])
+                ref = Fetch(ref, scratch[at], scratch[count].at[QUARTERS * at])
                 at += 1
             given.append(ref)
         for ref, is_far in zip(results, far_out):
             if is_far:
-                ref = Store(scratch[at], ref, scratch[count].at[at])
+                sems = [scratch[count].at[QUARTERS * at + part] for part in range(QUARTERS)]
+                ref = Store(scratch[at], ref, sems)
                 stores.append(ref)
                 at += 1
             given.append(ref)
         kernel(*given)
         for store in stores:
-            store.copy.wait()
+            for copy in store.copies:
+                copy.wait()
 
     scratch = [pltpu.VMEM(item.shape, item.dtype) for item in moved]
     if count:
-        scratch.append(pltpu.SemaphoreType.DMA((count,)))
+        scratch.append(pltpu.SemaphoreType.DMA((count * QUARTERS,)))
     return pl.pallas_call(
         body,
         out_shape=tuple(outs),
@@ -795,6 +800,7 @@
 
 
 LIMIT = 28 * 2**20
+QUARTERS = 4
 GY = ("gh", "gl")
 NEAR = ("gx", "gh")
 FIELD = shaped(ROWS, NODES)

time: 106 us -> 106 us (level)
  no operation moved by 1% of the time
where the time goes in v8:
time: 106 us
  blocking collectives  72.1 us (68%)
  starting transfers between devices  16.8 us (16%)
  Pallas kernels  12 us (11%)
  local copies, waits for them, and re-layouts  2.24 us (2%)
  waiting for transfers between devices  1.68 us (2%)
    all_to_all x2, blocking collectives, surrounded(): gathered = lax.all_to_all(coeffs, NEAR, 0, 0)  27.6 us
    all_to_all x1, blocking collectives, per_device(): sums = lax.all_to_all(sums, ('gx', *GY), 0, 0, tiled=True)  22.3 us
    all_to_all x2, blocking collectives, surrounded(): return (part, below, above, left, right, lax.all_to_all(spread, 'gl', 0, 0))  22.2 us
    ppermute x6, starting transfers between devices, neighbours(): lax.ppermute(second, axis, others)  12.4 us
    pallas_call x7, Pallas kernels, run(): pl.pallas_call(body, out_shape=tuple(outs), in_specs=[far if is_far else...  12 us
    ppermute x6, starting transfers between devices, neighbours(): lax.ppermute(first, axis, pairs)  4.32 us
    unnamed x20, local copies, waits for them, and re-layouts  2.24 us
  transfers between devices with their start and end apart: 12, of which 1 were waited for; matrix products, arithmetic and copies ran while one was open for 0% of the time, Pallas kernels for 0%

profile of v8, /device:TPU:1, one launch (start us, length us, event | category | flops | bytes accessed | tf_op | source)
XLA Modules:
  0.0 105.8 jit_solution(13073219959945730162)
XLA Ops:
  0.6 0.0 copy-start.2
  0.6 0.0 copy-start.8
  0.7 0.0 copy-start.7
  0.7 0.0 copy-start.6
  0.7 0.0 copy-start.4
  0.7 1.0 copy.21
  1.7 1.2 %copy_bitcast_fusion = (f32[425,256]{1,0:T(8,128)S(1)}, f32[425,256]{1,0:T(8,128)S(1)}) fusion(f32[1,1,425,256]{3,1,2,0:T(1,128)} %param.18, f32[1,1,425,256]{3,1,2,0:T(1,128)} %param.17), kind=kLoop, calls=%fused_computation | loop fusion | bytes 1740800
  2.9 0.0 copy-done.2
  2.9 0.0 copy-done.8
  2.9 0.0 copy-done.7
  2.9 0.0 copy-done.6
  2.9 0.0 copy-done.4
  2.9 0.0 copy-start
  2.9 0.0 copy-start.1
  3.0 0.0 copy-start.3
  3.0 0.0 copy-start.5
  3.0 1.3 %shard_map.131 = (f32[256,512]{1,0:T(8,128)S(1)}, f32[64,640]{1,0:T(8,128)S(1)}, f32[64,640]{1,0:T(8,128)S(1)}, f32[16,4,256]{2,1,0:T(4,128)S(1)}, f32[1,256]{1,...) custom-call(s32[1,256]{1,0:T(1,128)S(1)} %bitcast.21, ...), custom_call_target="tpu_custom_call" | custom-call | tf_op jit(solution)/shard_map/pallas_call | solution.py:792
  4.3 2.5 %collective-permute-start = (f32[64,640]{1,0:T(8,128)S(1)}, f32[64,640]{1,0:T(8,128)S(1)}, u32[]{:S(2)}, u32[]{:S(2)}) collective-permute-start(f32[64,640]{1,0:T(8,128)S(1)} %get-tuple-element.39), channel_id=1, source_target_pairs={{0,1},{1,0},{2,3},{3,2},{4,5},{5,4},{6,7},{7,6},{8,9},{9,8},{10,11... | collective-permute-start | bytes 491528 | tf_op jit(solution)/shard_map/ppermute | solution.py:815
  6.8 7.1 %collective-permute-start.1 = (f32[64,640]{1,0:T(8,128)S(1)}, f32[64,640]{1,0:T(8,128)S(1)}, u32[]{:S(2)}, u32[]{:S(2)}) collective-permute-start(f32[64,640]{1,0:T(8,128)S(1)} %get-tuple-element.40), channel_id=1, source_target_pairs={{0,31},{1,2},{2,1},{3,4},{4,3},{5,6},{6,5},{7,8},{8,7},{9,10},{10,... | collective-permute-start | bytes 491528 | tf_op jit(solution)/shard_map/ppermute | solution.py:815
  13.9 13.0 %all_to_all.31.refs_3_ = f32[16,4,256]{2,1,0:T(4,128)S(1)} all-to-all(f32[16,4,256]{2,1,0:T(4,128)S(1)} %get-tuple-element.41), channel_id=1, replica_groups=mesh['gx'=8,'gh'=2,'gl'=16] {'gx','gh'}, dimensions={0} | all-to-all | bytes 131072 | tf_op jit(solution)/shard_map/all_to_all | solution.py:821
  26.9 0.0 collective-permute-done.refs_1_
  26.9 0.0 collective-permute-done.1.refs_2_
  26.9 0.1 shard_map.132
  27.1 0.5 collective-permute-start.2
  27.6 0.2 collective-permute-start.3
  27.8 10.5 %all_to_all.32.refs_6_ = f32[16,4,256]{2,1,0:T(4,128)S(1)} all-to-all(f32[16,4,256]{2,1,0:T(4,128)S(1)} %get-tuple-element.45), channel_id=1, replica_groups=mesh['gx'=8,'gh'=2,'gl'=16] {'gl'}, dimensions={0} | all-to-all | bytes 131072 | tf_op jit(solution)/shard_map/all_to_all | solution.py:829
  38.3 0.0 collective-permute-done.2.refs_3_
  38.3 0.0 collective-permute-done.3.refs_4_
  38.3 0.0 copy-done
  38.3 0.0 copy-done.1
  38.3 0.0 copy-done.3
  38.3 0.0 copy-done.5
  38.3 3.7 %shard_map.133 = (f32[256,512]{1,0:T(8,128)S(1)}, f32[256,512]{1,0:T(8,128)S(1)}, f32[576,512]{1,0:T(8,128)S(1)}, f32[256,512]{1,0:T(8,128)S(1)}, f32[64,512]{1,...) custom-call(f32[256,512]{1,0:T(8,128)S(1)} %get-tuple-element.38.refs_0_, ...), custom_call_target="tpu_custom_call" | custom-call | tf_op jit(solution)/shard_map/pallas_call | solution.py:792
  42.1 0.7 collective-permute-start.4
  42.8 0.5 collective-permute-start.5
  43.3 14.6 %all_to_all.33.refs_3_ = f32[16,4,256]{2,1,0:T(4,128)S(1)} all-to-all(f32[16,4,256]{2,1,0:T(4,128)S(1)} %get-tuple-element.53), channel_id=1, replica_groups=mesh['gx'=8,'gh'=2,'gl'=16] {'gx','gh'}, dimensions={0} | all-to-all | bytes 131072 | tf_op jit(solution)/shard_map/all_to_all | solution.py:821
  57.9 0.0 collective-permute-done.4.refs_1_
  57.9 0.0 collective-permute-done.5.refs_2_
  57.9 0.2 shard_map.134
  58.0 0.5 collective-permute-start.6
  58.5 0.2 collective-permute-start.7
  58.7 11.7 %all_to_all.34.refs_6_ = f32[16,4,256]{2,1,0:T(4,128)S(1)} all-to-all(f32[16,4,256]{2,1,0:T(4,128)S(1)} %get-tuple-element.56), channel_id=1, replica_groups=mesh['gx'=8,'gh'=2,'gl'=16] {'gl'}, dimensions={0} | all-to-all | bytes 131072 | tf_op jit(solution)/shard_map/all_to_all | solution.py:829
  70.4 0.0 collective-permute-done.6.refs_3_
  70.4 0.0 collective-permute-done.7.refs_4_
  70.4 3.7 %shard_map.135 = (f32[256,512]{1,0:T(8,128)S(1)}, f32[256,512]{1,0:T(8,128)S(1)}, f32[256,512]{1,0:T(8,128)S(1)}, f32[64,128]{1,0:T(8,128)S(1)}, f32[64,128]{1,0...) custom-call(f32[256,512]{1,0:T(8,128)S(1)} %get-tuple-element.50.ref, ...), custom_call_target="tpu_custom_call" | custom-call | tf_op jit(solution)/shard_map/pallas_call | solution.py:792
  74.1 0.9 collective-permute-start.8
  75.0 0.1 collective-permute-start.9
  75.1 3.5 %collective-permute-start.10 = (f32[64,128]{1,0:T(8,128)S(1)}, f32[64,128]{1,0:T(8,128)S(1)}, u32[]{:S(2)}, u32[]{:S(2)}) collective-permute-start(f32[64,128]{1,0:T(8,128)S(1)} %get-tuple-element.64), channel_id=1, source_target_pairs={{0,224},{32,64},{64,32},{96,128},{128,96},{160,192},{192,160},{224... | collective-permute-start | bytes 98312 | tf_op jit(solution)/shard_map/ppermute | solution.py:815
  78.6 0.0 collective-permute-start.11
  78.7 1.7 %collective-permute-done.8.refs_1_ = f32[64,128]{1,0:T(8,128)S(1)} collective-permute-done((f32[64,128]{1,0:T(8,128)S(1)}, f32[64,128]{1,0:T(8,128)S(1)}, u32[]{:S(2)}, u32[]{:S(2)}) %collective-permute-start.8) | collective-permute-done | bytes 32800 | tf_op jit(solution)/shard_map/ppermute | solution.py:815
  80.3 0.0 collective-permute-done.9.refs_2_
  80.3 0.0 collective-permute-done.10.refs_3_
  80.3 0.0 collective-permute-done.11.refs_4_
  80.3 0.4 shard_map.136
  80.7 22.3 %all_to_all.35 = f32[256,1,128]{2,1,0:T(1,128)S(1)} all-to-all(f32[256,1,128]{2,1,0:T(1,128)S(1)} %bitcast.20), channel_id=1, replica_groups=mesh['gx'=8,'gh'=2,'gl'=16] {'gx','gh','gl'}, dimensions={0} | all-to-all | bytes 262144 | tf_op jit(solution)/shard_map/all_to_all | solution.py:869
  103.0 2.6 %shard_map.137 = (f32[256,512]{1,0:T(8,128)}, f32[256,512]{1,0:T(8,128)}) custom-call(f32[256,128]{1,0:T(8,128)S(1)} %bitcast.18, f32[4,256]{1,0:T(4,128)S(1)} %get-tuple-element.68.refs_1_, f32[256,512]{1,0:T(8,128)S(1)} %get-tuple-element.69.refs_2_, s32[1,256]{1,0:T(1,128)S(1)} %bitcast.22, f32[256,512]{1,0:T(8,128)S(1)} %get-tuple-element.59.refs_15_.refs_4_, ...), custom_call_target="tpu_custom_call" | custom-call | tf_op jit(solution)/shard_map/pallas_call | solution.py:792
Async XLA Ops:
  0.6 2.3 %copy-start.2 = (bf16[2,512,128]{2,1,0:T(8,128)(2,1)S(1)}, bf16[2,512,128]{2,1,0:T(8,128)(2,1)}, u32[]{:S(2)}) copy-start(bf16[2,512,128]{2,1,0:T(8,128)(2,1)} %constant.12.clone.refs_7_.refs_15_) | copy-start | bytes 786436
  0.6 2.3 %copy-start.8 = (f32[1,1,256]{2,1,0:T(1,128)S(1)}, f32[1,1,256]{2,1,0:T(1,128)}, u32[]{:S(2)}) copy-start(f32[1,1,256]{2,1,0:T(1,128)} %param.15) | copy-start | bytes 3076
  0.7 2.3 %copy-start.7 = (f32[1,1,256]{2,1,0:T(1,128)S(1)}, f32[1,1,256]{2,1,0:T(1,128)}, u32[]{:S(2)}) copy-start(f32[1,1,256]{2,1,0:T(1,128)} %param.14) | copy-start | bytes 3076
  0.7 2.3 %copy-start.6 = (s32[1,1,256]{2,1,0:T(1,128)S(1)}, s32[1,1,256]{2,1,0:T(1,128)}, u32[]{:S(2)}) copy-start(s32[1,1,256]{2,1,0:T(1,128)} %param.13) | copy-start | bytes 3076
  0.7 2.3 %copy-start.4 = (f32[1,1,256,512]{3,2,1,0:T(8,128)S(1)}, f32[1,1,256,512]{3,2,1,0:T(8,128)}, u32[]{:S(2)}) copy-start(f32[1,1,256,512]{3,2,1,0:T(8,128)} %param.12) | copy-start | bytes 1572868
  2.9 35.3 %copy-start = (bf16[2,2,256,256]{3,2,1,0:T(8,128)(2,1)S(1)}, bf16[2,2,256,256]{3,2,1,0:T(8,128)(2,1)}, u32[]{:S(2)}) copy-start(bf16[2,2,256,256]{3,2,1,0:T(8,128)(2,1)} %constant.11.clone.refs_9_.refs_10_) | copy-start | bytes 1572868
  2.9 35.3 %copy-start.1 = (bf16[2,2,256,256]{3,2,1,0:T(8,128)(2,1)S(1)}, bf16[2,2,256,256]{3,2,1,0:T(8,128)(2,1)}, u32[]{:S(2)}) copy-start(bf16[2,2,256,256]{3,2,1,0:T(8,128)(2,1)} %constant.10.clone.refs_14_.refs_17_) | copy-start | bytes 1572868
  3.0 35.3 %copy-start.3 = (bf16[2,128,512]{2,1,0:T(8,128)(2,1)S(1)}, bf16[2,128,512]{2,1,0:T(8,128)(2,1)}, u32[]{:S(2)}) copy-start(bf16[2,128,512]{2,1,0:T(8,128)(2,1)} %constant.13.clone.refs_10_.refs_11_) | copy-start | bytes 786436
  3.0 35.3 %copy-start.5 = (f32[8,512]{1,0:T(8,128)S(1)}, f32[8,512]{1,0:T(8,128)}, u32[]{:S(2)}) copy-start(f32[8,512]{1,0:T(8,128)} %constant.14.clone.refs_8_.refs_6_) | copy-start | bytes 49156
  4.3 22.7 %collective-permute-start = (f32[64,640]{1,0:T(8,128)S(1)}, f32[64,640]{1,0:T(8,128)S(1)}, u32[]{:S(2)}, u32[]{:S(2)}) collective-permute-start(f32[64,640]{1,0:T(8,128)S(1)} %get-tuple-element.39), channel_id=1, source_target_pairs={{0,1},{1,0},{2,3},{3,2},{4,5},{5,4},{6,7},{7,6},{8,9},{9,8},{10,11... | collective-permute-start | bytes 491528 | tf_op jit(solution)/shard_map/ppermute | solution.py:815
  6.8 20.1 %collective-permute-start.1 = (f32[64,640]{1,0:T(8,128)S(1)}, f32[64,640]{1,0:T(8,128)S(1)}, u32[]{:S(2)}, u32[]{:S(2)}) collective-permute-start(f32[64,640]{1,0:T(8,128)S(1)} %get-tuple-element.40), channel_id=1, source_target_pairs={{0,31},{1,2},{2,1},{3,4},{4,3},{5,6},{6,5},{7,8},{8,7},{9,10},{10,... | collective-permute-start | bytes 491528 | tf_op jit(solution)/shard_map/ppermute | solution.py:815
  27.1 11.2 %collective-permute-start.2 = (f32[96,640]{1,0:T(8,128)S(1)}, f32[96,640]{1,0:T(8,128)S(1)}, u32[]{:S(2)}, u32[]{:S(2)}) collective-permute-start(f32[96,640]{1,0:T(8,128)S(1)} %get-tuple-element.43), channel_id=1, source_target_pairs={{0,32},{32,0},{64,96},{96,64},{128,160},{160,128},{192,224},{224,1... | collective-permute-start | bytes 737288 | tf_op jit(solution)/shard_map/ppermute | solution.py:815
  27.6 10.7 %collective-permute-start.3 = (f32[96,640]{1,0:T(8,128)S(1)}, f32[96,640]{1,0:T(8,128)S(1)}, u32[]{:S(2)}, u32[]{:S(2)}) collective-permute-start(f32[96,640]{1,0:T(8,128)S(1)} %get-tuple-element.44), channel_id=1, source_target_pairs={{0,224},{32,64},{64,32},{96,128},{128,96},{160,192},{192,160},{224... | collective-permute-start | bytes 737288 | tf_op jit(solution)/shard_map/ppermute | solution.py:815
  42.1 15.8 %collective-permute-start.4 = (f32[64,512]{1,0:T(8,128)S(1)}, f32[64,512]{1,0:T(8,128)S(1)}, u32[]{:S(2)}, u32[]{:S(2)}) collective-permute-start(f32[64,512]{1,0:T(8,128)S(1)} %get-tuple-element.51), channel_id=1, source_target_pairs={{0,1},{1,0},{2,3},{3,2},{4,5},{5,4},{6,7},{7,6},{8,9},{9,8},{10,11... | collective-permute-start | bytes 393224 | tf_op jit(solution)/shard_map/ppermute | solution.py:815
  42.8 15.1 %collective-permute-start.5 = (f32[64,512]{1,0:T(8,128)S(1)}, f32[64,512]{1,0:T(8,128)S(1)}, u32[]{:S(2)}, u32[]{:S(2)}) collective-permute-start(f32[64,512]{1,0:T(8,128)S(1)} %get-tuple-element.52), channel_id=1, source_target_pairs={{0,31},{1,2},{2,1},{3,4},{4,3},{5,6},{6,5},{7,8},{8,7},{9,10},{10,... | collective-permute-start | bytes 393224 | tf_op jit(solution)/shard_map/ppermute | solution.py:815
  58.0 12.4 %collective-permute-start.6 = (f32[96,512]{1,0:T(8,128)S(1)}, f32[96,512]{1,0:T(8,128)S(1)}, u32[]{:S(2)}, u32[]{:S(2)}) collective-permute-start(f32[96,512]{1,0:T(8,128)S(1)} %get-tuple-element.54), channel_id=1, source_target_pairs={{0,32},{32,0},{64,96},{96,64},{128,160},{160,128},{192,224},{224,1... | collective-permute-start | bytes 589832 | tf_op jit(solution)/shard_map/ppermute | solution.py:815
  58.5 11.9 %collective-permute-start.7 = (f32[96,512]{1,0:T(8,128)S(1)}, f32[96,512]{1,0:T(8,128)S(1)}, u32[]{:S(2)}, u32[]{:S(2)}) collective-permute-start(f32[96,512]{1,0:T(8,128)S(1)} %get-tuple-element.55), channel_id=1, source_target_pairs={{0,224},{32,64},{64,32},{96,128},{128,96},{160,192},{192,160},{224... | collective-permute-start | bytes 589832 | tf_op jit(solution)/shard_map/ppermute | solution.py:815
  74.1 6.2 %collective-permute-start.8 = (f32[64,128]{1,0:T(8,128)S(1)}, f32[64,128]{1,0:T(8,128)S(1)}, u32[]{:S(2)}, u32[]{:S(2)}) collective-permute-start(f32[64,128]{1,0:T(8,128)S(1)} %get-tuple-element.62), channel_id=1, source_target_pairs={{0,31},{1,2},{2,1},{3,4},{4,3},{5,6},{6,5},{7,8},{8,7},{9,10},{10,... | collective-permute-start | bytes 98312 | tf_op jit(solution)/shard_map/ppermute | solution.py:815
  75.0 5.3 %collective-permute-start.9 = (f32[64,128]{1,0:T(8,128)S(1)}, f32[64,128]{1,0:T(8,128)S(1)}, u32[]{:S(2)}, u32[]{:S(2)}) collective-permute-start(f32[64,128]{1,0:T(8,128)S(1)} %get-tuple-element.63), channel_id=1, source_target_pairs={{0,1},{1,0},{2,3},{3,2},{4,5},{5,4},{6,7},{7,6},{8,9},{9,8},{10,11... | collective-permute-start | bytes 98312 | tf_op jit(solution)/shard_map/ppermute | solution.py:815
  75.1 5.2 %collective-permute-start.10 = (f32[64,128]{1,0:T(8,128)S(1)}, f32[64,128]{1,0:T(8,128)S(1)}, u32[]{:S(2)}, u32[]{:S(2)}) collective-permute-start(f32[64,128]{1,0:T(8,128)S(1)} %get-tuple-element.64), channel_id=1, source_target_pairs={{0,224},{32,64},{64,32},{96,128},{128,96},{160,192},{192,160},{224... | collective-permute-start | bytes 98312 | tf_op jit(solution)/shard_map/ppermute | solution.py:815
  78.6 1.7 %collective-permute-start.11 = (f32[64,128]{1,0:T(8,128)S(1)}, f32[64,128]{1,0:T(8,128)S(1)}, u32[]{:S(2)}, u32[]{:S(2)}) collective-permute-start(f32[64,128]{1,0:T(8,128)S(1)} %get-tuple-element.65), channel_id=1, source_target_pairs={{0,32},{32,0},{64,96},{96,64},{128,160},{160,128},{192,224},{224,1... | collective-permute-start | bytes 98312 | tf_op jit(solution)/shard_map/ppermute | solution.py:815
